TPU v7x, 512 devices: a whole 4x8x8 slice. The times are simulated.
512 devices in a mesh: seq: 64 (over y, x, core), head: 8 (over z).
Axes of the slice: x: 4, y: 8, z: 8, core: 2. Of those that a mesh axis runs over, the one named last changes fastest.
Arguments:
- ssm_input: bfloat16 [32768, 3072], P('seq', 'head'), may hold values from -125 to 125
- input_map: bfloat16 [32768, 1024], P('seq', 'head'), may hold values from -0.4375 to 0.4375
- output_map: bfloat16 [32768, 1024], P('seq', 'head'), may hold values from -0.4375 to 0.4375
- decay_forward: bfloat16 [48, 32768], P('head', 'seq'), may hold values from -2 to 0
- decay_reverse: bfloat16 [48, 32768], P('head', 'seq'), may hold values from -2 to 0
- skip_gain: float32 [48], P('head'), may hold values from 0.2 to 1
- norm_gain: float32 [3072], P('head'), may hold values from 0.5 to 1.5
- scan_order: int32 [4096], P('seq'), may hold values from 0 to 4095, as said below
- raster_order: int32 [4096], P('seq'), may hold values from 0 to 4095, as said below
- grad_normed: bfloat16 [32768, 3072], P('seq', 'head'), may hold values from -6 to 6
Outputs:
- normed_output: bfloat16 [32768, 3072], P('seq', 'head')
- grad_input: bfloat16 [32768, 3072], P('seq', 'head')
Inputs may be any that keep to these rules, and one draw needn't show every extreme that they name: scan_order is a permutation of the units; the units held by any index of seq, as positions 64 * e to 64 * e + 63, come one from every index of seq. raster_order is the inverse of scan_order.
All inputs are finite; a program needn't handle non-finite values.
Results may differ from a plain program's by a relative error of at most 0.011.
Values may be sent and summed in bfloat16 or wider, within the bound.
No kernel may reach another device: no remote copies, remote signals or barrier semaphores. Data moves between devices by JAX's collectives and lax.ppermute only.
A program may use at most 128 MiB of HBM per device.

v0:
```python
import jax
import jax.numpy as jnp
from jax import lax
from jax.sharding import PartitionSpec as P

HEAD_DIM = 64
STATE = 128
SPAN = 256
FEATURES = 3072


EPSILON = 1e-05


def passed_along(block, axis, distance):
    devices = range(lax.axis_size(axis))
    route = [(i - distance, i) for i in devices if i - distance in devices]
    return lax.ppermute(block, axis, route)


def combine(earlier, latter):
    return (earlier[0] + latter[0], jnp.exp(latter[0])[..., None, None] * earlier[1] + latter[1])


def carried(device_sum, reverse):
    direction = -1 if reverse else 1
    shifted = passed_along((device_sum[0], device_sum[1]), "seq", direction)
    for bit_index in range(lax.axis_size("seq").bit_length() - 1):
        arrived = passed_along((shifted[0], shifted[1]), "seq", direction * (1 << bit_index))
        shifted = combine(arrived, shifted)
    return shifted


def scan_block(values, key_rows, query_rows, log_decay, reverse):
    tok_rows = values.shape[0]
    head_count = log_decay.shape[0]
    head_width = values.shape[1] // head_count
    group_count = key_rows.shape[1] // STATE
    per_group = head_count // group_count
    span_count = tok_rows // SPAN
    value_blocks = values.reshape(span_count, SPAN, group_count, per_group, head_width)
    key_blocks = key_rows.reshape(span_count, SPAN, group_count, STATE)
    query_blocks = query_rows.reshape(span_count, SPAN, group_count, STATE)
    cumulative = jnp.cumsum(
        log_decay.astype(jnp.float32).reshape(group_count, per_group, span_count, SPAN), axis=3
    )
    scores = jnp.einsum(
        "cign,cjgn->gcij", query_blocks, key_blocks, preferred_element_type=jnp.float32
    )
    spread = cumulative[..., :, None] - cumulative[..., None, :]
    row_ids = lax.broadcasted_iota(jnp.int32, (SPAN, SPAN), 0)
    col_ids = lax.broadcasted_iota(jnp.int32, (SPAN, SPAN), 1)
    span_end = cumulative[..., -1]
    if reverse:
        allowed = col_ids >= row_ids
        damping = jnp.exp(jnp.minimum(-spread, 0.0))
        key_weight = jnp.exp(cumulative)
        query_weight = jnp.exp(span_end[..., None] - cumulative)
    else:
        allowed = col_ids <= row_ids
        damping = jnp.exp(jnp.minimum(spread, 0.0))
        key_weight = jnp.exp(span_end[..., None] - cumulative)
        query_weight = jnp.exp(cumulative)
    weights = jnp.where(allowed, scores[:, None] * damping, 0.0).astype(jnp.bfloat16)
    inner_part = jnp.einsum(
        "ghcij,cjghp->cighp", weights, value_blocks, preferred_element_type=jnp.float32
    )
    scaled_keys = (jnp.transpose(key_blocks, (2, 0, 1, 3))[:, None] * key_weight[..., None]).astype(
        jnp.bfloat16
    )
    span_states = jnp.einsum(
        "ghcjn,cjghp->ghcnp", scaled_keys, value_blocks, preferred_element_type=jnp.float32
    )
    visit_order = list(range(span_count))
    if reverse:
        visit_order = visit_order[::-1]
    running = (jnp.zeros_like(span_end[..., 0]), jnp.zeros_like(span_states[:, :, 0]))
    preceding = [running] * span_count
    for position in visit_order:
        preceding[position] = running
        running = combine(running, (span_end[..., position], span_states[:, :, position]))
    incoming = carried(running, reverse)
    entering = jnp.stack(
        [piece[1] + jnp.exp(piece[0])[..., None, None] * incoming[1] for piece in preceding], axis=2
    )
    entering = entering.astype(jnp.bfloat16)
    outer_part = jnp.einsum(
        "cign,ghcnp->cighp", query_blocks, entering, preferred_element_type=jnp.float32
    )
    outer_part = outer_part * jnp.transpose(query_weight, (2, 3, 0, 1))[..., None]
    return (inner_part + outer_part).reshape(tok_rows, head_count * head_width)


def reorder(array, send_index, recv_index):
    outgoing = jnp.take(array, send_index, axis=0)
    arrived = lax.all_to_all(outgoing, "seq", split_axis=0, concat_axis=0, tiled=True)
    return jnp.take(arrived, recv_index, axis=0)


def shards(
    ssm_input,
    input_map,
    output_map,
    decay_forward,
    decay_reverse,
    skip_gain,
    norm_gain,
    scan_order,
    raster_order,
    grad_normed,
):
    unit_count = scan_order.shape[0]
    tok_rows = ssm_input.shape[0]
    unit_rows = tok_rows // unit_count
    head_width = ssm_input.shape[1]
    state_width = input_map.shape[1]
    raster_dest = raster_order // unit_count
    scan_source = scan_order // unit_count
    send_scan = jnp.argsort(raster_dest, stable=True)
    send_raster = jnp.argsort(scan_source, stable=True)

    def to_scan(array):
        return reorder(array.reshape(unit_count, unit_rows, -1), send_scan, scan_source).reshape(
            tok_rows, -1
        )

    def to_raster(array):
        return reorder(array.reshape(unit_count, unit_rows, -1), send_raster, raster_dest).reshape(
            tok_rows, -1
        )

    joined = jnp.concatenate([ssm_input, input_map, output_map], axis=1)
    joined_scan = to_scan(joined)
    values_scan = joined_scan[:, :head_width]
    in_map_scan = joined_scan[:, head_width : head_width + state_width]
    out_map_scan = joined_scan[:, head_width + state_width :]
    y_forward = scan_block(ssm_input, input_map, output_map, decay_forward, False).astype(
        jnp.bfloat16
    )
    y_reverse = to_raster(
        scan_block(values_scan, in_map_scan, out_map_scan, decay_reverse, True).astype(jnp.bfloat16)
    )
    skip_cols = jnp.repeat(skip_gain, HEAD_DIM)
    combined = (
        y_forward.astype(jnp.float32)
        + y_reverse.astype(jnp.float32)
        + skip_cols * ssm_input.astype(jnp.float32)
    )
    squares = lax.psum(jnp.sum(combined * combined, axis=1), "head")
    inv_rms = lax.rsqrt(squares / FEATURES + EPSILON)
    normed_output = (combined * inv_rms[:, None] * norm_gain).astype(jnp.bfloat16)
    scaled_grad = norm_gain * grad_normed.astype(jnp.float32)
    inner_sum = lax.psum(jnp.sum(combined * scaled_grad, axis=1), "head")
    grad_combined = (
        inv_rms[:, None] * scaled_grad - combined * (inv_rms**3 * inner_sum / FEATURES)[:, None]
    )
    grad_combined = grad_combined.astype(jnp.bfloat16)
    grad_forward = scan_block(grad_combined, output_map, input_map, decay_forward, True).astype(
        jnp.bfloat16
    )
    grad_scan = scan_block(
        to_scan(grad_combined), out_map_scan, in_map_scan, decay_reverse, False
    ).astype(jnp.bfloat16)
    grad_reverse = to_raster(grad_scan)
    grad_input = (
        grad_forward.astype(jnp.float32)
        + grad_reverse.astype(jnp.float32)
        + skip_cols * grad_combined.astype(jnp.float32)
    )
    return (normed_output, grad_input.astype(jnp.bfloat16))


def solution(mesh):
    return jax.shard_map(
        shards,
        mesh=mesh,
        in_specs=(
            P("seq", "head"),
            P("seq", "head"),
            P("seq", "head"),
            P("head", "seq"),
            P("head", "seq"),
            P("head"),
            P("head"),
            P("seq"),
            P("seq"),
            P("seq", "head"),
        ),
        out_specs=(P("seq", "head"), P("seq", "head")),
        check_vma=False,
    )
```

profile of v0, /device:TPU:1, one launch (start us, length us, event | category | flops | bytes accessed | tf_op | source)
XLA Modules:
  0.0 442.5 jit_solution(11062706161288408343)
XLA Ops:
  1.4 3.6 reduce-window.16
  6.3 8.8 %collective-permute-start.13 = (f32[1,6]{1,0:T(1,128)}, f32[1,6]{1,0:T(1,128)}, u32[]{:S(2)}, u32[]{:S(2)}) collective-permute-start(f32[1,6]{1,0:T(1,128)} %get-tuple-element.85), channel_id=1, source_target_pairs={{8,0},{16,8},{24,16},{32,24},{40,32},{48,40},{56,48},{64,56},{72,6... | collective-permute-start | bytes 80 | tf_op jit(solution)/shard_map/ppermute | solution.py:18
  17.0 3.6 reduce-window.14
  23.8 3.0 collective-permute-start.26
  27.3 2.0 sort.31
  31.2 8.4 %all-to-all-start = ((bf16[64,8,640]{2,1,0:T(8,128)(2,1)}), bf16[64,8,640]{2,1,0:T(8,128)(2,1)S(1)}, u32[]{:S(2)}, u32[]{:S(2)}) async-start(bf16[64,8,640]{2,1,0:T(8,128)(2,1)} %broadcast_select_fusion), calls=%async_computation | async-start | bytes 1310720 | tf_op jit(solution)/shard_map/all_to_all | solution.py:96
  43.3 3.5 collective-permute-start.6
  51.0 2.1 sort.32
  66.4 3.6 collective-permute-start.1
  72.0 2.4 collective-permute-start.27
  76.9 4.0 collective-permute-start.2
  82.2 3.1 collective-permute-start.41
  89.1 9.8 %collective-permute-start.3 = (f32[1,6]{1,0:T(1,128)S(1)}, f32[1,6]{1,0:T(1,128)S(1)}, u32[]{:S(2)}, u32[]{:S(2)}) collective-permute-start(f32[1,6]{1,0:T(1,128)S(1)} %get-tuple-element.56), channel_id=1, source_target_pairs={{0,32},{8,40},{16,48},{24,56},{32,64},{40,72},{48,80},{56,88},{64,... | collective-permute-start | bytes 80 | tf_op jit(solution)/shard_map/ppermute | solution.py:18
  99.5 5.8 %collective-permute-start.42 = (f32[1,6]{1,0:T(1,128)S(1)}, f32[1,6]{1,0:T(1,128)S(1)}, u32[]{:S(2)}, u32[]{:S(2)}) collective-permute-start(f32[1,6]{1,0:T(1,128)S(1)} %get-tuple-element.21), channel_id=1, source_target_pairs={{0,32},{8,40},{16,48},{24,56},{32,64},{40,72},{48,80},{56,88},{64,... | collective-permute-start | bytes 80 | tf_op jit(solution)/shard_map/ppermute | solution.py:18
  109.0 6.1 %collective-permute-start.4 = (f32[1,6]{1,0:T(1,128)S(1)}, f32[1,6]{1,0:T(1,128)S(1)}, u32[]{:S(2)}, u32[]{:S(2)}) collective-permute-start(f32[1,6]{1,0:T(1,128)S(1)} %get-tuple-element.54), channel_id=1, source_target_pairs={{0,64},{8,72},{16,80},{24,88},{32,96},{40,104},{48,112},{56,120},{... | collective-permute-start | bytes 80 | tf_op jit(solution)/shard_map/ppermute | solution.py:18
  115.8 3.4 collective-permute-start.43
  123.3 11.6 %collective-permute-start.5 = (f32[1,6]{1,0:T(1,128)}, f32[1,6]{1,0:T(1,128)}, u32[]{:S(2)}, u32[]{:S(2)}) collective-permute-start(f32[1,6]{1,0:T(1,128)} %get-tuple-element.52), channel_id=1, source_target_pairs={{0,128},{8,136},{16,144},{24,152},{32,160},{40,168},{48,176},{56,1... | collective-permute-start | bytes 80 | tf_op jit(solution)/shard_map/ppermute | solution.py:18
  135.5 5.8 %collective-permute-start.44 = (f32[1,6]{1,0:T(1,128)}, f32[1,6]{1,0:T(1,128)}, u32[]{:S(2)}, u32[]{:S(2)}) collective-permute-start(f32[1,6]{1,0:T(1,128)} %get-tuple-element.17), channel_id=1, source_target_pairs={{0,128},{8,136},{16,144},{24,152},{32,160},{40,168},{48,176},{56,1... | collective-permute-start | bytes 80 | tf_op jit(solution)/shard_map/ppermute | solution.py:18
  143.2 4.5 %collective-permute-start.7 = (f32[1,6,128,64]{2,3,1,0:T(8,128)}, f32[1,6,128,64]{2,3,1,0:T(8,128)}, u32[]{:S(2)}, u32[]{:S(2)}) collective-permute-start(f32[1,6,128,64]{2,3,1,0:T(8,128)} %collective-permute-done.6), channel_id=1, source_target_pairs={{0,8},{8,16},{16,24},{24,32},{32,40},{40,48},{48,56},{56,64},{64,7... | collective-permute-start | bytes 589832 | tf_op jit(solution)/shard_map/ppermute | solution.py:18
  151.7 4.6 %collective-permute-start.19 = (f32[1,6,128,64]{2,3,1,0:T(8,128)S(1)}, f32[1,6,128,64]{2,3,1,0:T(8,128)S(1)}, u32[]{:S(2)}, u32[]{:S(2)}) collective-permute-start(f32[1,6,128,64]{2,3,1,0:T(8,128)S(1)} %fusion.88), channel_id=1, source_target_pairs={{8,0},{16,8},{24,16},{32,24},{40,32},{48,40},{56,48},{64,56},{72,6... | collective-permute-start | bytes 589832 | tf_op jit(solution)/shard_map/ppermute | solution.py:18
  156.3 2.4 collective-permute-done.19
  161.7 3.9 collective-permute-start.8
  167.0 3.0 collective-permute-done.8
  170.1 7.5 %collective-permute-start.9 = (f32[1,6,128,64]{2,3,1,0:T(8,128)S(1)}, f32[1,6,128,64]{2,3,1,0:T(8,128)S(1)}, u32[]{:S(2)}, u32[]{:S(2)}) collective-permute-start(f32[1,6,128,64]{2,3,1,0:T(8,128)S(1)} %multiply_add_fusion.23), channel_id=1, source_target_pairs={{0,32},{8,40},{16,48},{24,56},{32,64},{40,72},{48,80},{56,88},{64,... | collective-permute-start | bytes 589832 | tf_op jit(solution)/shard_map/ppermute | solution.py:18
  179.1 2.9 collective-permute-done.9
  182.0 8.1 %collective-permute-start.10 = (f32[1,6,128,64]{2,3,1,0:T(8,128)S(1)}, f32[1,6,128,64]{2,3,1,0:T(8,128)S(1)}, u32[]{:S(2)}, u32[]{:S(2)}) collective-permute-start(f32[1,6,128,64]{2,3,1,0:T(8,128)S(1)} %multiply_add_fusion.22), channel_id=1, source_target_pairs={{0,64},{8,72},{16,80},{24,88},{32,96},{40,104},{48,112},{56,120},{... | collective-permute-start | bytes 589832 | tf_op jit(solution)/shard_map/ppermute | solution.py:18
  193.5 11.2 %collective-permute-start.11 = (f32[1,6,128,64]{2,3,1,0:T(8,128)}, f32[1,6,128,64]{2,3,1,0:T(8,128)}, u32[]{:S(2)}, u32[]{:S(2)}) collective-permute-start(f32[1,6,128,64]{2,3,1,0:T(8,128)} %multiply_add_fusion.21), channel_id=1, source_target_pairs={{0,128},{8,136},{16,144},{24,152},{32,160},{40,168},{48,176},{56,1... | collective-permute-start | bytes 589832 | tf_op jit(solution)/shard_map/ppermute | solution.py:18
  206.3 13.6 %collective-permute-done.24 = f32[1,6,128,64]{2,3,1,0:T(8,128)S(1)} collective-permute-done((f32[1,6,128,64]{2,3,1,0:T(8,128)S(1)}, f32[1,6,128,64]{2,3,1,0:T(8,128)S(1)}, u32[]{:S(2)}, u32[]{:S(2)}) %collective-permute-start.24) | collective-permute-done | bytes 196640 | tf_op jit(solution)/shard_map/ppermute | solution.py:18
  222.5 7.9 %collective-permute-done.25 = f32[1,6,128,64]{2,3,1,0:T(8,128)S(1)} collective-permute-done((f32[1,6,128,64]{2,3,1,0:T(8,128)S(1)}, f32[1,6,128,64]{2,3,1,0:T(8,128)S(1)}, u32[]{:S(2)}, u32[]{:S(2)}) %collective-permute-start.25) | collective-permute-done | bytes 196640 | tf_op jit(solution)/shard_map/ppermute | solution.py:18
  234.5 16.1 %all-to-all-start.1 = ((bf16[64,8,384]{2,1,0:T(8,128)(2,1)}), bf16[64,8,384]{2,1,0:T(8,128)(2,1)S(1)}, u32[]{:S(2)}, u32[]{:S(2)}) async-start(bf16[64,8,384]{2,1,0:T(8,128)(2,1)} %broadcast_select_fusion.4), calls=%async_computation.1 | async-start | bytes 786432 | tf_op jit(solution)/shard_map/all_to_all | solution.py:96
  251.7 7.3 %collective-permute-start.12 = (f32[1,6,128,64]{2,3,1,0:T(8,128)S(1)}, f32[1,6,128,64]{2,3,1,0:T(8,128)S(1)}, u32[]{:S(2)}, u32[]{:S(2)}) collective-permute-start(f32[1,6,128,64]{2,3,1,0:T(8,128)S(1)} %multiply_add_fusion.20), channel_id=1, source_target_pairs={{0,256},{8,264},{16,272},{24,280},{32,288},{40,296},{48,304},{56,3... | collective-permute-start | bytes 589832 | tf_op jit(solution)/shard_map/ppermute | solution.py:18
  259.7 4.9 %collective-permute-done.12 = f32[1,6,128,64]{2,3,1,0:T(8,128)S(1)} collective-permute-done((f32[1,6,128,64]{2,3,1,0:T(8,128)S(1)}, f32[1,6,128,64]{2,3,1,0:T(8,128)S(1)}, u32[]{:S(2)}, u32[]{:S(2)}) %collective-permute-start.12) | collective-permute-done | bytes 196640 | tf_op jit(solution)/shard_map/ppermute | solution.py:18
  269.3 19.4 %all-reduce = (f32[512]{0:T(512)S(1)}, f32[512]{0:T(512)S(1)}) all-reduce(f32[512]{0:T(512)S(1)} %get-tuple-element.13, f32[512]{0:T(512)S(1)} %get-tuple-element.12), channel_id=1, replica_groups=mesh['seq'=64,'head'=8] {'head'}, use_global_device_ids=true, to_apply=%region_7.10 | all-reduce | flops 1024 | bytes 8192 | tf_op jit(solution)/shard_map/psum | solution.py:149
  290.9 18.2 %all-to-all-start.2 = ((bf16[64,8,384]{2,1,0:T(8,128)(2,1)}), bf16[64,8,384]{2,1,0:T(8,128)(2,1)S(1)}, u32[]{:S(2)}, u32[]{:S(2)}) async-start(bf16[64,8,384]{2,1,0:T(8,128)(2,1)} %broadcast_select_fusion.2), calls=%async_computation.2 | async-start | bytes 786432 | tf_op jit(solution)/shard_map/all_to_all | solution.py:96
  311.5 2.4 collective-permute-start.32
  315.8 4.5 %collective-permute-done.32 = f32[1,6,128,64]{2,3,1,0:T(8,128)} collective-permute-done((f32[1,6,128,64]{2,3,1,0:T(8,128)S(1)}, f32[1,6,128,64]{2,3,1,0:T(8,128)}, u32[]{:S(2)}, u32[]{:S(2)}) %collective-permute-start.32) | collective-permute-done | bytes 196640 | tf_op jit(solution)/shard_map/ppermute | solution.py:18
  322.3 2.0 all-to-all-done.2
  328.9 3.2 collective-permute-start.45
  334.7 4.5 %collective-permute-start.46 = (f32[1,6,128,64]{2,3,1,0:T(8,128)}, f32[1,6,128,64]{2,3,1,0:T(8,128)S(1)}, u32[]{:S(2)}, u32[]{:S(2)}) collective-permute-start(f32[1,6,128,64]{2,3,1,0:T(8,128)} %collective-permute-done.45), channel_id=1, source_target_pairs={{0,8},{8,16},{16,24},{24,32},{32,40},{40,48},{48,56},{56,64},{64,7... | collective-permute-start | bytes 589832 | tf_op jit(solution)/shard_map/ppermute | solution.py:18
  343.1 3.6 collective-permute-start.47
  350.3 9.7 %collective-permute-start.48 = (f32[1,6,128,64]{2,3,1,0:T(8,128)S(1)}, f32[1,6,128,64]{2,3,1,0:T(8,128)S(1)}, u32[]{:S(2)}, u32[]{:S(2)}) collective-permute-start(f32[1,6,128,64]{2,3,1,0:T(8,128)S(1)} %multiply_add_fusion.5), channel_id=1, source_target_pairs={{0,32},{8,40},{16,48},{24,56},{32,64},{40,72},{48,80},{56,88},{64,... | collective-permute-start | bytes 589832 | tf_op jit(solution)/shard_map/ppermute | solution.py:18
  360.9 4.6 %collective-permute-done.48 = f32[1,6,128,64]{2,3,1,0:T(8,128)S(1)} collective-permute-done((f32[1,6,128,64]{2,3,1,0:T(8,128)S(1)}, f32[1,6,128,64]{2,3,1,0:T(8,128)S(1)}, u32[]{:S(2)}, u32[]{:S(2)}) %collective-permute-start.48) | collective-permute-done | bytes 196640 | tf_op jit(solution)/shard_map/ppermute | solution.py:18
  365.6 8.0 %collective-permute-start.49 = (f32[1,6,128,64]{2,3,1,0:T(8,128)S(1)}, f32[1,6,128,64]{2,3,1,0:T(8,128)S(1)}, u32[]{:S(2)}, u32[]{:S(2)}) collective-permute-start(f32[1,6,128,64]{2,3,1,0:T(8,128)S(1)} %multiply_add_fusion.4), channel_id=1, source_target_pairs={{0,64},{8,72},{16,80},{24,88},{32,96},{40,104},{48,112},{56,120},{... | collective-permute-start | bytes 589832 | tf_op jit(solution)/shard_map/ppermute | solution.py:18
  376.3 4.0 collective-permute-start.50
  383.7 17.4 %collective-permute-start.51 = (f32[1,6,128,64]{2,3,1,0:T(8,128)S(1)}, f32[1,6,128,64]{2,3,1,0:T(8,128)S(1)}, u32[]{:S(2)}, u32[]{:S(2)}) collective-permute-start(f32[1,6,128,64]{2,3,1,0:T(8,128)S(1)} %multiply_add_fusion.2), channel_id=1, source_target_pairs={{0,256},{8,264},{16,272},{24,280},{32,288},{40,296},{48,304},{56,3... | collective-permute-start | bytes 589832 | tf_op jit(solution)/shard_map/ppermute | solution.py:18
  407.1 17.6 %all-to-all-start.3 = ((bf16[64,8,384]{2,1,0:T(8,128)(2,1)}), bf16[64,8,384]{2,1,0:T(8,128)(2,1)S(1)}, u32[]{:S(2)}, u32[]{:S(2)}) async-start(bf16[64,8,384]{2,1,0:T(8,128)(2,1)} %broadcast_select_fusion.3), calls=%async_computation.3 | async-start | bytes 786432 | tf_op jit(solution)/shard_map/all_to_all | solution.py:96
  424.8 2.0 fusion.52
  428.8 11.0 %all-to-all-done.3 = bf16[64,8,384]{2,1,0:T(8,128)(2,1)S(1)} async-done(((bf16[64,8,384]{2,1,0:T(8,128)(2,1)}), bf16[64,8,384]{2,1,0:T(8,128)(2,1)S(1)}, u32[]{:S(2)}, u32[]{:S(2)}) %all-to-all-start.3) | async-done | bytes 393248 | tf_op jit(solution)/shard_map/all_to_all | solution.py:96
  (375 shorter events, 119.1 us)
Async XLA Ops:
  6.3 58.1 %collective-permute-start.13 = (f32[1,6]{1,0:T(1,128)}, f32[1,6]{1,0:T(1,128)}, u32[]{:S(2)}, u32[]{:S(2)}) collective-permute-start(f32[1,6]{1,0:T(1,128)} %get-tuple-element.85), channel_id=1, source_target_pairs={{8,0},{16,8},{24,16},{32,24},{40,32},{48,40},{56,48},{64,56},{72,6... | collective-permute-start | bytes 80 | tf_op jit(solution)/shard_map/ppermute | solution.py:18
  15.1 54.9 %collective-permute-start.39 = (f32[1,6]{1,0:T(1,128)}, f32[1,6]{1,0:T(1,128)}, u32[]{:S(2)}, u32[]{:S(2)}) collective-permute-start(f32[1,6]{1,0:T(1,128)} %get-tuple-element.85), channel_id=1, source_target_pairs={{0,8},{8,16},{16,24},{24,32},{32,40},{40,48},{48,56},{56,64},{64,7... | collective-permute-start | bytes 80 | tf_op jit(solution)/shard_map/ppermute | solution.py:18
  21.9 44.5 %collective-permute-start = (f32[1,6]{1,0:T(1,128)}, f32[1,6]{1,0:T(1,128)}, u32[]{:S(2)}, u32[]{:S(2)}) collective-permute-start(f32[1,6]{1,0:T(1,128)} %get-tuple-element.86), channel_id=1, source_target_pairs={{0,8},{8,16},{16,24},{24,32},{32,40},{40,48},{48,56},{56,64},{64,7... | collective-permute-start | bytes 80 | tf_op jit(solution)/shard_map/ppermute | solution.py:18
  23.8 48.2 %collective-permute-start.26 = (f32[1,6]{1,0:T(1,128)}, f32[1,6]{1,0:T(1,128)}, u32[]{:S(2)}, u32[]{:S(2)}) collective-permute-start(f32[1,6]{1,0:T(1,128)} %get-tuple-element.86), channel_id=1, source_target_pairs={{8,0},{16,8},{24,16},{32,24},{40,32},{48,40},{56,48},{64,56},{72,6... | collective-permute-start | bytes 80 | tf_op jit(solution)/shard_map/ppermute | solution.py:18
  31.2 116.6 %all-to-all-start = ((bf16[64,8,640]{2,1,0:T(8,128)(2,1)}), bf16[64,8,640]{2,1,0:T(8,128)(2,1)S(1)}, u32[]{:S(2)}, u32[]{:S(2)}) async-start(bf16[64,8,640]{2,1,0:T(8,128)(2,1)} %broadcast_select_fusion), calls=%async_computation | async-start | bytes 1310720 | tf_op jit(solution)/shard_map/all_to_all | solution.py:96
  43.3 99.9 %collective-permute-start.6 = (f32[1,6,128,64]{2,3,1,0:T(8,128)}, f32[1,6,128,64]{2,3,1,0:T(8,128)}, u32[]{:S(2)}, u32[]{:S(2)}) collective-permute-start(f32[1,6,128,64]{2,3,1,0:T(8,128)} %fusion.90), channel_id=1, source_target_pairs={{0,8},{8,16},{16,24},{24,32},{32,40},{40,48},{48,56},{56,64},{64,7... | collective-permute-start | bytes 589832 | tf_op jit(solution)/shard_map/ppermute | solution.py:18
  64.4 9.9 %collective-permute-start.14 = (f32[1,6]{1,0:T(1,128)}, f32[1,6]{1,0:T(1,128)S(1)}, u32[]{:S(2)}, u32[]{:S(2)}) collective-permute-start(f32[1,6]{1,0:T(1,128)} %collective-permute-done.13), channel_id=1, source_target_pairs={{8,0},{16,8},{24,16},{32,24},{40,32},{48,40},{56,48},{64,56},{72,6... | collective-permute-start | bytes 80 | tf_op jit(solution)/shard_map/ppermute | solution.py:18
  66.4 9.9 %collective-permute-start.1 = (f32[1,6]{1,0:T(1,128)}, f32[1,6]{1,0:T(1,128)S(1)}, u32[]{:S(2)}, u32[]{:S(2)}) collective-permute-start(f32[1,6]{1,0:T(1,128)} %collective-permute-done), channel_id=1, source_target_pairs={{0,8},{8,16},{16,24},{24,32},{32,40},{40,48},{48,56},{56,64},{64,7... | collective-permute-start | bytes 80 | tf_op jit(solution)/shard_map/ppermute | solution.py:18
  70.0 10.9 %collective-permute-start.40 = (f32[1,6]{1,0:T(1,128)}, f32[1,6]{1,0:T(1,128)S(1)}, u32[]{:S(2)}, u32[]{:S(2)}) collective-permute-start(f32[1,6]{1,0:T(1,128)} %collective-permute-done.39), channel_id=1, source_target_pairs={{0,8},{8,16},{16,24},{24,32},{32,40},{40,48},{48,56},{56,64},{64,7... | collective-permute-start | bytes 80 | tf_op jit(solution)/shard_map/ppermute | solution.py:18
  72.0 13.3 %collective-permute-start.27 = (f32[1,6]{1,0:T(1,128)}, f32[1,6]{1,0:T(1,128)S(1)}, u32[]{:S(2)}, u32[]{:S(2)}) collective-permute-start(f32[1,6]{1,0:T(1,128)} %collective-permute-done.26), channel_id=1, source_target_pairs={{8,0},{16,8},{24,16},{32,24},{40,32},{48,40},{56,48},{64,56},{72,6... | collective-permute-start | bytes 80 | tf_op jit(solution)/shard_map/ppermute | solution.py:18
  75.0 12.8 %collective-permute-start.15 = (f32[1,6]{1,0:T(1,128)S(1)}, f32[1,6]{1,0:T(1,128)S(1)}, u32[]{:S(2)}, u32[]{:S(2)}) collective-permute-start(f32[1,6]{1,0:T(1,128)S(1)} %get-tuple-element.48), channel_id=1, source_target_pairs={{16,0},{24,8},{32,16},{40,24},{48,32},{56,40},{64,48},{72,56},{80,... | collective-permute-start | bytes 80 | tf_op jit(solution)/shard_map/ppermute | solution.py:18
  76.9 12.1 %collective-permute-start.2 = (f32[1,6]{1,0:T(1,128)S(1)}, f32[1,6]{1,0:T(1,128)S(1)}, u32[]{:S(2)}, u32[]{:S(2)}) collective-permute-start(f32[1,6]{1,0:T(1,128)S(1)} %get-tuple-element.58), channel_id=1, source_target_pairs={{0,16},{8,24},{16,32},{24,40},{32,48},{40,56},{48,64},{56,72},{64,... | collective-permute-start | bytes 80 | tf_op jit(solution)/shard_map/ppermute | solution.py:18
  82.2 16.7 %collective-permute-start.41 = (f32[1,6]{1,0:T(1,128)S(1)}, f32[1,6]{1,0:T(1,128)S(1)}, u32[]{:S(2)}, u32[]{:S(2)}) collective-permute-start(f32[1,6]{1,0:T(1,128)S(1)} %get-tuple-element.23), channel_id=1, source_target_pairs={{0,16},{8,24},{16,32},{24,40},{32,48},{40,56},{48,64},{56,72},{64,... | collective-permute-start | bytes 80 | tf_op jit(solution)/shard_map/ppermute | solution.py:18
  86.5 18.8 %collective-permute-start.28 = (f32[1,6]{1,0:T(1,128)S(1)}, f32[1,6]{1,0:T(1,128)S(1)}, u32[]{:S(2)}, u32[]{:S(2)}) collective-permute-start(f32[1,6]{1,0:T(1,128)S(1)} %get-tuple-element.35), channel_id=1, source_target_pairs={{16,0},{24,8},{32,16},{40,24},{48,32},{56,40},{64,48},{72,56},{80,... | collective-permute-start | bytes 80 | tf_op jit(solution)/shard_map/ppermute | solution.py:18
  87.8 19.4 %collective-permute-start.16 = (f32[1,6]{1,0:T(1,128)S(1)}, f32[1,6]{1,0:T(1,128)S(1)}, u32[]{:S(2)}, u32[]{:S(2)}) collective-permute-start(f32[1,6]{1,0:T(1,128)S(1)} %get-tuple-element.46), channel_id=1, source_target_pairs={{32,0},{40,8},{48,16},{56,24},{64,32},{72,40},{80,48},{88,56},{96,... | collective-permute-start | bytes 80 | tf_op jit(solution)/shard_map/ppermute | solution.py:18
  89.1 19.9 %collective-permute-start.3 = (f32[1,6]{1,0:T(1,128)S(1)}, f32[1,6]{1,0:T(1,128)S(1)}, u32[]{:S(2)}, u32[]{:S(2)}) collective-permute-start(f32[1,6]{1,0:T(1,128)S(1)} %get-tuple-element.56), channel_id=1, source_target_pairs={{0,32},{8,40},{16,48},{24,56},{32,64},{40,72},{48,80},{56,88},{64,... | collective-permute-start | bytes 80 | tf_op jit(solution)/shard_map/ppermute | solution.py:18
  99.5 15.7 %collective-permute-start.42 = (f32[1,6]{1,0:T(1,128)S(1)}, f32[1,6]{1,0:T(1,128)S(1)}, u32[]{:S(2)}, u32[]{:S(2)}) collective-permute-start(f32[1,6]{1,0:T(1,128)S(1)} %get-tuple-element.21), channel_id=1, source_target_pairs={{0,32},{8,40},{16,48},{24,56},{32,64},{40,72},{48,80},{56,88},{64,... | collective-permute-start | bytes 80 | tf_op jit(solution)/shard_map/ppermute | solution.py:18
  105.9 13.3 %collective-permute-start.29 = (f32[1,6]{1,0:T(1,128)S(1)}, f32[1,6]{1,0:T(1,128)S(1)}, u32[]{:S(2)}, u32[]{:S(2)}) collective-permute-start(f32[1,6]{1,0:T(1,128)S(1)} %get-tuple-element.33), channel_id=1, source_target_pairs={{32,0},{40,8},{48,16},{56,24},{64,32},{72,40},{80,48},{88,56},{96,... | collective-permute-start | bytes 80 | tf_op jit(solution)/shard_map/ppermute | solution.py:18
  107.7 13.2 %collective-permute-start.17 = (f32[1,6]{1,0:T(1,128)S(1)}, f32[1,6]{1,0:T(1,128)S(1)}, u32[]{:S(2)}, u32[]{:S(2)}) collective-permute-start(f32[1,6]{1,0:T(1,128)S(1)} %get-tuple-element.44), channel_id=1, source_target_pairs={{64,0},{72,8},{80,16},{88,24},{96,32},{104,40},{112,48},{120,56},{... | collective-permute-start | bytes 80 | tf_op jit(solution)/shard_map/ppermute | solution.py:18
  109.0 13.7 %collective-permute-start.4 = (f32[1,6]{1,0:T(1,128)S(1)}, f32[1,6]{1,0:T(1,128)S(1)}, u32[]{:S(2)}, u32[]{:S(2)}) collective-permute-start(f32[1,6]{1,0:T(1,128)S(1)} %get-tuple-element.54), channel_id=1, source_target_pairs={{0,64},{8,72},{16,80},{24,88},{32,96},{40,104},{48,112},{56,120},{... | collective-permute-start | bytes 80 | tf_op jit(solution)/shard_map/ppermute | solution.py:18
  115.8 19.1 %collective-permute-start.43 = (f32[1,6]{1,0:T(1,128)S(1)}, f32[1,6]{1,0:T(1,128)S(1)}, u32[]{:S(2)}, u32[]{:S(2)}) collective-permute-start(f32[1,6]{1,0:T(1,128)S(1)} %get-tuple-element.19), channel_id=1, source_target_pairs={{0,64},{8,72},{16,80},{24,88},{32,96},{40,104},{48,112},{56,120},{... | collective-permute-start | bytes 80 | tf_op jit(solution)/shard_map/ppermute | solution.py:18
  119.7 21.7 %collective-permute-start.30 = (f32[1,6]{1,0:T(1,128)S(1)}, f32[1,6]{1,0:T(1,128)S(1)}, u32[]{:S(2)}, u32[]{:S(2)}) collective-permute-start(f32[1,6]{1,0:T(1,128)S(1)} %get-tuple-element.31), channel_id=1, source_target_pairs={{64,0},{72,8},{80,16},{88,24},{96,32},{104,40},{112,48},{120,56},{... | collective-permute-start | bytes 80 | tf_op jit(solution)/shard_map/ppermute | solution.py:18
  121.5 30.2 %collective-permute-start.18 = (f32[1,6]{1,0:T(1,128)S(1)}, f32[1,6]{1,0:T(1,128)S(1)}, u32[]{:S(2)}, u32[]{:S(2)}) collective-permute-start(f32[1,6]{1,0:T(1,128)S(1)} %get-tuple-element.42), channel_id=1, source_target_pairs={{128,0},{136,8},{144,16},{152,24},{160,32},{168,40},{176,48},{184,... | collective-permute-start | bytes 80 | tf_op jit(solution)/shard_map/ppermute | solution.py:18
  123.3 135.8 %collective-permute-start.5 = (f32[1,6]{1,0:T(1,128)}, f32[1,6]{1,0:T(1,128)}, u32[]{:S(2)}, u32[]{:S(2)}) collective-permute-start(f32[1,6]{1,0:T(1,128)} %get-tuple-element.52), channel_id=1, source_target_pairs={{0,128},{8,136},{16,144},{24,152},{32,160},{40,168},{48,176},{56,1... | collective-permute-start | bytes 80 | tf_op jit(solution)/shard_map/ppermute | solution.py:18
  135.5 173.7 %collective-permute-start.44 = (f32[1,6]{1,0:T(1,128)}, f32[1,6]{1,0:T(1,128)}, u32[]{:S(2)}, u32[]{:S(2)}) collective-permute-start(f32[1,6]{1,0:T(1,128)} %get-tuple-element.17), channel_id=1, source_target_pairs={{0,128},{8,136},{16,144},{24,152},{32,160},{40,168},{48,176},{56,1... | collective-permute-start | bytes 80 | tf_op jit(solution)/shard_map/ppermute | solution.py:18
  141.9 172.0 %collective-permute-start.31 = (f32[1,6]{1,0:T(1,128)}, f32[1,6]{1,0:T(1,128)}, u32[]{:S(2)}, u32[]{:S(2)}) collective-permute-start(f32[1,6]{1,0:T(1,128)} %get-tuple-element.29), channel_id=1, source_target_pairs={{128,0},{136,8},{144,16},{152,24},{160,32},{168,40},{176,48},{184,... | collective-permute-start | bytes 80 | tf_op jit(solution)/shard_map/ppermute | solution.py:18
  143.2 17.4 %collective-permute-start.7 = (f32[1,6,128,64]{2,3,1,0:T(8,128)}, f32[1,6,128,64]{2,3,1,0:T(8,128)}, u32[]{:S(2)}, u32[]{:S(2)}) collective-permute-start(f32[1,6,128,64]{2,3,1,0:T(8,128)} %collective-permute-done.6), channel_id=1, source_target_pairs={{0,8},{8,16},{16,24},{24,32},{32,40},{40,48},{48,56},{56,64},{64,7... | collective-permute-start | bytes 589832 | tf_op jit(solution)/shard_map/ppermute | solution.py:18
  161.7 8.3 %collective-permute-start.8 = (f32[1,6,128,64]{2,3,1,0:T(8,128)S(1)}, f32[1,6,128,64]{2,3,1,0:T(8,128)S(1)}, u32[]{:S(2)}, u32[]{:S(2)}) collective-permute-start(f32[1,6,128,64]{2,3,1,0:T(8,128)S(1)} %multiply_add_fusion.24), channel_id=1, source_target_pairs={{0,16},{8,24},{16,32},{24,40},{32,48},{40,56},{48,64},{56,72},{64,... | collective-permute-start | bytes 589832 | tf_op jit(solution)/shard_map/ppermute | solution.py:18
  165.7 11.9 %collective-permute-start.21 = (f32[1,6,128,64]{2,3,1,0:T(8,128)S(1)}, f32[1,6,128,64]{2,3,1,0:T(8,128)S(1)}, u32[]{:S(2)}, u32[]{:S(2)}) collective-permute-start(f32[1,6,128,64]{2,3,1,0:T(8,128)S(1)} %multiply_add_fusion.18), channel_id=1, source_target_pairs={{16,0},{24,8},{32,16},{40,24},{48,32},{56,40},{64,48},{72,56},{80,... | collective-permute-start | bytes 589832 | tf_op jit(solution)/shard_map/ppermute | solution.py:18
  170.1 11.8 %collective-permute-start.9 = (f32[1,6,128,64]{2,3,1,0:T(8,128)S(1)}, f32[1,6,128,64]{2,3,1,0:T(8,128)S(1)}, u32[]{:S(2)}, u32[]{:S(2)}) collective-permute-start(f32[1,6,128,64]{2,3,1,0:T(8,128)S(1)} %multiply_add_fusion.23), channel_id=1, source_target_pairs={{0,32},{8,40},{16,48},{24,56},{32,64},{40,72},{48,80},{56,88},{64,... | collective-permute-start | bytes 589832 | tf_op jit(solution)/shard_map/ppermute | solution.py:18
  177.8 12.4 %collective-permute-start.22 = (f32[1,6,128,64]{2,3,1,0:T(8,128)S(1)}, f32[1,6,128,64]{2,3,1,0:T(8,128)S(1)}, u32[]{:S(2)}, u32[]{:S(2)}) collective-permute-start(f32[1,6,128,64]{2,3,1,0:T(8,128)S(1)} %multiply_add_fusion.17), channel_id=1, source_target_pairs={{32,0},{40,8},{48,16},{56,24},{64,32},{72,40},{80,48},{88,56},{96,... | collective-permute-start | bytes 589832 | tf_op jit(solution)/shard_map/ppermute | solution.py:18
  182.0 10.7 %collective-permute-start.10 = (f32[1,6,128,64]{2,3,1,0:T(8,128)S(1)}, f32[1,6,128,64]{2,3,1,0:T(8,128)S(1)}, u32[]{:S(2)}, u32[]{:S(2)}) collective-permute-start(f32[1,6,128,64]{2,3,1,0:T(8,128)S(1)} %multiply_add_fusion.22), channel_id=1, source_target_pairs={{0,64},{8,72},{16,80},{24,88},{32,96},{40,104},{48,112},{56,120},{... | collective-permute-start | bytes 589832 | tf_op jit(solution)/shard_map/ppermute | solution.py:18
  190.2 14.5 %collective-permute-start.23 = (f32[1,6,128,64]{2,3,1,0:T(8,128)S(1)}, f32[1,6,128,64]{2,3,1,0:T(8,128)S(1)}, u32[]{:S(2)}, u32[]{:S(2)}) collective-permute-start(f32[1,6,128,64]{2,3,1,0:T(8,128)S(1)} %multiply_add_fusion.16), channel_id=1, source_target_pairs={{64,0},{72,8},{80,16},{88,24},{96,32},{104,40},{112,48},{120,56},{... | collective-permute-start | bytes 589832 | tf_op jit(solution)/shard_map/ppermute | solution.py:18
  193.5 57.1 %collective-permute-start.11 = (f32[1,6,128,64]{2,3,1,0:T(8,128)}, f32[1,6,128,64]{2,3,1,0:T(8,128)}, u32[]{:S(2)}, u32[]{:S(2)}) collective-permute-start(f32[1,6,128,64]{2,3,1,0:T(8,128)} %multiply_add_fusion.21), channel_id=1, source_target_pairs={{0,128},{8,136},{16,144},{24,152},{32,160},{40,168},{48,176},{56,1... | collective-permute-start | bytes 589832 | tf_op jit(solution)/shard_map/ppermute | solution.py:18
  204.8 15.1 %collective-permute-start.24 = (f32[1,6,128,64]{2,3,1,0:T(8,128)S(1)}, f32[1,6,128,64]{2,3,1,0:T(8,128)S(1)}, u32[]{:S(2)}, u32[]{:S(2)}) collective-permute-start(f32[1,6,128,64]{2,3,1,0:T(8,128)S(1)} %multiply_add_fusion.15), channel_id=1, source_target_pairs={{128,0},{136,8},{144,16},{152,24},{160,32},{168,40},{176,48},{184,... | collective-permute-start | bytes 589832 | tf_op jit(solution)/shard_map/ppermute | solution.py:18
  220.1 10.4 %collective-permute-start.25 = (f32[1,6,128,64]{2,3,1,0:T(8,128)S(1)}, f32[1,6,128,64]{2,3,1,0:T(8,128)S(1)}, u32[]{:S(2)}, u32[]{:S(2)}) collective-permute-start(f32[1,6,128,64]{2,3,1,0:T(8,128)S(1)} %multiply_add_fusion.14), channel_id=1, source_target_pairs={{256,0},{264,8},{272,16},{280,24},{288,32},{296,40},{304,48},{312,... | collective-permute-start | bytes 589832 | tf_op jit(solution)/shard_map/ppermute | solution.py:18
  234.5 31.2 %all-to-all-start.1 = ((bf16[64,8,384]{2,1,0:T(8,128)(2,1)}), bf16[64,8,384]{2,1,0:T(8,128)(2,1)S(1)}, u32[]{:S(2)}, u32[]{:S(2)}) async-start(bf16[64,8,384]{2,1,0:T(8,128)(2,1)} %broadcast_select_fusion.4), calls=%async_computation.1 | async-start | bytes 786432 | tf_op jit(solution)/shard_map/all_to_all | solution.py:96
  251.7 12.8 %collective-permute-start.12 = (f32[1,6,128,64]{2,3,1,0:T(8,128)S(1)}, f32[1,6,128,64]{2,3,1,0:T(8,128)S(1)}, u32[]{:S(2)}, u32[]{:S(2)}) collective-permute-start(f32[1,6,128,64]{2,3,1,0:T(8,128)S(1)} %multiply_add_fusion.20), channel_id=1, source_target_pairs={{0,256},{8,264},{16,272},{24,280},{32,288},{40,296},{48,304},{56,3... | collective-permute-start | bytes 589832 | tf_op jit(solution)/shard_map/ppermute | solution.py:18
  290.9 33.3 %all-to-all-start.2 = ((bf16[64,8,384]{2,1,0:T(8,128)(2,1)}), bf16[64,8,384]{2,1,0:T(8,128)(2,1)S(1)}, u32[]{:S(2)}, u32[]{:S(2)}) async-start(bf16[64,8,384]{2,1,0:T(8,128)(2,1)} %broadcast_select_fusion.2), calls=%async_computation.2 | async-start | bytes 786432 | tf_op jit(solution)/shard_map/all_to_all | solution.py:96
  311.5 8.8 %collective-permute-start.32 = (f32[1,6,128,64]{2,3,1,0:T(8,128)S(1)}, f32[1,6,128,64]{2,3,1,0:T(8,128)}, u32[]{:S(2)}, u32[]{:S(2)}) collective-permute-start(f32[1,6,128,64]{2,3,1,0:T(8,128)S(1)} %fusion.86), channel_id=1, source_target_pairs={{8,0},{16,8},{24,16},{32,24},{40,32},{48,40},{56,48},{64,56},{72,6... | collective-permute-start | bytes 589832 | tf_op jit(solution)/shard_map/ppermute | solution.py:18
  320.4 18.8 %collective-permute-start.33 = (f32[1,6,128,64]{2,3,1,0:T(8,128)}, f32[1,6,128,64]{2,3,1,0:T(8,128)}, u32[]{:S(2)}, u32[]{:S(2)}) collective-permute-start(f32[1,6,128,64]{2,3,1,0:T(8,128)} %collective-permute-done.32), channel_id=1, source_target_pairs={{8,0},{16,8},{24,16},{32,24},{40,32},{48,40},{56,48},{64,56},{72,6... | collective-permute-start | bytes 589832 | tf_op jit(solution)/shard_map/ppermute | solution.py:18
  347.9 25.8 %collective-permute-start.35 = (f32[1,6,128,64]{2,3,1,0:T(8,128)S(1)}, f32[1,6,128,64]{2,3,1,0:T(8,128)S(1)}, u32[]{:S(2)}, u32[]{:S(2)}) collective-permute-start(f32[1,6,128,64]{2,3,1,0:T(8,128)S(1)} %multiply_add_fusion.11), channel_id=1, source_target_pairs={{32,0},{40,8},{48,16},{56,24},{64,32},{72,40},{80,48},{88,56},{96,... | collective-permute-start | bytes 589832 | tf_op jit(solution)/shard_map/ppermute | solution.py:18
  350.3 15.2 %collective-permute-start.48 = (f32[1,6,128,64]{2,3,1,0:T(8,128)S(1)}, f32[1,6,128,64]{2,3,1,0:T(8,128)S(1)}, u32[]{:S(2)}, u32[]{:S(2)}) collective-permute-start(f32[1,6,128,64]{2,3,1,0:T(8,128)S(1)} %multiply_add_fusion.5), channel_id=1, source_target_pairs={{0,32},{8,40},{16,48},{24,56},{32,64},{40,72},{48,80},{56,88},{64,... | collective-permute-start | bytes 589832 | tf_op jit(solution)/shard_map/ppermute | solution.py:18
  365.6 10.6 %collective-permute-start.49 = (f32[1,6,128,64]{2,3,1,0:T(8,128)S(1)}, f32[1,6,128,64]{2,3,1,0:T(8,128)S(1)}, u32[]{:S(2)}, u32[]{:S(2)}) collective-permute-start(f32[1,6,128,64]{2,3,1,0:T(8,128)S(1)} %multiply_add_fusion.4), channel_id=1, source_target_pairs={{0,64},{8,72},{16,80},{24,88},{32,96},{40,104},{48,112},{56,120},{... | collective-permute-start | bytes 589832 | tf_op jit(solution)/shard_map/ppermute | solution.py:18
  380.4 20.7 %collective-permute-start.37 = (f32[1,6,128,64]{2,3,1,0:T(8,128)S(1)}, f32[1,6,128,64]{2,3,1,0:T(8,128)S(1)}, u32[]{:S(2)}, u32[]{:S(2)}) collective-permute-start(f32[1,6,128,64]{2,3,1,0:T(8,128)S(1)} %multiply_add_fusion.9), channel_id=1, source_target_pairs={{128,0},{136,8},{144,16},{152,24},{160,32},{168,40},{176,48},{184,... | collective-permute-start | bytes 589832 | tf_op jit(solution)/shard_map/ppermute | solution.py:18
  383.7 20.0 %collective-permute-start.51 = (f32[1,6,128,64]{2,3,1,0:T(8,128)S(1)}, f32[1,6,128,64]{2,3,1,0:T(8,128)S(1)}, u32[]{:S(2)}, u32[]{:S(2)}) collective-permute-start(f32[1,6,128,64]{2,3,1,0:T(8,128)S(1)} %multiply_add_fusion.2), channel_id=1, source_target_pairs={{0,256},{8,264},{16,272},{24,280},{32,288},{40,296},{48,304},{56,3... | collective-permute-start | bytes 589832 | tf_op jit(solution)/shard_map/ppermute | solution.py:18
  401.2 25.6 %collective-permute-start.38 = (f32[1,6,128,64]{2,3,1,0:T(8,128)S(1)}, f32[1,6,128,64]{2,3,1,0:T(8,128)}, u32[]{:S(2)}, u32[]{:S(2)}) collective-permute-start(f32[1,6,128,64]{2,3,1,0:T(8,128)S(1)} %multiply_add_fusion.8), channel_id=1, source_target_pairs={{256,0},{264,8},{272,16},{280,24},{288,32},{296,40},{304,48},{312,... | collective-permute-start | bytes 589832 | tf_op jit(solution)/shard_map/ppermute | solution.py:18
  407.1 32.7 %all-to-all-start.3 = ((bf16[64,8,384]{2,1,0:T(8,128)(2,1)}), bf16[64,8,384]{2,1,0:T(8,128)(2,1)S(1)}, u32[]{:S(2)}, u32[]{:S(2)}) async-start(bf16[64,8,384]{2,1,0:T(8,128)(2,1)} %broadcast_select_fusion.3), calls=%async_computation.3 | async-start | bytes 786432 | tf_op jit(solution)/shard_map/all_to_all | solution.py:96
  (75 other events, 1134.1 us)
where the time goes:
time: 445 us; the launch traced here: 443 us
  starting transfers between devices  266 us (60%)
  waiting for transfers between devices  65.9 us (15%)
  other arithmetic  50 us (11%)
  local copies, waits for them, and re-layouts  24.5 us (6%)
  blocking collectives  19.4 us (4%)
  matrix products  13.8 us (3%)
    ppermute x52, starting transfers between devices, passed_along(): return lax.ppermute(block, axis, route)  206 us
    all_to_all x4, starting transfers between devices, reorder(): lax.all_to_all(outgoing, 'seq', split_axis=0, concat_axis=0, tiled=True)  60.3 us
    ppermute x52, waiting for transfers between devices, passed_along(): return lax.ppermute(block, axis, route)  52.9 us
    psum x1, blocking collectives, shards(): squares = lax.psum(jnp.sum(combined * combined, axis=1), 'head')  19.4 us
    all_to_all x4, waiting for transfers between devices, reorder(): lax.all_to_all(outgoing, 'seq', split_axis=0, concat_axis=0, tiled=True)  12.9 us
    mul x22, other arithmetic, combine(): jnp.exp(latter[0])[..., None, None] * earlier[1] + latter[1]  12.9 us
  transfers between devices with their start and end apart: 56, of which 19 were waited for; matrix products, arithmetic and copies ran while one was open for 18% of the time, Pallas kernels for 0%

commit v1 on v0

v1 whole, which is shorter than its diff:
```python
import jax
import jax.numpy as jnp
from jax import lax
from jax.experimental import pallas as pl
from jax.experimental.pallas import tpu as pltpu
from jax.sharding import PartitionSpec as P

TOK = 512
UNIT = 8
UNITS = 64
HEADS = 6
WIDTH = 384
STATE = 128
SPAN = 256
FEATURES = 3072
CUT = 96
LANES = 128
EPSILON = 1e-05
F32 = jnp.float32
BF16 = jnp.bfloat16


def dot(a, b, ca=1, cb=0, precision=None):
    return lax.dot_general(
        a, b, (((ca,), (cb,)), ((), ())), precision=precision, preferred_element_type=F32
    )


def iota(shape, dim):
    return lax.broadcasted_iota(jnp.int32, shape, dim)


def indicator(mask, dtype=BF16):
    return jnp.where(mask, 1.0, 0.0).astype(dtype)


def partner_rows(index_ref):
    partner = (index_ref[...] >> 6).astype(F32)
    return jnp.broadcast_to(partner, (16, UNITS)).astype(BF16)


def send_matrix(index_ref):
    repeat = indicator((iota((UNITS, TOK), 1) >> 3) == iota((UNITS, TOK), 0))
    partner = dot(partner_rows(index_ref), repeat)[0:1].astype(jnp.int32)
    target = partner * UNIT + (iota((1, TOK), 1) & 7)
    return indicator(iota((TOK, TOK), 0) == target)


def receive_matrix(index_ref):
    repeat = indicator((iota((TOK, UNITS), 0) >> 3) == iota((TOK, UNITS), 1))
    partner = dot(repeat, partner_rows(index_ref), 1, 1)[:, 0:1].astype(jnp.int32)
    source = partner * UNIT + (iota((TOK, 1), 0) & 7)
    return indicator(iota((TOK, TOK), 1) == source)


def padded_decay(decay_ref):
    decay = decay_ref[...].astype(F32)
    return jnp.concatenate([decay, jnp.zeros((16 - HEADS, TOK), F32)], axis=0).astype(BF16)


def lower_ones():
    return indicator(iota((TOK, TOK), 1) <= iota((TOK, TOK), 0))


def running_wide(decay, lower):
    spread = indicator((iota((16, WIDTH), 1) >> 6) == iota((16, WIDTH), 0))
    return dot(lower, dot(decay, spread, 0, 0).astype(BF16))


def cut_state(state):
    state = state.astype(BF16)
    row, col = iota((WIDTH, LANES), 0), iota((WIDTH, LANES), 1)
    parts = [
        dot(state, indicator((row == CUT * part + col) & (col < CUT))) for part in range(WIDTH // CUT)
    ]
    return jnp.concatenate(parts, axis=0)


def join_state(slices):
    row, col = iota((LANES, WIDTH), 0), iota((LANES, WIDTH), 1)
    total = None
    for part in range(WIDTH // CUT):
        place = indicator((col == CUT * part + row) & (row < CUT))
        piece = dot(slices[STATE * part : STATE * (part + 1)], place)
        total = piece if total is None else total + piece
    return total.astype(BF16)


def local_state(keys, values, weight):
    return dot(keys, (values.astype(F32) * weight).astype(BF16), 0, 0)


def three_parts(value):
    high = value.astype(BF16).astype(F32)
    middle = (value - high).astype(BF16).astype(F32)
    return high, middle, value - high - middle


def slice_heads():
    part = lax.axis_index("seq") >> 4
    first = part + (part >> 1)
    return first, first + 1, 64 - 32 * (part & 1)


def link_logs(slices, lane):
    column = iota((TOK, LANES), 1)
    held = jnp.where((column >= lane) & (column < lane + 3), slices.astype(F32), 0.0)
    total = jnp.sum(held, axis=1, keepdims=True)
    first, second, _ = slice_heads()
    earlier = indicator((iota((UNITS, TOK), 1) >> 3) < iota((UNITS, TOK), 0), F32)
    result = []
    for head in (first, second):
        own = jnp.where((iota((TOK, 1), 0) & 7) == head, total, 0.0)
        past = jnp.where((iota((TOK, UNITS), 0) >> 3) > iota((TOK, UNITS), 1), own, 0.0)
        logs = dot(earlier, past, precision=lax.Precision.HIGHEST)
        before = iota((UNITS, UNITS), 1) < iota((UNITS, UNITS), 0)
        result.append(jnp.where(before, jnp.exp(jnp.minimum(logs, 0.0)), 0.0).astype(BF16))
    return result


def expand_links(links, causal):
    unit = indicator((iota((TOK, UNITS), 0) >> 3) == iota((TOK, UNITS), 1))
    same = (iota((TOK, TOK), 0) & 7) == (iota((TOK, TOK), 1) & 7)
    half = dot(unit, links, 1, 0 if causal else 1).astype(BF16)
    return jnp.where(same, dot(half, unit, 1, 1), 0.0).astype(BF16)


def carry(first, second, slices):
    lane = iota((TOK, LANES), 1)
    _, _, border = slice_heads()
    mixed = jnp.where(lane < border, dot(first, slices), dot(second, slices))
    return jnp.where(lane < CUT, mixed, 0.0)


def span_rows(index):
    return slice(SPAN * index, SPAN * (index + 1))


def build_inner(rows_ref, cols_ref, decay, lower, inner_ref):
    down = dot(lower, decay, 1, 1)
    across = dot(decay, lower, 1, 1)
    allowed = iota((SPAN, SPAN), 1) <= iota((SPAN, SPAN), 0)
    for index in range(TOK // SPAN):
        span = span_rows(index)
        scores = jnp.where(allowed, dot(rows_ref[span, :], cols_ref[span, :], 1, 1), 0.0)
        for head in range(HEADS):
            spread = down[span, head : head + 1] - across[head : head + 1, span]
            weight = scores * jnp.exp(jnp.minimum(spread, 0.0))
            inner_ref[index, head] = weight.astype(BF16)


def apply_inner(inner_ref, values_ref, keys_ref, queries_ref, running, causal, out_ref):
    lane = iota((SPAN, LANES), 1)
    border = running[SPAN - 1 : SPAN]
    source, target = (0, 1) if causal else (1, 0)
    sign = 1.0 if causal else -1.0
    near = jnp.exp(sign * (border - running[span_rows(source)]))
    state = local_state(keys_ref[span_rows(source), :], values_ref[span_rows(source), :], near)
    far = jnp.exp(sign * (running[span_rows(target)] - border))
    crossing = far * dot(queries_ref[span_rows(target), :], state.astype(BF16))
    side = 1 if causal else 0
    for index in range(TOK // SPAN):
        span = span_rows(index)
        for pair in range(HEADS // 2):
            cols = slice(LANES * pair, LANES * (pair + 1))
            block = values_ref[span, cols]
            nothing = jnp.zeros_like(block)
            total = dot(inner_ref[index, 2 * pair], jnp.where(lane < 64, block, nothing), side, 0)
            total += dot(
                inner_ref[index, 2 * pair + 1], jnp.where(lane < 64, nothing, block), side, 0
            )
            if index == target:
                total += crossing[:, cols]
            out_ref[span, cols] = total


def open_raster(x, in_map, out_map, decay_f, decay_r, grad, route, pay):
    send = send_matrix(route)
    pay[:, 0:384] = dot(send, x[...]).astype(BF16)
    pay[:, 384:512] = dot(send, in_map[...]).astype(BF16)
    pay[:, 512:640] = dot(send, out_map[...]).astype(BF16)
    pay[:, 640:1024] = dot(send, grad[...]).astype(BF16)
    running = running_wide(padded_decay(decay_f), lower_ones())
    state = local_state(in_map[...], x[...], jnp.exp(running[TOK - 1 : TOK] - running))
    lane = iota((UNIT, LANES), 1)
    note = jnp.zeros((UNIT, LANES), F32)
    for place, decay_ref in ((CUT, decay_f), (CUT + 3, decay_r)):
        decay = jnp.concatenate([decay_ref[...].astype(F32), jnp.zeros((2, TOK), F32)], axis=0)
        for offset, part in enumerate(three_parts(jnp.sum(decay, axis=1, keepdims=True))):
            note = jnp.where(lane == place + offset, part, note)
    note = jnp.broadcast_to(note[None], (UNITS, UNIT, LANES)).reshape(TOK, LANES)
    pay[:, 1024:1152] = (cut_state(state) + note).astype(BF16)


def inner_raster(x, in_map, out_map, decay_f, decay_r, inner, local, run_f, run_r):
    lower = lower_ones()
    decay = padded_decay(decay_f)
    running = running_wide(decay, lower)
    run_f[...] = running
    run_r[...] = running_wide(padded_decay(decay_r), lower)
    build_inner(out_map, in_map, decay, lower, inner)
    apply_inner(inner, x, in_map, out_map, running, True, local)


def open_scan(got, run_r, route, x, in_map, out_map, grad, pay):
    take = receive_matrix(route)
    x[...] = dot(take, got[:, 0:384]).astype(BF16)
    in_map[...] = dot(take, got[:, 384:512]).astype(BF16)
    out_map[...] = dot(take, got[:, 512:640]).astype(BF16)
    grad[...] = dot(take, got[:, 640:1024]).astype(BF16)
    slices = got[:, 1024:1152]
    first, second = [expand_links(links, True) for links in link_logs(slices, CUT)]
    pay[:, 0:128] = carry(first, second, slices).astype(BF16)
    state = local_state(in_map[...], x[...], jnp.exp(run_r[...]))
    pay[:, 128:256] = cut_state(state).astype(BF16)


def inner_scan(got, x, in_map, out_map, decay_r, run_r, inner, local, links):
    lower = lower_ones()
    build_inner(in_map, out_map, padded_decay(decay_r), lower, inner)
    apply_inner(inner, x, in_map, out_map, run_r[...], False, local)
    slices = got[:, 1024:1152]
    for place, pair in enumerate(link_logs(slices, CUT + 3)):
        links[place] = expand_links(pair, False)
        links[2 + place] = expand_links(pair, True)
    for place, pair in enumerate(link_logs(slices, CUT)):
        links[4 + place] = expand_links(pair, False)


def finish_raster(got, out_map, local, run_f, links, route, y, pay):
    entering = join_state(got[:, 0:128])
    value = local[...] + jnp.exp(run_f[...]) * dot(out_map[...], entering)
    y[...] = value.astype(BF16)
    pay[:, 384:512] = carry(links[0], links[1], got[:, 128:256]).astype(BF16)
    pay[:, 0:384] = dot(send_matrix(route), y[...]).astype(BF16)


def finish_scan(got, out_map, local, run_r, x, grad, skip, gain, route, y, combined, stats):
    entering = join_state(got[:, 384:512])
    weight = jnp.exp(run_r[TOK - 1 : TOK, :] - run_r[...])
    y[...] = (local[...] + weight * dot(out_map[...], entering)).astype(BF16)
    y_forward = dot(receive_matrix(route), got[:, 0:384])
    total = y_forward + y[...].astype(F32) + skip[...] * x[...].astype(F32)
    combined[...] = total
    scaled = gain[...] * grad[...].astype(F32)
    ones = jnp.ones((16, WIDTH), F32)
    squares = dot(ones, total * total, 1, 1, lax.Precision.HIGHEST)[0:1]
    inner = dot(ones, total * scaled, 1, 1, lax.Precision.HIGHEST)[0:1]
    rows = [row[:, LANES * k : LANES * (k + 1)] for row in (squares, inner) for k in range(4)]
    tile = jnp.concatenate(rows, axis=0)
    stats[...] = jnp.broadcast_to(tile[None], (8, 8, LANES)).reshape(64, LANES)


def gradient(combined, scaled, scale, pull):
    return (scale * scaled - combined * pull).astype(BF16)


def open_back(stats, combined, y, out_map, grad, gain, run_r, route, back, pay):
    tile = jnp.sum(stats[...].reshape(8, 8, LANES), axis=0)
    squares = jnp.concatenate([tile[k : k + 1] for k in range(4)], axis=1)
    inner = jnp.concatenate([tile[k : k + 1] for k in range(4, 8)], axis=1)
    scale = lax.rsqrt(squares / FEATURES + EPSILON)
    pull = scale * scale * scale * inner / FEATURES
    parts = [*three_parts(scale), *three_parts(pull), jnp.zeros((10, TOK), F32)]
    parts = jnp.concatenate(parts, axis=0).astype(BF16)
    row, col = iota((16, 2 * WIDTH), 0), iota((16, 2 * WIDTH), 1)
    both = indicator(((row < 3) & (col < WIDTH)) | ((row >= 3) & (row < 6) & (col >= WIDTH)))
    wide = dot(parts, both, 0, 0)
    scaled = gain[...] * grad[...].astype(F32)
    back[...] = gradient(combined[...], scaled, wide[:, 0:WIDTH], wide[:, WIDTH:])
    running = run_r[...]
    state = local_state(out_map[...], back[...], jnp.exp(running[TOK - 1 : TOK] - running))
    send = send_matrix(route)
    pay[:, 0:384] = dot(send, y[...]).astype(BF16)
    lanes = indicator(iota((16, LANES), 1) == CUT + iota((16, LANES), 0))
    note = dot(send, dot(parts, lanes, 0, 0).astype(BF16))
    pay[:, 384:512] = (cut_state(state) + note).astype(BF16)


def inner_back_scan(inner, back, in_map, out_map, run_r, local):
    apply_inner(inner, back, out_map, in_map, run_r[...], True, local)


def middle_raster(
    got, y_forward, x, out_map, grad, skip, gain, run_f, links, route, normed, back, pay
):
    take = receive_matrix(route)
    y_reverse = dot(take, got[:, 0:384])
    slices = got[:, 384:512]
    notes = dot(take, slices).astype(BF16)
    row, col = iota((LANES, 2 * WIDTH), 0) - CUT, iota((LANES, 2 * WIDTH), 1)
    both = indicator(
        ((row >= 0) & (row < 3) & (col < WIDTH)) | ((row >= 3) & (row < 6) & (col >= WIDTH))
    )
    wide = dot(notes, both)
    combined = y_forward[...].astype(F32) + y_reverse + skip[...] * x[...].astype(F32)
    scale = wide[:, 0:WIDTH]
    normed[...] = (combined * scale * gain[...]).astype(BF16)
    scaled = gain[...] * grad[...].astype(F32)
    back[...] = gradient(combined, scaled, scale, wide[:, WIDTH:])
    state = local_state(out_map[...], back[...], jnp.exp(run_f[...]))
    pay[:, 0:128] = carry(links[2], links[3], slices).astype(BF16)
    pay[:, 128:256] = cut_state(state).astype(BF16)


def inner_back_raster(inner, back, in_map, out_map, run_f, local):
    apply_inner(inner, back, out_map, in_map, run_f[...], False, local)


def finish_back_scan(got, in_map, local, run_r, links, route, pay):
    entering = join_state(got[:, 0:128])
    value = (local[...] + jnp.exp(run_r[...]) * dot(in_map[...], entering)).astype(BF16)
    pay[:, 384:512] = carry(links[4], links[5], got[:, 128:256]).astype(BF16)
    pay[:, 0:384] = dot(send_matrix(route), value).astype(BF16)


def finish_back_raster(got, in_map, local, run_f, back, skip, route, out):
    entering = join_state(got[:, 384:512])
    weight = jnp.exp(run_f[TOK - 1 : TOK, :] - run_f[...])
    grad_forward = (local[...] + weight * dot(in_map[...], entering)).astype(BF16).astype(F32)
    grad_reverse = dot(receive_matrix(route), got[:, 0:384])
    total = grad_forward + grad_reverse + skip[...] * back[...].astype(F32)
    out[...] = total.astype(BF16)


def kernel(body, outs, *operands, flops=400_000_000):
    shapes = [jax.ShapeDtypeStruct(shape, dtype) for shape, dtype in outs]
    size = sum(a.size * a.dtype.itemsize for a in (*operands, *shapes))
    return pl.pallas_call(
        body,
        out_shape=shapes,
        compiler_params=pltpu.CompilerParams(vmem_limit_bytes=40 * 2**20),
        cost_estimate=pl.CostEstimate(flops=flops, bytes_accessed=size, transcendentals=0),
        name=body.__name__,
    )(*operands)


def exchange(pay):
    return lax.all_to_all(pay, "seq", split_axis=0, concat_axis=0, tiled=True)


def shards(
    ssm_input,
    input_map,
    output_map,
    decay_forward,
    decay_reverse,
    skip_gain,
    norm_gain,
    scan_order,
    raster_order,
    grad_normed,
):
    to_scan = raster_order.reshape(1, UNITS)
    to_raster = scan_order.reshape(1, UNITS)
    skip = jnp.repeat(skip_gain, WIDTH // HEADS).reshape(1, WIDTH)
    gain = norm_gain.reshape(1, WIDTH)
    wide16, wide32 = ((TOK, WIDTH), BF16), ((TOK, WIDTH), F32)
    rows16 = ((TOK, STATE), BF16)
    inner16 = ((TOK // SPAN, HEADS, SPAN, SPAN), BF16)

    def pay(lanes):
        return ((TOK, lanes), BF16)

    (pay1,) = kernel(
        open_raster, [pay(1152)],
        ssm_input, input_map, output_map, decay_forward, decay_reverse, grad_normed, to_scan,
    )
    got1 = exchange(pay1)
    inner_f, local_f, run_f, run_r = kernel(
        inner_raster, [inner16, wide32, wide32, wide32],
        ssm_input, input_map, output_map, decay_forward, decay_reverse, flops=8_000_000_000,
    )
    x_scan, in_scan, out_scan, grad_scan, pay2 = kernel(
        open_scan, [wide16, rows16, rows16, wide16, pay(256)], got1, run_r, to_raster
    )
    got2 = exchange(pay2)
    inner_r, local_r, links = kernel(
        inner_scan, [inner16, wide32, ((6, TOK, TOK), BF16)],
        got1, x_scan, in_scan, out_scan, decay_reverse, run_r, flops=8_000_000_000,
    )
    y_forward, pay3 = kernel(
        finish_raster, [wide16, pay(512)], got2, output_map, local_f, run_f, links, to_scan
    )
    got3 = exchange(pay3)
    y_scan, combined, stats = kernel(
        finish_scan, [wide16, wide32, ((64, LANES), F32)],
        got3, out_scan, local_r, run_r, x_scan, grad_scan, skip, gain, to_raster,
    )
    all_stats = lax.all_to_all(stats, "head", split_axis=0, concat_axis=0, tiled=True)
    back_scan, pay4 = kernel(
        open_back, [wide16, pay(512)],
        all_stats, combined, y_scan, out_scan, grad_scan, gain, run_r, to_raster,
    )
    got4 = exchange(pay4)
    (local_br,) = kernel(
        inner_back_scan, [wide32], inner_r, back_scan, in_scan, out_scan, run_r,
        flops=4_000_000_000,
    )
    normed, back, pay5 = kernel(
        middle_raster, [wide16, wide16, pay(256)],
        got4, y_forward, ssm_input, output_map, grad_normed, skip, gain, run_f, links, to_scan,
    )
    got5 = exchange(pay5)
    (local_bf,) = kernel(
        inner_back_raster, [wide32], inner_f, back, input_map, output_map, run_f,
        flops=4_000_000_000,
    )
    (pay6,) = kernel(
        finish_back_scan, [pay(512)], got5, in_scan, local_br, run_r, links, to_raster
    )
    got6 = exchange(pay6)
    (grad_input,) = kernel(
        finish_back_raster, [wide16], got6, input_map, local_bf, run_f, back, skip, to_scan
    )
    return normed, grad_input


def solution(mesh):
    return jax.shard_map(
        shards,
        mesh=mesh,
        in_specs=(
            P("seq", "head"),
            P("seq", "head"),
            P("seq", "head"),
            P("head", "seq"),
            P("head", "seq"),
            P("head"),
            P("head"),
            P("seq"),
            P("seq"),
            P("seq", "head"),
        ),
        out_specs=(P("seq", "head"), P("seq", "head")),
        check_vma=False,
    )
```

time: 445 us -> 217 us (0.49)
  starting transfers between devices: 266 us -> 37.9 us
  other arithmetic: 50 us -> 0 us
  Pallas kernels: 0 us -> 27.1 us
  blocking collectives: 19.4 us -> 41.4 us
  local copies, waits for them, and re-layouts: 24.5 us -> 46.3 us
  matrix products: 13.8 us -> 0 us
  waiting for transfers between devices: 65.9 us -> 61.1 us
    ppermute x52 -> x0, starting transfers between devices: 206 us -> none  [passed_along(): return lax.ppermute(block, axis, route)]
    ppermute x52 -> x0, waiting for transfers between devices: 52.9 us -> none  [passed_along(): return lax.ppermute(block, axis, route)]
    all_to_all x4 -> x5, waiting for transfers between devices: 12.9 us -> 61.1 us  [exchange(): return lax.all_to_all(pay, 'seq', split_axis=0, concat_axis=0, tiled=True)]
    unnamed x140 -> x136, local copies, waits for them, and re-layouts: 3.97 us -> 45.5 us
    all_to_all x0 -> x2, blocking collectives: none -> 41.4 us  [the longest x1 24.6 us: exchange(): return lax.all_to_all(pay, 'seq', split_axis=0, concat_axis=0, tiled=True)]
    pallas_call x0 -> x12, Pallas kernels: none -> 27.1 us  [kernel(): pl.pallas_call(body, out_shape=shapes, compiler_params=pltpu.CompilerPara...]
    all_to_all x4 -> x5, starting transfers between devices: 60.3 us -> 37.9 us  [exchange(): return lax.all_to_all(pay, 'seq', split_axis=0, concat_axis=0, tiled=True)]
    psum x1 -> x0, blocking collectives: 19.4 us -> none  [shards(): squares = lax.psum(jnp.sum(combined * combined, axis=1), 'head')]
  transfers between devices with their start and end apart: 56 -> 5, of which waited for: 19 -> 5; matrix products, arithmetic and copies ran while one was open for 18% -> 0% of each run, Pallas kernels for 0% -> 4%
where the time goes in v1:
time: 217 us; the launch traced here: 215 us
  waiting for transfers between devices  61.1 us (28%)
  local copies, waits for them, and re-layouts  46.3 us (21%)
  blocking collectives  41.4 us (19%)
  starting transfers between devices  37.9 us (17%)
  Pallas kernels  27.1 us (12%)
    all_to_all x5, waiting for transfers between devices, exchange(): return lax.all_to_all(pay, 'seq', split_axis=0, concat_axis=0, tiled=True)  61.1 us
    unnamed x136, local copies, waits for them, and re-layouts  45.5 us
    all_to_all x5, starting transfers between devices, exchange(): return lax.all_to_all(pay, 'seq', split_axis=0, concat_axis=0, tiled=True)  37.9 us
    pallas_call x12, Pallas kernels, kernel(): pl.pallas_call(body, out_shape=shapes, compiler_params=pltpu.CompilerPara...  27.1 us
    all_to_all x1, blocking collectives, exchange(): return lax.all_to_all(pay, 'seq', split_axis=0, concat_axis=0, tiled=True)  24.6 us
    all_to_all x1, blocking collectives, shards(): lax.all_to_all(stats, 'head', split_axis=0, concat_axis=0, tiled=True)  16.8 us
  transfers between devices with their start and end apart: 5, of which 5 were waited for; matrix products, arithmetic and copies ran while one was open for 0% of the time, Pallas kernels for 4%

profile of v1, /device:TPU:1, one launch (start us, length us, event | category | flops | bytes accessed | tf_op | source)
XLA Modules:
  0.0 214.9 jit_solution(10391600102105196173)
XLA Ops:
  0.6 1.0 copy-done.13
  1.6 1.0 copy-done.15
  2.6 0.9 copy-done.20
  3.5 0.9 copy-done.33
  6.5 3.1 %open_raster.1 = bf16[512,1152]{1,0:T(8,128)(2,1)} custom-call(bf16[512,384]{1,0:T(8,128)(2,1)S(1)} %copy-done.13, bf16[512,128]{1,0:T(8,128)(2,1)S(1)} %copy-done.33, bf16[512,128]{1,0:T(8,128)(2,1)S(1)} %copy-done.20, bf16[6,512]{1,0:T(8,128)(2,1)S(1)} %copy-done.54, bf16[6,512]{1,0:T(8,128)(2,1)S(1)} %copy-done.56, bf16[512,384]{1,0:T(8,128)(2,1)S(1)} %copy-done.15, ...), custom_call_target="tpu_custom_call" | custom-call | flops 400000000 | bytes 2240768 | tf_op jit(solution)/shard_map/open_raster/pallas_call | solution.py:329
  9.6 11.8 %all-to-all-start = ((bf16[64,8,1152]{2,1,0:T(8,128)(2,1)}), bf16[64,8,1152]{2,1,0:T(8,128)(2,1)S(1)}, u32[]{:S(2)}, u32[]{:S(2)}) async-start(bf16[64,8,1152]{2,1,0:T(8,128)(2,1)} %bitcast.1), calls=%async_computation | async-start | bytes 2359296 | tf_op jit(solution)/shard_map/all_to_all | solution.py:339
  21.5 2.4 %inner_raster.1 = (bf16[2,6,256,256]{3,2,1,0:T(8,128)(2,1)S(1)}, f32[512,384]{1,0:T(8,128)S(1)}, f32[512,384]{1,0:T(8,128)S(1)}, f32[512,384]{1,0:T(8,128)S(1)}) custom-call(bf16[512,384]{1,0:T(8,128)(2,1)S(1)} %copy-done.14, bf16[512,128]{1,0:T(8,128)(2,1)S(1)} %copy-done.34, bf16[512,128]{1,0:T(8,128)(2,1)S(1)} %copy-done.21, ...), custom_call_target="tpu_custom_call" | custom-call | flops 8000000000 | bytes 4599808 | tf_op jit(solution)/shard_map/inner_raster/pallas_call | solution.py:329
  24.8 0.9 copy-done.29
  25.7 1.1 copy-done.63
  26.8 25.2 %all-to-all-done = bf16[64,8,1152]{2,1,0:T(8,128)(2,1)S(1)} async-done(((bf16[64,8,1152]{2,1,0:T(8,128)(2,1)}), bf16[64,8,1152]{2,1,0:T(8,128)(2,1)S(1)}, u32[]{:S(2)}, u32[]{:S(2)}) %all-to-all-start) | async-done | bytes 1179680 | tf_op jit(solution)/shard_map/all_to_all | solution.py:339
  52.0 3.4 %open_scan.1 = (bf16[512,384]{1,0:T(8,128)(2,1)S(1)}, bf16[512,128]{1,0:T(8,128)(2,1)S(1)}, bf16[512,128]{1,0:T(8,128)(2,1)S(1)}, bf16[512,384]{1,0:T(8,128)(2,1)S(1)}, bf16[512,256]{1,0:T(8,128)(2,1)}) custom-call(bf16[512,1152]{1,0:T(8,128)(2,1)S(1)} %bitcast.16, f32[512,384]{1,0:T(8,128)S(1)} %get-tuple-element.24.run_r, s32[1,64]{1,0:T(1,128)S(1)} %bitcast.27), custom_call_target="tpu_custom_call" | custom-call | flops 400000000 | bytes 3277056 | tf_op jit(solution)/shard_map/open_scan/pallas_call | solution.py:329
  56.8 6.8 %all-to-all-start.1 = ((bf16[64,8,256]{2,1,0:T(8,128)(2,1)}), bf16[64,8,256]{2,1,0:T(8,128)(2,1)}, u32[]{:S(2)}, u32[]{:S(2)}) async-start(bf16[64,8,256]{2,1,0:T(8,128)(2,1)} %bitcast.4), calls=%async_computation.1 | async-start | bytes 524288 | tf_op jit(solution)/shard_map/all_to_all | solution.py:339
  63.7 1.1 copy-done.1
  64.8 1.3 copy-done.11
  67.0 1.0 copy-done.47
  68.9 4.2 %inner_scan.1 = (bf16[2,6,256,256]{3,2,1,0:T(8,128)(2,1)S(1)}, f32[512,384]{1,0:T(8,128)S(1)}, bf16[6,512,512]{2,1,0:T(8,128)(2,1)S(1)}) custom-call(bf16[512,1152]{1,0:T(8,128)(2,1)S(1)} %bitcast.17, bf16[512,384]{1,0:T(8,128)(2,1)S(1)} %copy-done.47, bf16[512,128]{1,0:T(8,128)(2,1)S(1)} %copy-done.51, bf16[512,128]{1,0:T(8,128)(2,1)S(1)} %copy-done.38, ...), custom_call_target="tpu_custom_call" | custom-call | flops 8000000000 | bytes 8132608 | tf_op jit(solution)/shard_map/inner_scan/pallas_call | solution.py:329
  73.9 1.2 copy-done.65
  75.1 1.6 all-to-all-done.1
  76.7 1.1 copy-done.6
  78.7 1.1 copy-done.30
  79.9 2.1 finish_raster.1
  83.6 8.9 %all-to-all-start.2 = ((bf16[64,8,512]{2,1,0:T(8,128)(2,1)}), bf16[64,8,512]{2,1,0:T(8,128)(2,1)}, u32[]{:S(2)}, u32[]{:S(2)}) async-start(bf16[64,8,512]{2,1,0:T(8,128)(2,1)} %bitcast.22), calls=%async_computation.2 | async-start | bytes 1048576 | tf_op jit(solution)/shard_map/all_to_all | solution.py:339
  93.3 16.8 %all-to-all-done.2 = bf16[64,8,512]{2,1,0:T(8,128)(2,1)} async-done(((bf16[64,8,512]{2,1,0:T(8,128)(2,1)}), bf16[64,8,512]{2,1,0:T(8,128)(2,1)}, u32[]{:S(2)}, u32[]{:S(2)}) %all-to-all-start.2) | async-done | bytes 524320 | tf_op jit(solution)/shard_map/all_to_all | solution.py:339
  110.1 1.1 copy-done.2
  111.2 1.0 copy-done.18
  112.2 1.1 copy-done.26
  114.3 1.0 copy-done.48
  115.3 3.4 %finish_scan.1 = (bf16[512,384]{1,0:T(8,128)(2,1)S(1)}, f32[512,384]{1,0:T(8,128)S(1)}, f32[64,128]{1,0:T(8,128)S(1)}) custom-call(bf16[512,512]{1,0:T(8,128)(2,1)} %bitcast.7.got, bf16[512,128]{1,0:T(8,128)(2,1)S(1)} %copy-done.39, f32[512,384]{1,0:T(8,128)S(1)} %copy-done.26, f32[512,384]{1,0:T(8,128)S(1)} %copy-done.2, bf16[512,384]{1,0:T(8,128)(2,1)S(1)} %copy-done.48, ...), custom_call_target="tpu_custom_call" | custom-call | flops 400000000 | bytes 4230400 | tf_op jit(solution)/shard_map/finish_scan/pallas_call | solution.py:329
  118.7 16.8 %all_to_all.77 = f32[8,8,128]{2,1,0:T(8,128)S(1)} all-to-all(f32[8,8,128]{2,1,0:T(8,128)S(1)} %bitcast.26), channel_id=1, replica_groups=mesh['seq'=64,'head'=8] {'head'}, dimensions={0} | all-to-all | bytes 65536 | tf_op jit(solution)/shard_map/all_to_all | solution.py:390
  135.6 1.5 open_back.1
  137.1 24.6 %all_to_all.78 = bf16[64,8,512]{2,1,0:T(8,128)(2,1)S(1)} all-to-all(bf16[64,8,512]{2,1,0:T(8,128)(2,1)S(1)} %bitcast.23), channel_id=1, replica_groups=mesh['seq'=64,'head'=8] {'seq'}, dimensions={0} | all-to-all | bytes 1048576 | tf_op jit(solution)/shard_map/all_to_all | solution.py:339
  161.7 2.4 %middle_raster.1 = (bf16[512,384]{1,0:T(8,128)(2,1)}, bf16[512,384]{1,0:T(8,128)(2,1)S(1)}, bf16[512,256]{1,0:T(8,128)(2,1)S(1)}) custom-call(bf16[512,512]{1,0:T(8,128)(2,1)S(1)} %bitcast.20, bf16[512,384]{1,0:T(8,128)(2,1)S(1)} %copy-done.45, bf16[512,384]{1,0:T(8,128)(2,1)S(1)} %copy-done.14, bf16[512,128]{1,0:T(8,128)(2,1)S(1)} %copy-done.23, ...), custom_call_target="tpu_custom_call" | custom-call | flops 400000000 | bytes 6819072 | tf_op jit(solution)/shard_map/middle_raster/pallas_call | solution.py:329
  165.6 5.7 %all-to-all-start.5 = ((bf16[64,8,256]{2,1,0:T(8,128)(2,1)}), bf16[64,8,256]{2,1,0:T(8,128)(2,1)S(1)}, u32[]{:S(2)}, u32[]{:S(2)}) async-start(bf16[64,8,256]{2,1,0:T(8,128)(2,1)} %bitcast.24), calls=%async_computation.5 | async-start | bytes 524288 | tf_op jit(solution)/shard_map/all_to_all | solution.py:339
  171.3 1.1 copy-done.3
  174.2 1.0 copy-done.62
  175.2 1.4 copy-done.66
  178.4 6.1 %all-to-all-done.5 = bf16[64,8,256]{2,1,0:T(8,128)(2,1)S(1)} async-done(((bf16[64,8,256]{2,1,0:T(8,128)(2,1)}), bf16[64,8,256]{2,1,0:T(8,128)(2,1)S(1)}, u32[]{:S(2)}, u32[]{:S(2)}) %all-to-all-start.5) | async-done | bytes 262176 | tf_op jit(solution)/shard_map/all_to_all | solution.py:339
  184.4 1.1 copy-done.4
  185.6 1.1 copy-done.32
  187.6 1.1 finish_back_scan.1
  189.5 4.7 %all-to-all-start.6 = ((bf16[64,8,512]{2,1,0:T(8,128)(2,1)}), bf16[64,8,512]{2,1,0:T(8,128)(2,1)S(1)}, u32[]{:S(2)}, u32[]{:S(2)}) async-start(bf16[64,8,512]{2,1,0:T(8,128)(2,1)} %bitcast.19), calls=%async_computation.6 | async-start | bytes 1048576 | tf_op jit(solution)/shard_map/all_to_all | solution.py:339
  194.3 1.1 copy-done.8
  196.3 1.0 copy-done.43
  197.3 1.4 copy-done.64
  198.7 0.9 inner_back_raster.1.local
  200.5 11.5 %all-to-all-done.6 = bf16[64,8,512]{2,1,0:T(8,128)(2,1)S(1)} async-done(((bf16[64,8,512]{2,1,0:T(8,128)(2,1)}), bf16[64,8,512]{2,1,0:T(8,128)(2,1)S(1)}, u32[]{:S(2)}, u32[]{:S(2)}) %all-to-all-start.6) | async-done | bytes 524320 | tf_op jit(solution)/shard_map/all_to_all | solution.py:339
  212.0 1.1 copy-done.28
  213.1 1.7 finish_back_raster.1
  (115 shorter events, 19.8 us)
Async XLA Ops:
  0.6 1.0 copy-start.13
  1.6 1.0 copy-start.15
  9.6 11.8 %copy-start.14 = (bf16[512,384]{1,0:T(8,128)(2,1)S(1)}, bf16[512,384]{1,0:T(8,128)(2,1)}, u32[]{:S(2)}) copy-start(bf16[512,384]{1,0:T(8,128)(2,1)} %x.5) | copy-start | bytes 1179652
  9.6 11.8 %copy-start.21 = (bf16[512,128]{1,0:T(8,128)(2,1)S(1)}, bf16[512,128]{1,0:T(8,128)(2,1)}, u32[]{:S(2)}) copy-start(bf16[512,128]{1,0:T(8,128)(2,1)} %out_map.9) | copy-start | bytes 393220
  9.6 11.8 %copy-start.34 = (bf16[512,128]{1,0:T(8,128)(2,1)S(1)}, bf16[512,128]{1,0:T(8,128)(2,1)}, u32[]{:S(2)}) copy-start(bf16[512,128]{1,0:T(8,128)(2,1)} %in_map.7) | copy-start | bytes 393220
  9.6 11.8 %copy-start.55 = (bf16[6,512]{1,0:T(8,128)(2,1)S(1)}, bf16[6,512]{1,0:T(8,128)(2,1)}, u32[]{:S(2)}) copy-start(bf16[6,512]{1,0:T(8,128)(2,1)} %decay_f.3) | copy-start | bytes 18436
  9.6 11.8 %copy-start.57 = (bf16[6,512]{1,0:T(8,128)(2,1)S(1)}, bf16[6,512]{1,0:T(8,128)(2,1)}, u32[]{:S(2)}) copy-start(bf16[6,512]{1,0:T(8,128)(2,1)} %decay_r.5) | copy-start | bytes 18436
  9.6 42.4 %all-to-all-start = ((bf16[64,8,1152]{2,1,0:T(8,128)(2,1)}), bf16[64,8,1152]{2,1,0:T(8,128)(2,1)S(1)}, u32[]{:S(2)}, u32[]{:S(2)}) async-start(bf16[64,8,1152]{2,1,0:T(8,128)(2,1)} %bitcast.1), calls=%async_computation | async-start | bytes 2359296 | tf_op jit(solution)/shard_map/all_to_all | solution.py:339
  21.4 30.5 %copy-start.58 = (s32[64]{0:T(128)S(1)}, s32[64]{0:T(128)}, u32[]{:S(2)}) copy-start(s32[64]{0:T(128)} %param.17) | copy-start | bytes 772
  25.7 1.1 copy-start.63
  26.8 36.8 %copy-start = (f32[512,384]{1,0:T(8,128)}, f32[512,384]{1,0:T(8,128)S(1)}, u32[]{:S(2)}) copy-start(f32[512,384]{1,0:T(8,128)S(1)} %get-tuple-element.24.run_r) | copy-start | bytes 2359300
  52.0 11.6 %copy-start.10 = (bf16[64,8,1152]{2,1,0:T(8,128)(2,1)}, bf16[64,8,1152]{2,1,0:T(8,128)(2,1)S(1)}, u32[]{:S(2)}) copy-start(bf16[64,8,1152]{2,1,0:T(8,128)(2,1)S(1)} %all-to-all-done) | copy-start | bytes 3538948
  56.8 6.9 %copy-start.17 = (bf16[512,384]{1,0:T(8,128)(2,1)}, bf16[512,384]{1,0:T(8,128)(2,1)S(1)}, u32[]{:S(2)}) copy-start(bf16[512,384]{1,0:T(8,128)(2,1)S(1)} %get-tuple-element.34.grad) | copy-start | bytes 1179652
  56.8 6.9 %copy-start.50 = (bf16[512,128]{1,0:T(8,128)(2,1)}, bf16[512,128]{1,0:T(8,128)(2,1)S(1)}, u32[]{:S(2)}) copy-start(bf16[512,128]{1,0:T(8,128)(2,1)S(1)} %get-tuple-element.29.in_map) | copy-start | bytes 393220
  56.8 19.9 %all-to-all-start.1 = ((bf16[64,8,256]{2,1,0:T(8,128)(2,1)}), bf16[64,8,256]{2,1,0:T(8,128)(2,1)}, u32[]{:S(2)}, u32[]{:S(2)}) async-start(bf16[64,8,256]{2,1,0:T(8,128)(2,1)} %bitcast.4), calls=%async_computation.1 | async-start | bytes 524288 | tf_op jit(solution)/shard_map/all_to_all | solution.py:339
  63.7 1.1 copy-start.1
  64.8 1.3 copy-start.11
  67.0 1.0 copy-start.47
  68.9 7.8 %copy-start.60 = (s32[64]{0:T(128)S(1)}, s32[64]{0:T(128)}, u32[]{:S(2)}) copy-start(s32[64]{0:T(128)} %param.18) | copy-start | bytes 772
  73.9 1.2 copy-start.65
  76.7 1.1 copy-start.6
  78.7 1.1 copy-start.30
  79.9 12.6 %copy-start.67 = (f32[6]{0:T(128)S(1)}, f32[6]{0:T(128)}, u32[]{:S(2)}) copy-start(f32[6]{0:T(128)} %param.15) | copy-start | bytes 76
  83.6 26.5 %all-to-all-start.2 = ((bf16[64,8,512]{2,1,0:T(8,128)(2,1)}), bf16[64,8,512]{2,1,0:T(8,128)(2,1)}, u32[]{:S(2)}, u32[]{:S(2)}) async-start(bf16[64,8,512]{2,1,0:T(8,128)(2,1)} %bitcast.22), calls=%async_computation.2 | async-start | bytes 1048576 | tf_op jit(solution)/shard_map/all_to_all | solution.py:339
  110.1 1.1 copy-start.2
  111.2 1.0 copy-start.18
  112.2 1.1 copy-start.26
  114.3 1.0 copy-start.48
  115.3 20.3 %copy-start.19 = (bf16[512,384]{1,0:T(8,128)(2,1)S(1)}, bf16[512,384]{1,0:T(8,128)(2,1)}, u32[]{:S(2)}) copy-start(bf16[512,384]{1,0:T(8,128)(2,1)} %copy-done.17) | copy-start | bytes 1179652
  115.3 20.3 %copy-start.40 = (bf16[512,128]{1,0:T(8,128)(2,1)S(1)}, bf16[512,128]{1,0:T(8,128)(2,1)}, u32[]{:S(2)}) copy-start(bf16[512,128]{1,0:T(8,128)(2,1)} %copy-done.37) | copy-start | bytes 393220
  135.5 26.1 %copy-start.7 = (f32[512,384]{1,0:T(8,128)S(1)}, f32[512,384]{1,0:T(8,128)}, u32[]{:S(2)}) copy-start(f32[512,384]{1,0:T(8,128)} %copy-done.5) | copy-start | bytes 2359300
  135.5 26.1 %copy-start.16 = (bf16[512,384]{1,0:T(8,128)(2,1)S(1)}, bf16[512,384]{1,0:T(8,128)(2,1)}, u32[]{:S(2)}) copy-start(bf16[512,384]{1,0:T(8,128)(2,1)} %grad.3) | copy-start | bytes 1179652
  135.6 26.1 %copy-start.23 = (bf16[512,128]{1,0:T(8,128)(2,1)S(1)}, bf16[512,128]{1,0:T(8,128)(2,1)}, u32[]{:S(2)}) copy-start(bf16[512,128]{1,0:T(8,128)(2,1)} %out_map.9) | copy-start | bytes 393220
  135.6 26.1 %copy-start.45 = (bf16[512,384]{1,0:T(8,128)(2,1)S(1)}, bf16[512,384]{1,0:T(8,128)(2,1)}, u32[]{:S(2)}) copy-start(bf16[512,384]{1,0:T(8,128)(2,1)} %copy-done.44) | copy-start | bytes 1179652
  137.1 27.0 %copy-start.61 = (bf16[512,384]{1,0:T(8,128)(2,1)}, bf16[512,384]{1,0:T(8,128)(2,1)S(1)}, u32[]{:S(2)}) copy-start(bf16[512,384]{1,0:T(8,128)(2,1)S(1)} %get-tuple-element.43.back) | copy-start | bytes 1179652
  165.6 18.9 %all-to-all-start.5 = ((bf16[64,8,256]{2,1,0:T(8,128)(2,1)}), bf16[64,8,256]{2,1,0:T(8,128)(2,1)S(1)}, u32[]{:S(2)}, u32[]{:S(2)}) async-start(bf16[64,8,256]{2,1,0:T(8,128)(2,1)} %bitcast.24), calls=%async_computation.5 | async-start | bytes 524288 | tf_op jit(solution)/shard_map/all_to_all | solution.py:339
  171.3 1.1 copy-start.3
  174.2 1.0 copy-start.62
  175.2 1.4 copy-start.66
  184.4 1.1 copy-start.4
  185.6 1.1 copy-start.32
  187.6 6.6 %copy-start.24 = (bf16[512,128]{1,0:T(8,128)(2,1)S(1)}, bf16[512,128]{1,0:T(8,128)(2,1)}, u32[]{:S(2)}) copy-start(bf16[512,128]{1,0:T(8,128)(2,1)} %out_map.9) | copy-start | bytes 393220
  189.5 22.4 %all-to-all-start.6 = ((bf16[64,8,512]{2,1,0:T(8,128)(2,1)}), bf16[64,8,512]{2,1,0:T(8,128)(2,1)S(1)}, u32[]{:S(2)}, u32[]{:S(2)}) async-start(bf16[64,8,512]{2,1,0:T(8,128)(2,1)} %bitcast.19), calls=%async_computation.6 | async-start | bytes 1048576 | tf_op jit(solution)/shard_map/all_to_all | solution.py:339
  194.3 1.1 copy-start.8
  196.3 1.0 copy-start.43
  197.3 1.4 copy-start.64
  198.7 13.3 %copy-start.9 = (f32[512,384]{1,0:T(8,128)S(1)}, f32[512,384]{1,0:T(8,128)}, u32[]{:S(2)}) copy-start(f32[512,384]{1,0:T(8,128)} %copy-done.5) | copy-start | bytes 2359300
  212.0 1.1 copy-start.28
  (25 other events, 20.8 us)

commit v2 on v1

v2 whole, which is shorter than its diff:
```python
import jax
import jax.numpy as jnp
from jax import lax
from jax.experimental import pallas as pl
from jax.experimental.pallas import tpu as pltpu
from jax.sharding import PartitionSpec as P

TOK = 512
UNIT = 8
UNITS = 64
HEADS = 6
WIDTH = 384
STATE = 128
SPAN = 256
FEATURES = 3072
CUT = 96
LANES = 128
EPSILON = 1e-05
F32 = jnp.float32
BF16 = jnp.bfloat16


def dot(a, b, ca=1, cb=0, precision=None):
    return lax.dot_general(
        a, b, (((ca,), (cb,)), ((), ())), precision=precision, preferred_element_type=F32
    )


def iota(shape, dim):
    return lax.broadcasted_iota(jnp.int32, shape, dim)


def indicator(mask, dtype=BF16):
    return jnp.where(mask, 1.0, 0.0).astype(dtype)


def partner_row(route, unit):
    return pl.ds(pl.multiple_of((route[0, unit] >> 6) * UNIT, UNIT), UNIT)


BAND = 128
ALL = slice(0, TOK)
BANDS = [slice(BAND * k, BAND * (k + 1)) for k in range(TOK // BAND)]


def put_band(stage, route, rows, values, first=0):
    for unit in range(rows.start // UNIT, rows.stop // UNIT):
        target, place = partner_row(route, unit), UNIT * unit - rows.start
        for plane in range(values.shape[1] // LANES):
            cols = slice(LANES * plane, LANES * (plane + 1))
            stage[first + plane, target, :] = values[place : place + UNIT, cols]


def sent(stage, planes, rows=slice(0, TOK)):
    return jnp.concatenate([stage[plane, rows, :] for plane in range(planes)], axis=1)


def fill(stage, values):
    for plane in range(values.shape[1] // LANES):
        stage[plane] = values[:, LANES * plane : LANES * (plane + 1)].astype(F32)


def own_band(stage, route, rows, planes):
    units = []
    for unit in range(rows.start // UNIT, rows.stop // UNIT):
        source = partner_row(route, unit)
        parts = [stage[plane, source, :] for plane in range(planes)]
        units.append(jnp.concatenate(parts, axis=1))
    return jnp.concatenate(units, axis=0)


def receive_matrix(index_ref):
    partner = jnp.broadcast_to((index_ref[...] >> 6).astype(F32), (16, UNITS)).astype(BF16)
    repeat = indicator((iota((TOK, UNITS), 0) >> 3) == iota((TOK, UNITS), 1))
    partner = dot(repeat, partner, 1, 1)[:, 0:1].astype(jnp.int32)
    source = partner * UNIT + (iota((TOK, 1), 0) & 7)
    return indicator(iota((TOK, TOK), 1) == source)


def padded_decay(decay_ref):
    decay = decay_ref[...].astype(F32)
    return jnp.concatenate([decay, jnp.zeros((16 - HEADS, TOK), F32)], axis=0).astype(BF16)


def lower_ones():
    return indicator(iota((TOK, TOK), 1) <= iota((TOK, TOK), 0))


def running_of(decay_ref):
    return running_wide(padded_decay(decay_ref), lower_ones())


def running_wide(decay, lower):
    spread = indicator((iota((16, WIDTH), 1) >> 6) == iota((16, WIDTH), 0))
    return dot(lower, dot(decay, spread, 0, 0).astype(BF16))


def rolled(tile, shift):
    return pltpu.roll(tile, shift % LANES, 1)


def cut_state(state):
    low, middle, high = [state[:, LANES * k : LANES * (k + 1)] for k in range(3)]
    lane = iota((STATE, LANES), 1)
    parts = [
        low,
        jnp.where(lane < 32, rolled(low, 32), rolled(middle, 32)),
        jnp.where(lane < 64, rolled(middle, 64), rolled(high, 64)),
        rolled(high, 96),
    ]
    return jnp.concatenate([jnp.where(lane < CUT, part, 0.0) for part in parts], axis=0)


def join_state(slices):
    slices = slices.astype(F32)
    first, second, third, fourth = [slices[STATE * k : STATE * (k + 1)] for k in range(4)]
    lane = iota((STATE, LANES), 1)
    tiles = [
        jnp.where(lane < 96, first, rolled(second, 96)),
        jnp.where(lane < 64, rolled(second, 96), rolled(third, 64)),
        jnp.where(lane < 32, rolled(third, 64), rolled(fourth, 32)),
    ]
    return jnp.concatenate(tiles, axis=1).astype(BF16)


def local_state(keys, values, weight):
    return dot(keys, (values.astype(F32) * weight).astype(BF16), 0, 0)


def three_parts(value):
    high = value.astype(BF16).astype(F32)
    middle = (value - high).astype(BF16).astype(F32)
    return high, middle, value - high - middle


def slice_heads():
    part = lax.axis_index("seq") >> 4
    first = part + (part >> 1)
    return first, first + 1, 64 - 32 * (part & 1)


def link_decays(slices, lane, work):
    column = iota((TOK, LANES), 1)
    held = jnp.where((column >= lane) & (column < lane + 3), slices.astype(F32), 0.0)
    work[0] = jnp.broadcast_to(jnp.sum(held, axis=1, keepdims=True), (TOK, LANES))
    first, second, border = slice_heads()
    wanted = jnp.where(iota((UNITS, LANES), 1) < border, first, second)
    total = jnp.zeros((UNITS, LANES), F32)
    for head in range(HEADS):
        total = jnp.where(wanted == head, work[0, pl.ds(head, UNITS, stride=UNIT), :], total)
    return jnp.exp(total)


def carry(decays, slices, causal):
    slices = jnp.where(iota((TOK, LANES), 1) < CUT, slices.astype(F32), 0.0)
    state = jnp.zeros((UNIT, LANES), F32)
    entering = [state] * UNITS
    for device in range(UNITS) if causal else reversed(range(UNITS)):
        entering[device] = state
        own = slices[UNIT * device : UNIT * (device + 1)]
        state = state * decays[device : device + 1, :] + own
    return jnp.concatenate(entering, axis=0)


def span_rows(index):
    return slice(SPAN * index, SPAN * (index + 1))


def build_inner(rows_ref, cols_ref, decay, lower, inner_ref):
    down = dot(lower, decay, 1, 1)
    across = dot(decay, lower, 1, 1)
    allowed = iota((SPAN, SPAN), 1) <= iota((SPAN, SPAN), 0)
    for index in range(TOK // SPAN):
        span = span_rows(index)
        scores = jnp.where(allowed, dot(rows_ref[span, :], cols_ref[span, :], 1, 1), 0.0)
        for head in range(HEADS):
            spread = down[span, head : head + 1] - across[head : head + 1, span]
            weight = scores * jnp.exp(jnp.minimum(spread, 0.0))
            inner_ref[index, head] = weight.astype(BF16)


def apply_inner(inner_ref, values_ref, keys_ref, queries_ref, running, causal, out_ref):
    lane = iota((SPAN, LANES), 1)
    border = running[SPAN - 1 : SPAN]
    source, target = (0, 1) if causal else (1, 0)
    sign = 1.0 if causal else -1.0
    near = jnp.exp(sign * (border - running[span_rows(source)]))
    state = local_state(keys_ref[span_rows(source), :], values_ref[span_rows(source), :], near)
    far = jnp.exp(sign * (running[span_rows(target)] - border))
    crossing = far * dot(queries_ref[span_rows(target), :], state.astype(BF16))
    side = 1 if causal else 0
    for index in range(TOK // SPAN):
        span = span_rows(index)
        for pair in range(HEADS // 2):
            cols = slice(LANES * pair, LANES * (pair + 1))
            block = values_ref[span, cols]
            nothing = jnp.zeros_like(block)
            total = dot(inner_ref[index, 2 * pair], jnp.where(lane < 64, block, nothing), side, 0)
            total += dot(
                inner_ref[index, 2 * pair + 1], jnp.where(lane < 64, nothing, block), side, 0
            )
            if index == target:
                total += crossing[:, cols]
            out_ref[span, cols] = total


def open_raster(x, in_map, out_map, decay_f, decay_r, grad, route, pay, stage):
    lane = iota((UNIT, LANES), 1)
    note = jnp.zeros((UNIT, LANES), F32)
    for place, decay_ref in ((CUT, decay_f), (CUT + 3, decay_r)):
        decay = jnp.concatenate([decay_ref[...].astype(F32), jnp.zeros((2, TOK), F32)], axis=0)
        for offset, part in enumerate(three_parts(jnp.sum(decay, axis=1, keepdims=True))):
            note = jnp.where(lane == place + offset, part, note)
    note = jnp.broadcast_to(note[None], (UNITS, UNIT, LANES)).reshape(TOK, LANES)
    running = running_of(decay_f)
    start = 0
    for source in (in_map, out_map, x, grad):
        put_band(stage, route, ALL, source[...].astype(F32))
        stop = start + source.held.shape[1]
        pay[:, start:stop] = sent(stage, (stop - start) // LANES).astype(BF16)
        if stop >= 640:
            pay.send(cols=slice(0 if stop == 640 else start, stop))
        start = stop
    state = local_state(in_map[...], x[...], jnp.exp(running[TOK - 1 : TOK] - running))
    pay[:, 1024:1152] = (cut_state(state) + note).astype(BF16)
    pay.send(cols=slice(1024, 1152))


def inner_raster(x, in_map, out_map, decay_f, inner, local):
    lower = lower_ones()
    decay = padded_decay(decay_f)
    build_inner(out_map, in_map, decay, lower, inner)
    apply_inner(inner, x, in_map, out_map, running_wide(decay, lower), True, local)


def open_scan(got, decay_r, route, x, in_map, pay, stage):
    slices = got[:, 1024:1152]
    running = running_of(decay_r)
    pay[:, 0:128] = carry(link_decays(slices, CUT, stage), slices, True).astype(BF16)
    pay.send(cols=slice(0, 128))
    fill(stage, jnp.concatenate([got[:, 256:640], got[:, 0:128]], axis=1))
    for rows in BANDS:
        moved = own_band(stage, route, rows, 4).astype(BF16)
        x[rows, :] = moved[:, 0:384]
        in_map[rows, :] = moved[:, 384:512]
    x.send()
    in_map.send()
    state = local_state(in_map[...], x[...], jnp.exp(running))
    pay[:, 128:256] = cut_state(state).astype(BF16)
    pay.send(cols=slice(128, 256))


def inner_scan(
    got, x, in_map, decay_r, route, out_map, grad, inner, local, links_f, links_r, work
):
    take = receive_matrix(route)
    out_map[...] = dot(take, got[:, 128:256]).astype(BF16)
    grad[...] = dot(take, got[:, 640:1024]).astype(BF16)
    lower = lower_ones()
    decay = padded_decay(decay_r)
    build_inner(in_map, out_map, decay, lower, inner)
    apply_inner(inner, x, in_map, out_map, running_wide(decay, lower), False, local)
    slices = got[:, 1024:1152]
    for links, lane in ((links_f, CUT), (links_r, CUT + 3)):
        links[...] = link_decays(slices, lane, work)


def finish_raster(got, out_map, local, decay_f, links, route, y, pay, stage):
    running = running_of(decay_f)
    entering = join_state(got[:, 0:128])
    pay[:, 384:512] = carry(links, got[:, 128:256], False).astype(BF16)
    pay.send(cols=slice(384, 512))
    for rows in BANDS:
        value = local[rows, :] + jnp.exp(running[rows]) * dot(out_map[rows, :], entering)
        y[rows, :] = value.astype(BF16)
        put_band(stage, route, rows, value)
    y.send()
    pay[:, 0:384] = sent(stage, 3).astype(BF16)
    pay.send(cols=slice(0, 384))


def finish_scan(
    got, out_map, local, decay_r, x, grad, skip, gain, route, y, combined, stats, stage
):
    entering = join_state(got[:, 384:512])
    running = running_of(decay_r)
    weight = jnp.exp(running[TOK - 1 : TOK, :] - running)
    fill(stage, got[:, 0:384])
    y_forward = own_band(stage, route, ALL, 3)
    y[...] = (local[...] + weight * dot(out_map[...], entering)).astype(BF16)
    y.send()
    total = y_forward + y[...].astype(F32) + skip[...] * x[...].astype(F32)
    combined[...] = total
    combined.send()
    scaled = gain[...] * grad[...].astype(F32)
    squares, inner = token_sums(total * total), token_sums(total * scaled)
    row = iota((UNIT, LANES), 0)
    tile = jnp.zeros((UNIT, LANES), F32)
    for place, sums in ((0, squares), (4, inner)):
        for k in range(4):
            tile = jnp.where(row == place + k, sums[:, LANES * k : LANES * (k + 1)], tile)
    for place in range(8):
        stats[UNIT * place : UNIT * (place + 1), :] = tile


def token_sums(value):
    folded = value[:, 0:128] + value[:, 128:256] + value[:, 256:384]
    ones = jnp.ones((16, LANES), BF16)
    return sum(dot(ones, part.astype(BF16), 1, 1)[0:1] for part in three_parts(folded)[:2])


def gradient(combined, scaled, scale, pull):
    return (scale * scaled - combined * pull).astype(BF16)


def open_back(stats, combined, y, out_map, grad, gain, decay_r, route, back, pay, stage):
    running = running_of(decay_r)
    tile = jnp.sum(stats[...].reshape(8, 8, LANES), axis=0)
    squares = jnp.concatenate([tile[k : k + 1] for k in range(4)], axis=1)
    inner = jnp.concatenate([tile[k : k + 1] for k in range(4, 8)], axis=1)
    scale = lax.rsqrt(squares / FEATURES + EPSILON)
    pull = scale * scale * scale * inner / FEATURES
    parts = [*three_parts(scale), *three_parts(pull), jnp.zeros((10, TOK), F32)]
    parts = jnp.concatenate(parts, axis=0).astype(BF16)
    row, col = iota((16, 2 * WIDTH), 0), iota((16, 2 * WIDTH), 1)
    both = indicator(((row < 3) & (col < WIDTH)) | ((row >= 3) & (row < 6) & (col >= WIDTH)))
    lanes = indicator(iota((16, LANES), 1) == CUT + iota((16, LANES), 0))
    wide = dot(parts, both, 0, 0)
    put_band(stage, route, ALL, dot(parts, lanes, 0, 0), 3)
    put_band(stage, route, ALL, y[...].astype(F32))
    pay[:, 0:384] = sent(stage, 3).astype(BF16)
    pay.send(cols=slice(0, 384))
    scaled = gain[...] * grad[...].astype(F32)
    back[...] = gradient(combined[...], scaled, wide[:, 0:WIDTH], wide[:, WIDTH:])
    back.send()
    state = local_state(out_map[...], back[...], jnp.exp(running[TOK - 1 : TOK] - running))
    pay[:, 384:512] = (cut_state(state) + stage[3]).astype(BF16)
    pay.send(cols=slice(384, 512))


def inner_back_scan(inner, back, in_map, out_map, decay_r, local):
    apply_inner(inner, back, out_map, in_map, running_of(decay_r), True, local)


def middle_raster(
    got, y_forward, x, out_map, grad, skip, gain, decay_f, links, route, normed, back, pay, stage
):
    running = running_of(decay_f)
    fill(stage, got[...])
    row, col = iota((LANES, 2 * WIDTH), 0) - CUT, iota((LANES, 2 * WIDTH), 1)
    both = indicator(
        ((row >= 0) & (row < 3) & (col < WIDTH)) | ((row >= 3) & (row < 6) & (col >= WIDTH))
    )
    pay[:, 0:128] = carry(links, got[:, 384:512], True).astype(BF16)
    pay.send(cols=slice(0, 128))
    for rows in BANDS:
        moved = own_band(stage, route, rows, 4)
        wide = dot(moved[:, 384:512].astype(BF16), both)
        scale = wide[:, 0:WIDTH]
        total = y_forward[rows, :].astype(F32) + moved[:, 0:384]
        total += skip[...] * x[rows, :].astype(F32)
        normed[rows, :] = (total * scale * gain[...]).astype(BF16)
        scaled = gain[...] * grad[rows, :].astype(F32)
        back[rows, :] = gradient(total, scaled, scale, wide[:, WIDTH:])
    normed.send()
    back.send()
    state = local_state(out_map[...], back[...], jnp.exp(running))
    pay[:, 128:256] = cut_state(state).astype(BF16)
    pay.send(cols=slice(128, 256))


def inner_back_raster(inner, back, in_map, out_map, decay_f, skip, local):
    apply_inner(inner, back, out_map, in_map, running_of(decay_f), False, local)
    local[...] += skip[...] * back[...].astype(F32)


def finish_back_scan(got, in_map, local, decay_r, links, route, pay, stage):
    running = running_of(decay_r)
    entering = join_state(got[:, 0:128])
    pay[:, 384:512] = carry(links, got[:, 128:256], False).astype(BF16)
    pay.send(cols=slice(384, 512))
    for rows in BANDS:
        value = local[rows, :] + jnp.exp(running[rows]) * dot(in_map[rows, :], entering)
        put_band(stage, route, rows, value)
    pay[:, 0:384] = sent(stage, 3).astype(BF16)
    pay.send(cols=slice(0, 384))


def finish_back_raster(got, in_map, local, decay_f, route, out, stage):
    entering = join_state(got[:, 384:512])
    running = running_of(decay_f)
    last = running[TOK - 1 : TOK, :]
    fill(stage, got[:, 0:384])
    for rows in BANDS:
        carried = jnp.exp(last - running[rows]) * dot(in_map[rows, :], entering)
        total = local[rows, :] + carried + own_band(stage, route, rows, 3)
        out[rows, :] = total.astype(BF16)
        out.send(rows)


class Arriving:
    def __init__(self, source, held, semaphore):
        self.held = held
        self.copy = pltpu.make_async_copy(source, held, semaphore)
        self.copy.start()

    def land(self):
        if self.copy is not None:
            self.copy.wait()
            self.copy = None

    def __getitem__(self, index):
        self.land()
        return self.held[index]


class Leaving:
    def __init__(self, held, target, semaphores):
        self.held, self.target, self.semaphores, self.copies = held, target, semaphores, []

    def __setitem__(self, index, value):
        self.held[index] = value

    def __getitem__(self, index):
        return self.held[index]

    def send(self, rows=None, cols=None):
        held, target = self.held, self.target
        if rows is not None or cols is not None:
            index = (rows or slice(0, TOK), cols or slice(0, held.shape[1]))
            held, target = held.at[index], target.at[index]
        copy = pltpu.make_async_copy(held, target, self.semaphores.at[len(self.copies)])
        copy.start()
        self.copies.append(copy)

    def finish(self):
        if not self.copies:
            self.send()
        for copy in self.copies:
            copy.wait()


def whole_kernel(body, outs, *operands, flops, work=False):
    shapes = [jax.ShapeDtypeStruct(shape, dtype) for shape, dtype in outs]
    size = sum(a.size * a.dtype.itemsize for a in (*operands, *shapes))
    return pl.pallas_call(
        body,
        out_shape=shapes,
        scratch_shapes=[pltpu.VMEM((1, TOK, LANES), F32)] * work,
        compiler_params=pltpu.CompilerParams(vmem_limit_bytes=60 * 2**20),
        cost_estimate=pl.CostEstimate(flops=flops, bytes_accessed=size, transcendentals=0),
        name=body.__name__,
    )(*operands)


def kernel(body, outs, *operands, arrived=0, stage=0, flops=400_000_000):
    shapes = [jax.ShapeDtypeStruct(*out[:2]) for out in outs]
    size = sum(a.size * a.dtype.itemsize for a in (*operands, *shapes))
    count = len(operands)
    own = [
        place >= arrived and (not arrived or a.dtype == jnp.int32 or a.size > 5_000)
        for place, a in enumerate(operands)
    ]

    def wrapped(*refs):
        sources, targets = refs[:count], refs[count : count + len(outs)]
        scratch = iter(refs[count + len(outs) :])
        held = [(next(scratch), next(scratch)) if mine else None for mine in own]
        given = list(sources)
        for place in sorted(range(count), key=lambda k: operands[k].size):
            if own[place]:
                given[place] = Arriving(sources[place], *held[place])
        results = [Leaving(next(scratch), target, next(scratch)) for target in targets]
        body(*given, *results, *([next(scratch)] if stage else []))
        for operand in given:
            if isinstance(operand, Arriving):
                operand.land()
        for result in results:
            result.finish()

    scratch_shapes = []
    for operand, mine in zip(operands, own, strict=True):
        if mine:
            space = pltpu.SMEM if operand.dtype == jnp.int32 else pltpu.VMEM
            scratch_shapes += [space(operand.shape, operand.dtype), pltpu.SemaphoreType.DMA]
    for shape, dtype, *sends in outs:
        scratch_shapes += [pltpu.VMEM(shape, dtype), pltpu.SemaphoreType.DMA((*sends, 1)[:1])]
    if stage:
        scratch_shapes.append(pltpu.VMEM((stage // LANES, TOK, LANES), F32))
    whole = pl.BlockSpec(memory_space=pltpu.VMEM)
    apart = pl.BlockSpec(memory_space=pl.ANY)
    operands = [
        pltpu.with_memory_space_constraint(a, pltpu.HBM) if mine else a
        for a, mine in zip(operands, own, strict=True)
    ]
    return pl.pallas_call(
        wrapped,
        out_shape=[pltpu.HBM(*out[:2]) for out in outs],
        in_specs=[apart if mine else whole for mine in own],
        out_specs=[apart] * len(outs),
        scratch_shapes=scratch_shapes,
        compiler_params=pltpu.CompilerParams(vmem_limit_bytes=48 * 2**20),
        cost_estimate=pl.CostEstimate(flops=flops, bytes_accessed=size, transcendentals=0),
        name=body.__name__,
    )(*operands)


def exchange(pay):
    return lax.all_to_all(pay, "seq", split_axis=0, concat_axis=0, tiled=True)


def shards(
    ssm_input,
    input_map,
    output_map,
    decay_forward,
    decay_reverse,
    skip_gain,
    norm_gain,
    scan_order,
    raster_order,
    grad_normed,
):
    to_scan = raster_order.reshape(1, UNITS)
    to_raster = scan_order.reshape(1, UNITS)
    skip = jnp.repeat(skip_gain, WIDTH // HEADS).reshape(1, WIDTH)
    gain = norm_gain.reshape(1, WIDTH)
    wide16, wide32 = ((TOK, WIDTH), BF16), ((TOK, WIDTH), F32)
    rows16 = ((TOK, STATE), BF16)
    inner16 = ((TOK // SPAN, HEADS, SPAN, SPAN), BF16)

    def pay(lanes, sends=2):
        return ((TOK, lanes), BF16, sends)

    (pay1,) = kernel(
        open_raster, [pay(1152, 3)],
        ssm_input, input_map, output_map, decay_forward, decay_reverse, grad_normed, to_scan,
        stage=384,
    )
    got1 = exchange(pay1)
    inner_f, local_f = whole_kernel(
        inner_raster, [inner16, wide32],
        ssm_input, input_map, output_map, decay_forward, flops=8_000_000_000,
    )
    x_scan, in_scan, pay2 = kernel(
        open_scan, [wide16, rows16, pay(256)],
        got1, decay_reverse, to_raster, arrived=1, stage=512,
    )
    got2 = exchange(pay2)
    links32 = ((UNITS, LANES), F32)
    out_scan, grad_scan, inner_r, local_r, links_f, links_r = whole_kernel(
        inner_scan, [rows16, wide16, inner16, wide32, links32, links32],
        got1, x_scan, in_scan, decay_reverse, to_raster, flops=8_000_000_000, work=True,
    )
    y_forward, pay3 = kernel(
        finish_raster, [wide16, pay(512)],
        got2, output_map, local_f, decay_forward, links_r, to_scan, arrived=1, stage=384,
    )
    got3 = exchange(pay3)
    y_scan, combined, stats = kernel(
        finish_scan, [wide16, wide32, ((64, LANES), F32)],
        got3, out_scan, local_r, decay_reverse, x_scan, grad_scan, skip, gain, to_raster, arrived=1, stage=384,
    )
    all_stats = lax.all_to_all(stats, "head", split_axis=0, concat_axis=0, tiled=True)
    back_scan, pay4 = kernel(
        open_back, [wide16, pay(512)],
        all_stats, combined, y_scan, out_scan, grad_scan, gain, decay_reverse, to_raster, arrived=1, stage=512,
    )
    got4 = exchange(pay4)
    (local_br,) = whole_kernel(
        inner_back_scan, [wide32], inner_r, back_scan, in_scan, out_scan, decay_reverse,
        flops=4_000_000_000,
    )
    normed, back, pay5 = kernel(
        middle_raster, [wide16, wide16, pay(256)],
        got4, y_forward, ssm_input, output_map, grad_normed, skip, gain, decay_forward, links_r,
        to_scan, arrived=1, stage=512,
    )
    got5 = exchange(pay5)
    (local_bf,) = whole_kernel(
        inner_back_raster, [wide32], inner_f, back, input_map, output_map, decay_forward, skip,
        flops=4_000_000_000,
    )
    (pay6,) = kernel(
        finish_back_scan, [pay(512)],
        got5, in_scan, local_br, decay_reverse, links_f, to_raster, arrived=1, stage=384,
    )
    got6 = exchange(pay6)
    (grad_input,) = kernel(
        finish_back_raster, [(*wide16, 4)],
        got6, input_map, local_bf, decay_forward, to_scan, arrived=1, stage=384,
    )
    return normed, grad_input


def solution(mesh):
    return jax.shard_map(
        shards,
        mesh=mesh,
        in_specs=(
            P("seq", "head"),
            P("seq", "head"),
            P("seq", "head"),
            P("head", "seq"),
            P("head", "seq"),
            P("head"),
            P("head"),
            P("seq"),
            P("seq"),
            P("seq", "head"),
        ),
        out_specs=(P("seq", "head"), P("seq", "head")),
        check_vma=False,
    )
```

time: 217 us -> 191 us (0.88)
  local copies, waits for them, and re-layouts: 46.3 us -> 0.2 us
  waiting for transfers between devices: 61.1 us -> 75.6 us
  Pallas kernels: 27.1 us -> 38.1 us
  starting transfers between devices: 37.9 us -> 33.4 us
    unnamed x136 -> x18, local copies, waits for them, and re-layouts: 45.5 us -> 0.05 us
    all_to_all x5, waiting for transfers between devices: 61.1 us -> 75.6 us  [exchange(): return lax.all_to_all(pay, 'seq', split_axis=0, concat_axis=0, tiled=True)]
    pallas_call x12, Pallas kernels: 27.1 us -> 38.1 us  [the longest x8 21.6 us: kernel(): pl.pallas_call(wrapped, out_shape=[pltpu.HBM(*out[:2]) for out in outs],...]
    all_to_all x5, starting transfers between devices: 37.9 us -> 33.4 us  [exchange(): return lax.all_to_all(pay, 'seq', split_axis=0, concat_axis=0, tiled=True)]
  transfers between devices with their start and end apart: 5 -> 5, of which waited for: 5 -> 5; matrix products, arithmetic and copies ran while one was open for 0% -> 0% of each run, Pallas kernels for 4% -> 9%
where the time goes in v2:
time: 191 us; the launch traced here: 190 us
  waiting for transfers between devices  75.6 us (40%)
  blocking collectives  41.8 us (22%)
  Pallas kernels  38.1 us (20%)
  starting transfers between devices  33.4 us (17%)
    all_to_all x5, waiting for transfers between devices, exchange(): return lax.all_to_all(pay, 'seq', split_axis=0, concat_axis=0, tiled=True)  75.6 us
    all_to_all x5, starting transfers between devices, exchange(): return lax.all_to_all(pay, 'seq', split_axis=0, concat_axis=0, tiled=True)  33.4 us
    all_to_all x1, blocking collectives, exchange(): return lax.all_to_all(pay, 'seq', split_axis=0, concat_axis=0, tiled=True)  24.8 us
    pallas_call x8, Pallas kernels, kernel(): pl.pallas_call(wrapped, out_shape=[pltpu.HBM(*out[:2]) for out in outs],...  21.6 us
    all_to_all x1, blocking collectives, shards(): lax.all_to_all(stats, 'head', split_axis=0, concat_axis=0, tiled=True)  17 us
    pallas_call x4, Pallas kernels, whole_kernel(): pl.pallas_call(body, out_shape=shapes, scratch_shapes=[pltpu.VMEM((1, TOK...  16.5 us
  transfers between devices with their start and end apart: 5, of which 5 were waited for; matrix products, arithmetic and copies ran while one was open for 0% of the time, Pallas kernels for 9%

profile of v2, /device:TPU:1, one launch (start us, length us, event | category | flops | bytes accessed | tf_op | source)
XLA Modules:
  0.0 190.1 jit_solution(16824026650992631809)
XLA Ops:
  0.6 3.0 %open_raster.1 = bf16[512,1152]{1,0:T(8,128)(2,1)} custom-call(bf16[512,384]{1,0:T(8,128)(2,1)} %refs_2_.3, bf16[512,128]{1,0:T(8,128)(2,1)} %refs_1_.7, bf16[512,128]{1,0:T(8,128)(2,1)} %out_map.3, bf16[6,512]{1,0:T(8,128)(2,1)} %refs_3_.11, bf16[6,512]{1,0:T(8,128)(2,1)} %refs_3_.10, bf16[512,384]{1,0:T(8,128)(2,1)} %refs_4_.3, s32[1,64]{1,0:T(1,128)} %bitcast.36), custom_call_target="tpu_custom_call" | custom-call | flops 400000000 | bytes 2240768 | tf_op jit(solution)/shard_map/open_raster/pallas_call | solution.py:496
  3.6 11.6 %all-to-all-start = ((bf16[64,8,1152]{2,1,0:T(8,128)(2,1)}), bf16[64,8,1152]{2,1,0:T(8,128)(2,1)S(1)}, u32[]{:S(2)}, u32[]{:S(2)}) async-start(bf16[64,8,1152]{2,1,0:T(8,128)(2,1)} %bitcast.24), calls=%async_computation | async-start | bytes 2359296 | tf_op jit(solution)/shard_map/all_to_all | solution.py:509
  15.2 0.0 copy-start.1
  15.3 3.8 %inner_raster.1 = (bf16[2,6,256,256]{3,2,1,0:T(8,128)(2,1)}, f32[512,384]{1,0:T(8,128)}) custom-call(bf16[512,384]{1,0:T(8,128)(2,1)} %refs_2_.3, bf16[512,128]{1,0:T(8,128)(2,1)} %refs_1_.7, bf16[512,128]{1,0:T(8,128)(2,1)} %out_map.3, bf16[6,512]{1,0:T(8,128)(2,1)} %refs_3_.11), custom_call_target="tpu_custom_call" | custom-call | flops 8000000000 | bytes 3020800 | tf_op jit(solution)/shard_map/inner_raster/pallas_call | solution.py:446
  19.0 26.8 %all-to-all-done = bf16[64,8,1152]{2,1,0:T(8,128)(2,1)S(1)} async-done(((bf16[64,8,1152]{2,1,0:T(8,128)(2,1)}), bf16[64,8,1152]{2,1,0:T(8,128)(2,1)S(1)}, u32[]{:S(2)}, u32[]{:S(2)}) %all-to-all-start) | async-done | bytes 1179680 | tf_op jit(solution)/shard_map/all_to_all | solution.py:509
  45.8 0.0 copy-start
  45.8 0.0 copy-done.1
  45.8 2.2 %open_scan.1 = (bf16[512,384]{1,0:T(8,128)(2,1)}, bf16[512,128]{1,0:T(8,128)(2,1)}, bf16[512,256]{1,0:T(8,128)(2,1)}) custom-call(bf16[512,1152]{1,0:T(8,128)(2,1)S(1)} %bitcast.19, bf16[6,512]{1,0:T(8,128)(2,1)S(1)} %copy-done.1, s32[1,64]{1,0:T(1,128)} %bitcast.31), custom_call_target="tpu_custom_call" | custom-call | flops 400000000 | bytes 1972480 | tf_op jit(solution)/shard_map/open_scan/pallas_call | solution.py:496
  48.0 6.6 %all-to-all-start.1 = ((bf16[64,8,256]{2,1,0:T(8,128)(2,1)}), bf16[64,8,256]{2,1,0:T(8,128)(2,1)S(1)}, u32[]{:S(2)}, u32[]{:S(2)}) async-start(bf16[64,8,256]{2,1,0:T(8,128)(2,1)} %bitcast.29), calls=%async_computation.1 | async-start | bytes 524288 | tf_op jit(solution)/shard_map/all_to_all | solution.py:509
  54.7 0.0 copy-done
  54.7 0.0 copy-start.4
  54.7 4.8 %inner_scan.1 = (bf16[512,128]{1,0:T(8,128)(2,1)}, bf16[512,384]{1,0:T(8,128)(2,1)}, bf16[2,6,256,256]{3,2,1,0:T(8,128)(2,1)}, f32[512,384]{1,0:T(8,128)}, f32[64,128]{1,0:T(8,128)}, /*index=5*/f32[64,128]{1,0:T(8,128)}) custom-call(bf16[512,1152]{1,0:T(8,128)(2,1)} %bitcast.20, bf16[512,384]{1,0:T(8,128)(2,1)} %get-tuple-element.25.x.refs_4_, ...), custom_call_target="tpu_custom_call" | custom-call | flops 8000000000 | bytes 4659456 | tf_op jit(solution)/shard_map/inner_scan/pallas_call | solution.py:446
  59.6 0.0 copy-start.7
  59.6 0.0 copy-start.8
  59.6 0.0 copy-start.2
  59.6 8.3 %all-to-all-done.1 = bf16[64,8,256]{2,1,0:T(8,128)(2,1)S(1)} async-done(((bf16[64,8,256]{2,1,0:T(8,128)(2,1)}), bf16[64,8,256]{2,1,0:T(8,128)(2,1)S(1)}, u32[]{:S(2)}, u32[]{:S(2)}) %all-to-all-start.1) | async-done | bytes 262176 | tf_op jit(solution)/shard_map/all_to_all | solution.py:509
  67.8 0.0 copy-done.4
  67.8 2.7 %finish_raster.1 = (bf16[512,384]{1,0:T(8,128)(2,1)}, bf16[512,512]{1,0:T(8,128)(2,1)}) custom-call(bf16[512,256]{1,0:T(8,128)(2,1)S(1)} %bitcast.22, bf16[512,128]{1,0:T(8,128)(2,1)} %out_map.3, f32[512,384]{1,0:T(8,128)} %get-tuple-element.24.refs_2_, bf16[6,512]{1,0:T(8,128)(2,1)S(1)} %copy-done.4, f32[64,128]{1,0:T(8,128)} %get-tuple-element.27.refs_4_.refs_8_, ...), custom_call_target="tpu_custom_call" | custom-call | flops 400000000 | bytes 2136320 | tf_op jit(solution)/shard_map/finish_raster/pallas_call | solution.py:496
  70.5 4.7 %all-to-all-start.2 = ((bf16[64,8,512]{2,1,0:T(8,128)(2,1)}), bf16[64,8,512]{2,1,0:T(8,128)(2,1)S(1)}, u32[]{:S(2)}, u32[]{:S(2)}) async-start(bf16[64,8,512]{2,1,0:T(8,128)(2,1)} %bitcast.26), calls=%async_computation.2 | async-start | bytes 1048576 | tf_op jit(solution)/shard_map/all_to_all | solution.py:509
  75.2 0.0 copy-done.7
  75.3 0.0 copy-done.8
  75.3 0.1 broadcast_in_dim.3
  75.3 0.1 reshape_reshape.3.refs_6_.refs_5_.skip
  75.4 0.0 copy-start.6
  75.4 17.5 %all-to-all-done.2 = bf16[64,8,512]{2,1,0:T(8,128)(2,1)S(1)} async-done(((bf16[64,8,512]{2,1,0:T(8,128)(2,1)}), bf16[64,8,512]{2,1,0:T(8,128)(2,1)S(1)}, u32[]{:S(2)}, u32[]{:S(2)}) %all-to-all-start.2) | async-done | bytes 524320 | tf_op jit(solution)/shard_map/all_to_all | solution.py:509
  93.0 0.0 copy-done.2
  93.0 3.3 %finish_scan.1 = (bf16[512,384]{1,0:T(8,128)(2,1)}, f32[512,384]{1,0:T(8,128)}, f32[64,128]{1,0:T(8,128)}) custom-call(bf16[512,512]{1,0:T(8,128)(2,1)S(1)} %bitcast.17, bf16[512,128]{1,0:T(8,128)(2,1)} %get-tuple-element.29.refs_1_.refs_3_.out_map, f32[512,384]{1,0:T(8,128)} %get-tuple-element.30.refs_2_, bf16[6,512]{1,0:T(8,128)(2,1)S(1)} %copy-done.2, ...), custom_call_target="tpu_custom_call" | custom-call | flops 400000000 | bytes 3450112 | tf_op jit(solution)/shard_map/finish_scan/pallas_call | solution.py:496
  96.3 17.0 %all_to_all.77 = f32[8,8,128]{2,1,0:T(8,128)S(1)} all-to-all(f32[8,8,128]{2,1,0:T(8,128)} %bitcast.30), channel_id=1, replica_groups=mesh['seq'=64,'head'=8] {'head'}, dimensions={0} | all-to-all | bytes 65536 | tf_op jit(solution)/shard_map/all_to_all | solution.py:564
  113.3 2.8 %open_back.1 = (bf16[512,384]{1,0:T(8,128)(2,1)}, bf16[512,512]{1,0:T(8,128)(2,1)}) custom-call(f32[64,128]{1,0:T(8,128)S(1)} %bitcast.23, f32[512,384]{1,0:T(8,128)} %get-tuple-element.33.refs_1_, bf16[512,384]{1,0:T(8,128)(2,1)} %get-tuple-element.34.refs_2_, bf16[512,128]{1,0:T(8,128)(2,1)} %get-tuple-element.29.refs_1_.refs_3_.out_map, ...), custom_call_target="tpu_custom_call" | custom-call | flops 400000000 | bytes 2662144 | tf_op jit(solution)/shard_map/open_back/pallas_call | solution.py:496
  116.1 24.8 %all_to_all.78 = bf16[64,8,512]{2,1,0:T(8,128)(2,1)S(1)} all-to-all(bf16[64,8,512]{2,1,0:T(8,128)(2,1)} %bitcast.27), channel_id=1, replica_groups=mesh['seq'=64,'head'=8] {'seq'}, dimensions={0} | all-to-all | bytes 1048576 | tf_op jit(solution)/shard_map/all_to_all | solution.py:509
  140.9 0.0 copy-done.6
  140.9 2.9 %middle_raster.1 = (bf16[512,384]{1,0:T(8,128)(2,1)}, bf16[512,384]{1,0:T(8,128)(2,1)}, bf16[512,256]{1,0:T(8,128)(2,1)}) custom-call(bf16[512,512]{1,0:T(8,128)(2,1)S(1)} %bitcast.16, bf16[512,384]{1,0:T(8,128)(2,1)} %get-tuple-element.36.refs_1_, bf16[512,384]{1,0:T(8,128)(2,1)} %refs_2_.3, bf16[512,128]{1,0:T(8,128)(2,1)} %out_map.3, ...), custom_call_target="tpu_custom_call" | custom-call | flops 400000000 | bytes 2925824 | tf_op jit(solution)/shard_map/middle_raster/pallas_call | solution.py:496
  143.8 5.7 %all-to-all-start.5 = ((bf16[64,8,256]{2,1,0:T(8,128)(2,1)}), bf16[64,8,256]{2,1,0:T(8,128)(2,1)S(1)}, u32[]{:S(2)}, u32[]{:S(2)}) async-start(bf16[64,8,256]{2,1,0:T(8,128)(2,1)} %bitcast.28), calls=%async_computation.5 | async-start | bytes 524288 | tf_op jit(solution)/shard_map/all_to_all | solution.py:509
  149.5 0.0 copy-start.3
  149.5 3.9 %inner_back_scan.1.refs_2_ = f32[512,384]{1,0:T(8,128)} custom-call(bf16[2,6,256,256]{3,2,1,0:T(8,128)(2,1)} %get-tuple-element.39.inner, bf16[512,384]{1,0:T(8,128)(2,1)} %get-tuple-element.40.back, bf16[512,128]{1,0:T(8,128)(2,1)} %get-tuple-element.26.in_map.refs_1_, bf16[512,128]{1,0:T(8,128)(2,1)} %get-tuple-element.29.refs_1_.refs_3_.out_map, ...), custom_call_target="tpu_custom_call" | custom-call | flops 4000000000 | bytes 3020800 | tf_op jit(solution)/shard_map/inner_back_scan/pallas_call | solution.py:446
  153.4 9.2 %all-to-all-done.5 = bf16[64,8,256]{2,1,0:T(8,128)(2,1)S(1)} async-done(((bf16[64,8,256]{2,1,0:T(8,128)(2,1)}), bf16[64,8,256]{2,1,0:T(8,128)(2,1)S(1)}, u32[]{:S(2)}, u32[]{:S(2)}) %all-to-all-start.5) | async-done | bytes 262176 | tf_op jit(solution)/shard_map/all_to_all | solution.py:509
  162.7 0.0 copy-done.3
  162.7 2.6 %finish_back_scan.1 = bf16[512,512]{1,0:T(8,128)(2,1)} custom-call(bf16[512,256]{1,0:T(8,128)(2,1)S(1)} %bitcast.21, bf16[512,128]{1,0:T(8,128)(2,1)} %get-tuple-element.26.in_map.refs_1_, f32[512,384]{1,0:T(8,128)} %inner_back_scan.1.refs_2_, bf16[6,512]{1,0:T(8,128)(2,1)S(1)} %copy-done.3, f32[64,128]{1,0:T(8,128)} %get-tuple-element.41.refs_4_, ...), custom_call_target="tpu_custom_call" | custom-call | flops 400000000 | bytes 1743104 | tf_op jit(solution)/shard_map/finish_back_scan/pallas_call | solution.py:496
  165.2 4.7 %all-to-all-start.6 = ((bf16[64,8,512]{2,1,0:T(8,128)(2,1)}), bf16[64,8,512]{2,1,0:T(8,128)(2,1)S(1)}, u32[]{:S(2)}, u32[]{:S(2)}) async-start(bf16[64,8,512]{2,1,0:T(8,128)(2,1)} %bitcast.25), calls=%async_computation.6 | async-start | bytes 1048576 | tf_op jit(solution)/shard_map/all_to_all | solution.py:509
  170.0 0.0 copy-start.5
  170.0 4.0 %inner_back_raster.1.refs_2_ = f32[512,384]{1,0:T(8,128)} custom-call(bf16[2,6,256,256]{3,2,1,0:T(8,128)(2,1)} %get-tuple-element.42.inner, bf16[512,384]{1,0:T(8,128)(2,1)} %get-tuple-element.43.back, bf16[512,128]{1,0:T(8,128)(2,1)} %refs_1_.7, bf16[512,128]{1,0:T(8,128)(2,1)} %out_map.3, bf16[6,512]{1,0:T(8,128)(2,1)} %refs_3_.11, f32[1,384]{1,0:T(1,128)} %copy-done.6), custom_call_target="tpu_custom_call" | custom-call | flops 4000000000 | bytes 3022336 | tf_op jit(solution)/shard_map/inner_back_raster/pallas_call | solution.py:446
  174.0 13.7 %all-to-all-done.6 = bf16[64,8,512]{2,1,0:T(8,128)(2,1)S(1)} async-done(((bf16[64,8,512]{2,1,0:T(8,128)(2,1)}), bf16[64,8,512]{2,1,0:T(8,128)(2,1)S(1)}, u32[]{:S(2)}, u32[]{:S(2)}) %all-to-all-start.6) | async-done | bytes 524320 | tf_op jit(solution)/shard_map/all_to_all | solution.py:509
  187.7 0.0 copy-done.5
  187.7 2.2 %finish_back_raster.1 = bf16[512,384]{1,0:T(8,128)(2,1)} custom-call(bf16[512,512]{1,0:T(8,128)(2,1)S(1)} %bitcast.18, bf16[512,128]{1,0:T(8,128)(2,1)} %refs_1_.7, f32[512,384]{1,0:T(8,128)} %inner_back_raster.1.refs_2_, bf16[6,512]{1,0:T(8,128)(2,1)S(1)} %copy-done.5, s32[1,64]{1,0:T(1,128)} %bitcast.39), custom_call_target="tpu_custom_call" | custom-call | flops 400000000 | bytes 1841408 | tf_op jit(solution)/shard_map/finish_back_raster/pallas_call | solution.py:496
  (1 shorter events, 0.0 us)
Async XLA Ops:
  3.6 42.2 %all-to-all-start = ((bf16[64,8,1152]{2,1,0:T(8,128)(2,1)}), bf16[64,8,1152]{2,1,0:T(8,128)(2,1)S(1)}, u32[]{:S(2)}, u32[]{:S(2)}) async-start(bf16[64,8,1152]{2,1,0:T(8,128)(2,1)} %bitcast.24), calls=%async_computation | async-start | bytes 2359296 | tf_op jit(solution)/shard_map/all_to_all | solution.py:509
  15.2 30.6 %copy-start.1 = (bf16[6,512]{1,0:T(8,128)(2,1)S(1)}, bf16[6,512]{1,0:T(8,128)(2,1)}, u32[]{:S(2)}) copy-start(bf16[6,512]{1,0:T(8,128)(2,1)} %refs_3_.10) | copy-start | bytes 18436
  45.8 8.8 %copy-start = (bf16[64,8,1152]{2,1,0:T(8,128)(2,1)}, bf16[64,8,1152]{2,1,0:T(8,128)(2,1)S(1)}, u32[]{:S(2)}) copy-start(bf16[64,8,1152]{2,1,0:T(8,128)(2,1)S(1)} %all-to-all-done) | copy-start | bytes 3538948
  48.0 19.8 %all-to-all-start.1 = ((bf16[64,8,256]{2,1,0:T(8,128)(2,1)}), bf16[64,8,256]{2,1,0:T(8,128)(2,1)S(1)}, u32[]{:S(2)}, u32[]{:S(2)}) async-start(bf16[64,8,256]{2,1,0:T(8,128)(2,1)} %bitcast.29), calls=%async_computation.1 | async-start | bytes 524288 | tf_op jit(solution)/shard_map/all_to_all | solution.py:509
  54.7 13.2 %copy-start.4 = (bf16[6,512]{1,0:T(8,128)(2,1)S(1)}, bf16[6,512]{1,0:T(8,128)(2,1)}, u32[]{:S(2)}) copy-start(bf16[6,512]{1,0:T(8,128)(2,1)} %refs_3_.11) | copy-start | bytes 18436
  59.6 15.7 %copy-start.7 = (f32[384]{0:T(512)S(1)}, f32[384]{0:T(512)}, u32[]{:S(2)}) copy-start(f32[384]{0:T(512)} %param.16) | copy-start | bytes 4612
  59.6 15.7 %copy-start.8 = (f32[6]{0:T(128)S(1)}, f32[6]{0:T(128)}, u32[]{:S(2)}) copy-start(f32[6]{0:T(128)} %param.15) | copy-start | bytes 76
  59.6 33.4 %copy-start.2 = (bf16[6,512]{1,0:T(8,128)(2,1)S(1)}, bf16[6,512]{1,0:T(8,128)(2,1)}, u32[]{:S(2)}) copy-start(bf16[6,512]{1,0:T(8,128)(2,1)} %refs_3_.10) | copy-start | bytes 18436
  70.5 22.4 %all-to-all-start.2 = ((bf16[64,8,512]{2,1,0:T(8,128)(2,1)}), bf16[64,8,512]{2,1,0:T(8,128)(2,1)S(1)}, u32[]{:S(2)}, u32[]{:S(2)}) async-start(bf16[64,8,512]{2,1,0:T(8,128)(2,1)} %bitcast.26), calls=%async_computation.2 | async-start | bytes 1048576 | tf_op jit(solution)/shard_map/all_to_all | solution.py:509
  75.4 65.5 %copy-start.6 = (f32[1,384]{1,0:T(1,128)}, f32[1,384]{1,0:T(1,128)S(1)}, u32[]{:S(2)}) copy-start(f32[1,384]{1,0:T(1,128)S(1)} %reshape_reshape.3.refs_6_.refs_5_.skip) | copy-start | bytes 4612
  143.8 18.9 %all-to-all-start.5 = ((bf16[64,8,256]{2,1,0:T(8,128)(2,1)}), bf16[64,8,256]{2,1,0:T(8,128)(2,1)S(1)}, u32[]{:S(2)}, u32[]{:S(2)}) async-start(bf16[64,8,256]{2,1,0:T(8,128)(2,1)} %bitcast.28), calls=%async_computation.5 | async-start | bytes 524288 | tf_op jit(solution)/shard_map/all_to_all | solution.py:509
  149.5 13.2 %copy-start.3 = (bf16[6,512]{1,0:T(8,128)(2,1)S(1)}, bf16[6,512]{1,0:T(8,128)(2,1)}, u32[]{:S(2)}) copy-start(bf16[6,512]{1,0:T(8,128)(2,1)} %refs_3_.10) | copy-start | bytes 18436
  165.2 22.4 %all-to-all-start.6 = ((bf16[64,8,512]{2,1,0:T(8,128)(2,1)}), bf16[64,8,512]{2,1,0:T(8,128)(2,1)S(1)}, u32[]{:S(2)}, u32[]{:S(2)}) async-start(bf16[64,8,512]{2,1,0:T(8,128)(2,1)} %bitcast.25), calls=%async_computation.6 | async-start | bytes 1048576 | tf_op jit(solution)/shard_map/all_to_all | solution.py:509
  170.0 17.7 %copy-start.5 = (bf16[6,512]{1,0:T(8,128)(2,1)S(1)}, bf16[6,512]{1,0:T(8,128)(2,1)}, u32[]{:S(2)}) copy-start(bf16[6,512]{1,0:T(8,128)(2,1)} %refs_3_.11) | copy-start | bytes 18436

commit v3 on v2

--- a/solution.py
+++ b/solution.py
@@ -201,7 +201,7 @@
             )
             if index == target:
                 total += crossing[:, cols]
-            out_ref[span, cols] = total
+            out_ref[span, cols] = total.astype(out_ref.dtype)
 
 
 def open_raster(x, in_map, out_map, decay_f, decay_r, grad, route, pay, stage):
@@ -226,7 +226,7 @@
     pay.send(cols=slice(1024, 1152))
 
 
-def inner_raster(x, in_map, out_map, decay_f, inner, local):
+def inner_raster(x, in_map, out_map, decay_f, skip, gain, inner, local):
     lower = lower_ones()
     decay = padded_decay(decay_f)
     build_inner(out_map, in_map, decay, lower, inner)
@@ -269,14 +269,12 @@
     running = running_of(decay_f)
     entering = join_state(got[:, 0:128])
     pay[:, 384:512] = carry(links, got[:, 128:256], False).astype(BF16)
-    pay.send(cols=slice(384, 512))
     for rows in BANDS:
-        value = local[rows, :] + jnp.exp(running[rows]) * dot(out_map[rows, :], entering)
+        value = local[rows, :].astype(F32) + jnp.exp(running[rows]) * dot(out_map[rows, :], entering)
         y[rows, :] = value.astype(BF16)
         put_band(stage, route, rows, value)
     y.send()
     pay[:, 0:384] = sent(stage, 3).astype(BF16)
-    pay.send(cols=slice(0, 384))
 
 
 def finish_scan(
@@ -287,11 +285,9 @@
     weight = jnp.exp(running[TOK - 1 : TOK, :] - running)
     fill(stage, got[:, 0:384])
     y_forward = own_band(stage, route, ALL, 3)
-    y[...] = (local[...] + weight * dot(out_map[...], entering)).astype(BF16)
-    y.send()
+    y[...] = (local[...].astype(F32) + weight * dot(out_map[...], entering)).astype(BF16)
     total = y_forward + y[...].astype(F32) + skip[...] * x[...].astype(F32)
     combined[...] = total
-    combined.send()
     scaled = gain[...] * grad[...].astype(F32)
     squares, inner = token_sums(total * total), token_sums(total * scaled)
     row = iota((UNIT, LANES), 0)
@@ -329,13 +325,11 @@
     put_band(stage, route, ALL, dot(parts, lanes, 0, 0), 3)
     put_band(stage, route, ALL, y[...].astype(F32))
     pay[:, 0:384] = sent(stage, 3).astype(BF16)
-    pay.send(cols=slice(0, 384))
     scaled = gain[...] * grad[...].astype(F32)
     back[...] = gradient(combined[...], scaled, wide[:, 0:WIDTH], wide[:, WIDTH:])
     back.send()
     state = local_state(out_map[...], back[...], jnp.exp(running[TOK - 1 : TOK] - running))
     pay[:, 384:512] = (cut_state(state) + stage[3]).astype(BF16)
-    pay.send(cols=slice(384, 512))
 
 
 def inner_back_scan(inner, back, in_map, out_map, decay_r, local):
@@ -371,7 +365,7 @@
 
 def inner_back_raster(inner, back, in_map, out_map, decay_f, skip, local):
     apply_inner(inner, back, out_map, in_map, running_of(decay_f), False, local)
-    local[...] += skip[...] * back[...].astype(F32)
+    local[...] = (local[...].astype(F32) + skip[...] * back[...].astype(F32)).astype(BF16)
 
 
 def finish_back_scan(got, in_map, local, decay_r, links, route, pay, stage):
@@ -380,7 +374,7 @@
     pay[:, 384:512] = carry(links, got[:, 128:256], False).astype(BF16)
     pay.send(cols=slice(384, 512))
     for rows in BANDS:
-        value = local[rows, :] + jnp.exp(running[rows]) * dot(in_map[rows, :], entering)
+        value = local[rows, :].astype(F32) + jnp.exp(running[rows]) * dot(in_map[rows, :], entering)
         put_band(stage, route, rows, value)
     pay[:, 0:384] = sent(stage, 3).astype(BF16)
     pay.send(cols=slice(0, 384))
@@ -393,7 +387,7 @@
     fill(stage, got[:, 0:384])
     for rows in BANDS:
         carried = jnp.exp(last - running[rows]) * dot(in_map[rows, :], entering)
-        total = local[rows, :] + carried + own_band(stage, route, rows, 3)
+        total = local[rows, :].astype(F32) + carried + own_band(stage, route, rows, 3)
         out[rows, :] = total.astype(BF16)
         out.send(rows)
 
@@ -456,6 +450,7 @@
 def kernel(body, outs, *operands, arrived=0, stage=0, flops=400_000_000):
     shapes = [jax.ShapeDtypeStruct(*out[:2]) for out in outs]
     size = sum(a.size * a.dtype.itemsize for a in (*operands, *shapes))
+    sends = [(*out, 1)[2] for out in outs]
     count = len(operands)
     own = [
         place >= arrived and (not arrived or a.dtype == jnp.int32 or a.size > 5_000)
@@ -470,21 +465,26 @@
         for place in sorted(range(count), key=lambda k: operands[k].size):
             if own[place]:
                 given[place] = Arriving(sources[place], *held[place])
-        results = [Leaving(next(scratch), target, next(scratch)) for target in targets]
+        results = [
+            Leaving(next(scratch), target, next(scratch)) if times else target
+            for target, times in zip(targets, sends, strict=True)
+        ]
         body(*given, *results, *([next(scratch)] if stage else []))
         for operand in given:
             if isinstance(operand, Arriving):
                 operand.land()
         for result in results:
-            result.finish()
+            if isinstance(result, Leaving):
+                result.finish()
 
     scratch_shapes = []
     for operand, mine in zip(operands, own, strict=True):
         if mine:
             space = pltpu.SMEM if operand.dtype == jnp.int32 else pltpu.VMEM
             scratch_shapes += [space(operand.shape, operand.dtype), pltpu.SemaphoreType.DMA]
-    for shape, dtype, *sends in outs:
-        scratch_shapes += [pltpu.VMEM(shape, dtype), pltpu.SemaphoreType.DMA((*sends, 1)[:1])]
+    for shape, times in zip(shapes, sends, strict=True):
+        if times:
+            scratch_shapes += [pltpu.VMEM(shape.shape, shape.dtype), pltpu.SemaphoreType.DMA((times,))]
     if stage:
         scratch_shapes.append(pltpu.VMEM((stage // LANES, TOK, LANES), F32))
     whole = pl.BlockSpec(memory_space=pltpu.VMEM)
@@ -495,9 +495,12 @@
     ]
     return pl.pallas_call(
         wrapped,
-        out_shape=[pltpu.HBM(*out[:2]) for out in outs],
+        out_shape=[
+            pltpu.HBM(shape.shape, shape.dtype) if times else shape
+            for shape, times in zip(shapes, sends, strict=True)
+        ],
         in_specs=[apart if mine else whole for mine in own],
-        out_specs=[apart] * len(outs),
+        out_specs=[apart if times else whole for times in sends],
         scratch_shapes=scratch_shapes,
         compiler_params=pltpu.CompilerParams(vmem_limit_bytes=48 * 2**20),
         cost_estimate=pl.CostEstimate(flops=flops, bytes_accessed=size, transcendentals=0),
@@ -539,8 +542,8 @@
     )
     got1 = exchange(pay1)
     inner_f, local_f = whole_kernel(
-        inner_raster, [inner16, wide32],
-        ssm_input, input_map, output_map, decay_forward, flops=8_000_000_000,
+        inner_raster, [inner16, wide16],
+        ssm_input, input_map, output_map, decay_forward, skip, gain, flops=8_000_000_000,
     )
     x_scan, in_scan, pay2 = kernel(
         open_scan, [wide16, rows16, pay(256)],
@@ -549,26 +552,26 @@
     got2 = exchange(pay2)
     links32 = ((UNITS, LANES), F32)
     out_scan, grad_scan, inner_r, local_r, links_f, links_r = whole_kernel(
-        inner_scan, [rows16, wide16, inner16, wide32, links32, links32],
+        inner_scan, [rows16, wide16, inner16, wide16, links32, links32],
         got1, x_scan, in_scan, decay_reverse, to_raster, flops=8_000_000_000, work=True,
     )
     y_forward, pay3 = kernel(
-        finish_raster, [wide16, pay(512)],
+        finish_raster, [wide16, pay(512, 0)],
         got2, output_map, local_f, decay_forward, links_r, to_scan, arrived=1, stage=384,
     )
     got3 = exchange(pay3)
     y_scan, combined, stats = kernel(
-        finish_scan, [wide16, wide32, ((64, LANES), F32)],
+        finish_scan, [(*wide16, 0), (*wide32, 0), ((64, LANES), F32, 0)],
         got3, out_scan, local_r, decay_reverse, x_scan, grad_scan, skip, gain, to_raster, arrived=1, stage=384,
     )
     all_stats = lax.all_to_all(stats, "head", split_axis=0, concat_axis=0, tiled=True)
     back_scan, pay4 = kernel(
-        open_back, [wide16, pay(512)],
-        all_stats, combined, y_scan, out_scan, grad_scan, gain, decay_reverse, to_raster, arrived=1, stage=512,
+        open_back, [wide16, pay(512, 0)],
+        all_stats, combined, y_scan, out_scan, grad_scan, gain, decay_reverse, to_raster, arrived=3, stage=512,
     )
     got4 = exchange(pay4)
     (local_br,) = whole_kernel(
-        inner_back_scan, [wide32], inner_r, back_scan, in_scan, out_scan, decay_reverse,
+        inner_back_scan, [wide16], inner_r, back_scan, in_scan, out_scan, decay_reverse,
         flops=4_000_000_000,
     )
     normed, back, pay5 = kernel(
@@ -578,7 +581,7 @@
     )
     got5 = exchange(pay5)
     (local_bf,) = whole_kernel(
-        inner_back_raster, [wide32], inner_f, back, input_map, output_map, decay_forward, skip,
+        inner_back_raster, [wide16], inner_f, back, input_map, output_map, decay_forward, skip,
         flops=4_000_000_000,
     )
     (pay6,) = kernel(

time: 191 us -> 188 us (0.984)
  blocking collectives: 41.8 us -> 63.6 us
  waiting for transfers between devices: 75.6 us -> 57.2 us
  starting transfers between devices: 33.4 us -> 28.7 us
  Pallas kernels: 38.1 us -> 35 us
    all_to_all x1 -> x2, blocking collectives: 24.8 us -> 46.8 us  [exchange(): return lax.all_to_all(pay, 'seq', split_axis=0, concat_axis=0, tiled=True)]
    all_to_all x5 -> x4, waiting for transfers between devices: 75.6 us -> 57.2 us  [exchange(): return lax.all_to_all(pay, 'seq', split_axis=0, concat_axis=0, tiled=True)]
    all_to_all x5 -> x4, starting transfers between devices: 33.4 us -> 28.7 us  [exchange(): return lax.all_to_all(pay, 'seq', split_axis=0, concat_axis=0, tiled=True)]
    pallas_call x8, Pallas kernels: 21.6 us -> 19 us  [kernel(): pl.pallas_call(wrapped, out_shape=[pltpu.HBM(shape.shape, shape.dtype) if...]
  transfers between devices with their start and end apart: 5 -> 4, of which waited for: 5 -> 4; matrix products, arithmetic and copies ran while one was open for 0% -> 1% of each run, Pallas kernels for 9% -> 9%
where the time goes in v3:
time: 188 us; the launch traced here: 187 us
  blocking collectives  63.6 us (34%)
  waiting for transfers between devices  57.2 us (30%)
  Pallas kernels  35 us (19%)
  starting transfers between devices  28.7 us (15%)
    all_to_all x4, waiting for transfers between devices, exchange(): return lax.all_to_all(pay, 'seq', split_axis=0, concat_axis=0, tiled=True)  57.2 us
    all_to_all x2, blocking collectives, exchange(): return lax.all_to_all(pay, 'seq', split_axis=0, concat_axis=0, tiled=True)  46.8 us
    all_to_all x4, starting transfers between devices, exchange(): return lax.all_to_all(pay, 'seq', split_axis=0, concat_axis=0, tiled=True)  28.7 us
    pallas_call x8, Pallas kernels, kernel(): pl.pallas_call(wrapped, out_shape=[pltpu.HBM(shape.shape, shape.dtype) if...  19 us
    all_to_all x1, blocking collectives, shards(): lax.all_to_all(stats, 'head', split_axis=0, concat_axis=0, tiled=True)  16.8 us
    pallas_call x4, Pallas kernels, whole_kernel(): pl.pallas_call(body, out_shape=shapes, scratch_shapes=[pltpu.VMEM((1, TOK...  16.1 us
  transfers between devices with their start and end apart: 4, of which 4 were waited for; matrix products, arithmetic and copies ran while one was open for 1% of the time, Pallas kernels for 9%

profile of v3, /device:TPU:1, one launch (start us, length us, event | category | flops | bytes accessed | tf_op | source)
XLA Modules:
  0.0 186.9 jit_solution(12285068641232234926)
XLA Ops:
  0.6 3.0 %open_raster.1 = bf16[512,1152]{1,0:T(8,128)(2,1)} custom-call(bf16[512,384]{1,0:T(8,128)(2,1)} %refs_2_.3, bf16[512,128]{1,0:T(8,128)(2,1)} %refs_1_.7, bf16[512,128]{1,0:T(8,128)(2,1)} %out_map.3, bf16[6,512]{1,0:T(8,128)(2,1)} %refs_3_.11, bf16[6,512]{1,0:T(8,128)(2,1)} %refs_3_.10, bf16[512,384]{1,0:T(8,128)(2,1)} %refs_4_.3, s32[1,64]{1,0:T(1,128)} %bitcast.36), custom_call_target="tpu_custom_call" | custom-call | flops 400000000 | bytes 2240768 | tf_op jit(solution)/shard_map/open_raster/pallas_call | solution.py:496
  3.6 0.0 copy-start.8
  3.7 0.0 copy-start.9
  3.7 11.6 %all-to-all-start = ((bf16[64,8,1152]{2,1,0:T(8,128)(2,1)}), bf16[64,8,1152]{2,1,0:T(8,128)(2,1)S(1)}, u32[]{:S(2)}, u32[]{:S(2)}) async-start(bf16[64,8,1152]{2,1,0:T(8,128)(2,1)} %bitcast.27), calls=%async_computation | async-start | bytes 2359296 | tf_op jit(solution)/shard_map/all_to_all | solution.py:512
  15.3 0.0 copy-done.8
  15.3 0.6 reshape.29.gain.refs_7_.refs_5_.refs_6_
  15.9 0.0 copy-done.9
  15.9 0.1 broadcast_in_dim.3
  16.0 0.6 reshape_reshape.3.skip.refs_6_.refs_5_
  16.6 0.0 copy-start.1
  16.6 3.6 %inner_raster.1 = (bf16[2,6,256,256]{3,2,1,0:T(8,128)(2,1)}, bf16[512,384]{1,0:T(8,128)(2,1)}) custom-call(bf16[512,384]{1,0:T(8,128)(2,1)} %refs_2_.3, bf16[512,128]{1,0:T(8,128)(2,1)} %refs_1_.7, bf16[512,128]{1,0:T(8,128)(2,1)} %out_map.3, bf16[6,512]{1,0:T(8,128)(2,1)} %refs_3_.11, f32[1,384]{1,0:T(1,128)} %reshape_reshape.3.skip.refs_6_.refs_5_, ...), custom_call_target="tpu_custom_call" | custom-call | flops 8000000000 | bytes 2630656 | tf_op jit(solution)/shard_map/inner_raster/pallas_call | solution.py:440
  20.3 25.6 %all-to-all-done = bf16[64,8,1152]{2,1,0:T(8,128)(2,1)S(1)} async-done(((bf16[64,8,1152]{2,1,0:T(8,128)(2,1)}), bf16[64,8,1152]{2,1,0:T(8,128)(2,1)S(1)}, u32[]{:S(2)}, u32[]{:S(2)}) %all-to-all-start) | async-done | bytes 1179680 | tf_op jit(solution)/shard_map/all_to_all | solution.py:512
  45.9 0.0 copy-start
  45.9 0.0 copy-done.1
  45.9 2.2 %open_scan.1 = (bf16[512,384]{1,0:T(8,128)(2,1)}, bf16[512,128]{1,0:T(8,128)(2,1)}, bf16[512,256]{1,0:T(8,128)(2,1)}) custom-call(bf16[512,1152]{1,0:T(8,128)(2,1)S(1)} %bitcast.18, bf16[6,512]{1,0:T(8,128)(2,1)S(1)} %copy-done.1, s32[1,64]{1,0:T(1,128)} %bitcast.31), custom_call_target="tpu_custom_call" | custom-call | flops 400000000 | bytes 1972480 | tf_op jit(solution)/shard_map/open_scan/pallas_call | solution.py:496
  48.1 6.6 %all-to-all-start.1 = ((bf16[64,8,256]{2,1,0:T(8,128)(2,1)}), bf16[64,8,256]{2,1,0:T(8,128)(2,1)S(1)}, u32[]{:S(2)}, u32[]{:S(2)}) async-start(bf16[64,8,256]{2,1,0:T(8,128)(2,1)} %bitcast.30), calls=%async_computation.1 | async-start | bytes 524288 | tf_op jit(solution)/shard_map/all_to_all | solution.py:512
  54.8 0.0 copy-done
  54.8 0.0 copy-start.4
  54.8 4.7 %inner_scan.1 = (bf16[512,128]{1,0:T(8,128)(2,1)}, bf16[512,384]{1,0:T(8,128)(2,1)}, bf16[2,6,256,256]{3,2,1,0:T(8,128)(2,1)}, bf16[512,384]{1,0:T(8,128)(2,1)}, f32[64,128]{1,0:T(8,128)}, /*index=5*/f32[64,128]{1,0:T(8,128)}) custom-call(bf16[512,1152]{1,0:T(8,128)(2,1)} %bitcast.19, bf16[512,384]{1,0:T(8,128)(2,1)} %get-tuple-element.25.x.refs_4_, ...), custom_call_target="tpu_custom_call" | custom-call | flops 8000000000 | bytes 4266240 | tf_op jit(solution)/shard_map/inner_scan/pallas_call | solution.py:440
  59.5 0.0 copy-start.2
  59.5 0.0 copy-start.6
  59.5 0.0 copy-start.7
  59.5 8.4 %all-to-all-done.1 = bf16[64,8,256]{2,1,0:T(8,128)(2,1)S(1)} async-done(((bf16[64,8,256]{2,1,0:T(8,128)(2,1)}), bf16[64,8,256]{2,1,0:T(8,128)(2,1)S(1)}, u32[]{:S(2)}, u32[]{:S(2)}) %all-to-all-start.1) | async-done | bytes 262176 | tf_op jit(solution)/shard_map/all_to_all | solution.py:512
  67.9 0.0 copy-done.4
  67.9 2.3 %finish_raster.1 = (bf16[512,384]{1,0:T(8,128)(2,1)}, bf16[512,512]{1,0:T(8,128)(2,1)S(1)}) custom-call(bf16[512,256]{1,0:T(8,128)(2,1)S(1)} %bitcast.23, bf16[512,128]{1,0:T(8,128)(2,1)} %out_map.3, bf16[512,384]{1,0:T(8,128)(2,1)} %get-tuple-element.24.refs_2_, bf16[6,512]{1,0:T(8,128)(2,1)S(1)} %copy-done.4, f32[64,128]{1,0:T(8,128)} %get-tuple-element.27.refs_4_.refs_8_, ...), custom_call_target="tpu_custom_call" | custom-call | flops 400000000 | bytes 1743104 | tf_op jit(solution)/shard_map/finish_raster/pallas_call | solution.py:496
  70.3 22.2 %all_to_all.77 = bf16[64,8,512]{2,1,0:T(8,128)(2,1)S(1)} all-to-all(bf16[64,8,512]{2,1,0:T(8,128)(2,1)S(1)} %bitcast.22), channel_id=1, replica_groups=mesh['seq'=64,'head'=8] {'seq'}, dimensions={0} | all-to-all | bytes 1048576 | tf_op jit(solution)/shard_map/all_to_all | solution.py:512
  92.5 0.0 copy-done.2
  92.5 0.0 copy-done.6
  92.5 0.0 copy-done.7
  92.5 1.9 %finish_scan.1 = (bf16[512,384]{1,0:T(8,128)(2,1)S(1)}, f32[512,384]{1,0:T(8,128)S(1)}, f32[64,128]{1,0:T(8,128)S(1)}) custom-call(bf16[512,512]{1,0:T(8,128)(2,1)S(1)} %bitcast.17, bf16[512,128]{1,0:T(8,128)(2,1)} %get-tuple-element.29.refs_1_.refs_3_.out_map, bf16[512,384]{1,0:T(8,128)(2,1)} %get-tuple-element.30.refs_2_, bf16[6,512]{1,0:T(8,128)(2,1)S(1)} %copy-done.2, ...), custom_call_target="tpu_custom_call" | custom-call | flops 400000000 | bytes 3056896 | tf_op jit(solution)/shard_map/finish_scan/pallas_call | solution.py:496
  94.5 16.8 %all_to_all.78 = f32[8,8,128]{2,1,0:T(8,128)S(1)} all-to-all(f32[8,8,128]{2,1,0:T(8,128)S(1)} %bitcast.26), channel_id=1, replica_groups=mesh['seq'=64,'head'=8] {'head'}, dimensions={0} | all-to-all | bytes 65536 | tf_op jit(solution)/shard_map/all_to_all | solution.py:567
  111.3 2.1 %open_back.1 = (bf16[512,384]{1,0:T(8,128)(2,1)}, bf16[512,512]{1,0:T(8,128)(2,1)S(1)}) custom-call(f32[64,128]{1,0:T(8,128)S(1)} %bitcast.25, f32[512,384]{1,0:T(8,128)S(1)} %get-tuple-element.33.refs_1_, bf16[512,384]{1,0:T(8,128)(2,1)S(1)} %get-tuple-element.34.refs_2_, bf16[512,128]{1,0:T(8,128)(2,1)} %get-tuple-element.29.refs_1_.refs_3_.out_map, ...), custom_call_target="tpu_custom_call" | custom-call | flops 400000000 | bytes 2662144 | tf_op jit(solution)/shard_map/open_back/pallas_call | solution.py:496
  113.3 24.6 %all_to_all.79 = bf16[64,8,512]{2,1,0:T(8,128)(2,1)S(1)} all-to-all(bf16[64,8,512]{2,1,0:T(8,128)(2,1)S(1)} %bitcast.21), channel_id=1, replica_groups=mesh['seq'=64,'head'=8] {'seq'}, dimensions={0} | all-to-all | bytes 1048576 | tf_op jit(solution)/shard_map/all_to_all | solution.py:512
  137.9 2.9 %middle_raster.1 = (bf16[512,384]{1,0:T(8,128)(2,1)}, bf16[512,384]{1,0:T(8,128)(2,1)}, bf16[512,256]{1,0:T(8,128)(2,1)}) custom-call(bf16[512,512]{1,0:T(8,128)(2,1)S(1)} %bitcast.16, bf16[512,384]{1,0:T(8,128)(2,1)} %get-tuple-element.36.refs_1_, bf16[512,384]{1,0:T(8,128)(2,1)} %refs_2_.3, bf16[512,128]{1,0:T(8,128)(2,1)} %out_map.3, ...), custom_call_target="tpu_custom_call" | custom-call | flops 400000000 | bytes 2925824 | tf_op jit(solution)/shard_map/middle_raster/pallas_call | solution.py:496
  140.8 5.7 %all-to-all-start.5 = ((bf16[64,8,256]{2,1,0:T(8,128)(2,1)}), bf16[64,8,256]{2,1,0:T(8,128)(2,1)S(1)}, u32[]{:S(2)}, u32[]{:S(2)}) async-start(bf16[64,8,256]{2,1,0:T(8,128)(2,1)} %bitcast.29), calls=%async_computation.5 | async-start | bytes 524288 | tf_op jit(solution)/shard_map/all_to_all | solution.py:512
  146.5 0.0 copy-start.3
  146.6 3.8 %inner_back_scan.1.refs_2_ = bf16[512,384]{1,0:T(8,128)(2,1)} custom-call(bf16[2,6,256,256]{3,2,1,0:T(8,128)(2,1)} %get-tuple-element.39.inner, bf16[512,384]{1,0:T(8,128)(2,1)} %get-tuple-element.40.back, bf16[512,128]{1,0:T(8,128)(2,1)} %get-tuple-element.26.in_map.refs_1_, bf16[512,128]{1,0:T(8,128)(2,1)} %get-tuple-element.29.refs_1_.refs_3_.out_map, ...), custom_call_target="tpu_custom_call" | custom-call | flops 4000000000 | bytes 2627584 | tf_op jit(solution)/shard_map/inner_back_scan/pallas_call | solution.py:440
  150.3 9.4 %all-to-all-done.5 = bf16[64,8,256]{2,1,0:T(8,128)(2,1)S(1)} async-done(((bf16[64,8,256]{2,1,0:T(8,128)(2,1)}), bf16[64,8,256]{2,1,0:T(8,128)(2,1)S(1)}, u32[]{:S(2)}, u32[]{:S(2)}) %all-to-all-start.5) | async-done | bytes 262176 | tf_op jit(solution)/shard_map/all_to_all | solution.py:512
  159.7 0.0 copy-done.3
  159.7 2.4 %finish_back_scan.1 = bf16[512,512]{1,0:T(8,128)(2,1)} custom-call(bf16[512,256]{1,0:T(8,128)(2,1)S(1)} %bitcast.24, bf16[512,128]{1,0:T(8,128)(2,1)} %get-tuple-element.26.in_map.refs_1_, bf16[512,384]{1,0:T(8,128)(2,1)} %inner_back_scan.1.refs_2_, bf16[6,512]{1,0:T(8,128)(2,1)S(1)} %copy-done.3, f32[64,128]{1,0:T(8,128)} %get-tuple-element.41.refs_4_, ...), custom_call_target="tpu_custom_call" | custom-call | flops 400000000 | bytes 1349888 | tf_op jit(solution)/shard_map/finish_back_scan/pallas_call | solution.py:496
  162.1 4.7 %all-to-all-start.6 = ((bf16[64,8,512]{2,1,0:T(8,128)(2,1)}), bf16[64,8,512]{2,1,0:T(8,128)(2,1)S(1)}, u32[]{:S(2)}, u32[]{:S(2)}) async-start(bf16[64,8,512]{2,1,0:T(8,128)(2,1)} %bitcast.28), calls=%async_computation.6 | async-start | bytes 1048576 | tf_op jit(solution)/shard_map/all_to_all | solution.py:512
  166.9 0.0 copy-start.5
  166.9 4.0 %inner_back_raster.1.refs_2_ = bf16[512,384]{1,0:T(8,128)(2,1)} custom-call(bf16[2,6,256,256]{3,2,1,0:T(8,128)(2,1)} %get-tuple-element.42.inner, bf16[512,384]{1,0:T(8,128)(2,1)} %get-tuple-element.43.back, bf16[512,128]{1,0:T(8,128)(2,1)} %refs_1_.7, bf16[512,128]{1,0:T(8,128)(2,1)} %out_map.3, bf16[6,512]{1,0:T(8,128)(2,1)} %refs_3_.11, ...), custom_call_target="tpu_custom_call" | custom-call | flops 4000000000 | bytes 2629120 | tf_op jit(solution)/shard_map/inner_back_raster/pallas_call | solution.py:440
  170.8 13.7 %all-to-all-done.6 = bf16[64,8,512]{2,1,0:T(8,128)(2,1)S(1)} async-done(((bf16[64,8,512]{2,1,0:T(8,128)(2,1)}), bf16[64,8,512]{2,1,0:T(8,128)(2,1)S(1)}, u32[]{:S(2)}, u32[]{:S(2)}) %all-to-all-start.6) | async-done | bytes 524320 | tf_op jit(solution)/shard_map/all_to_all | solution.py:512
  184.6 0.0 copy-done.5
  184.6 2.1 %finish_back_raster.1 = bf16[512,384]{1,0:T(8,128)(2,1)} custom-call(bf16[512,512]{1,0:T(8,128)(2,1)S(1)} %bitcast.20, bf16[512,128]{1,0:T(8,128)(2,1)} %refs_1_.7, bf16[512,384]{1,0:T(8,128)(2,1)} %inner_back_raster.1.refs_2_, bf16[6,512]{1,0:T(8,128)(2,1)S(1)} %copy-done.5, s32[1,64]{1,0:T(1,128)} %bitcast.39), custom_call_target="tpu_custom_call" | custom-call | flops 400000000 | bytes 1448192 | tf_op jit(solution)/shard_map/finish_back_raster/pallas_call | solution.py:496
Async XLA Ops:
  3.6 11.7 %copy-start.8 = (f32[384]{0:T(512)S(1)}, f32[384]{0:T(512)}, u32[]{:S(2)}) copy-start(f32[384]{0:T(512)} %param.16) | copy-start | bytes 4612
  3.7 12.3 %copy-start.9 = (f32[6]{0:T(128)S(1)}, f32[6]{0:T(128)}, u32[]{:S(2)}) copy-start(f32[6]{0:T(128)} %param.15) | copy-start | bytes 76
  3.7 42.2 %all-to-all-start = ((bf16[64,8,1152]{2,1,0:T(8,128)(2,1)}), bf16[64,8,1152]{2,1,0:T(8,128)(2,1)S(1)}, u32[]{:S(2)}, u32[]{:S(2)}) async-start(bf16[64,8,1152]{2,1,0:T(8,128)(2,1)} %bitcast.27), calls=%async_computation | async-start | bytes 2359296 | tf_op jit(solution)/shard_map/all_to_all | solution.py:512
  16.6 29.3 %copy-start.1 = (bf16[6,512]{1,0:T(8,128)(2,1)S(1)}, bf16[6,512]{1,0:T(8,128)(2,1)}, u32[]{:S(2)}) copy-start(bf16[6,512]{1,0:T(8,128)(2,1)} %refs_3_.10) | copy-start | bytes 18436
  45.9 8.9 %copy-start = (bf16[64,8,1152]{2,1,0:T(8,128)(2,1)}, bf16[64,8,1152]{2,1,0:T(8,128)(2,1)S(1)}, u32[]{:S(2)}) copy-start(bf16[64,8,1152]{2,1,0:T(8,128)(2,1)S(1)} %all-to-all-done) | copy-start | bytes 3538948
  48.1 19.8 %all-to-all-start.1 = ((bf16[64,8,256]{2,1,0:T(8,128)(2,1)}), bf16[64,8,256]{2,1,0:T(8,128)(2,1)S(1)}, u32[]{:S(2)}, u32[]{:S(2)}) async-start(bf16[64,8,256]{2,1,0:T(8,128)(2,1)} %bitcast.30), calls=%async_computation.1 | async-start | bytes 524288 | tf_op jit(solution)/shard_map/all_to_all | solution.py:512
  54.8 13.2 %copy-start.4 = (bf16[6,512]{1,0:T(8,128)(2,1)S(1)}, bf16[6,512]{1,0:T(8,128)(2,1)}, u32[]{:S(2)}) copy-start(bf16[6,512]{1,0:T(8,128)(2,1)} %refs_3_.11) | copy-start | bytes 18436
  59.5 33.0 %copy-start.2 = (bf16[6,512]{1,0:T(8,128)(2,1)S(1)}, bf16[6,512]{1,0:T(8,128)(2,1)}, u32[]{:S(2)}) copy-start(bf16[6,512]{1,0:T(8,128)(2,1)} %refs_3_.10) | copy-start | bytes 18436
  59.5 33.0 %copy-start.6 = (f32[1,384]{1,0:T(1,128)S(1)}, f32[1,384]{1,0:T(1,128)}, u32[]{:S(2)}) copy-start(f32[1,384]{1,0:T(1,128)} %reshape.29.gain.refs_7_.refs_5_.refs_6_) | copy-start | bytes 4612
  59.5 33.0 %copy-start.7 = (f32[1,384]{1,0:T(1,128)S(1)}, f32[1,384]{1,0:T(1,128)}, u32[]{:S(2)}) copy-start(f32[1,384]{1,0:T(1,128)} %reshape_reshape.3.skip.refs_6_.refs_5_) | copy-start | bytes 4612
  140.8 18.9 %all-to-all-start.5 = ((bf16[64,8,256]{2,1,0:T(8,128)(2,1)}), bf16[64,8,256]{2,1,0:T(8,128)(2,1)S(1)}, u32[]{:S(2)}, u32[]{:S(2)}) async-start(bf16[64,8,256]{2,1,0:T(8,128)(2,1)} %bitcast.29), calls=%async_computation.5 | async-start | bytes 524288 | tf_op jit(solution)/shard_map/all_to_all | solution.py:512
  146.5 13.2 %copy-start.3 = (bf16[6,512]{1,0:T(8,128)(2,1)S(1)}, bf16[6,512]{1,0:T(8,128)(2,1)}, u32[]{:S(2)}) copy-start(bf16[6,512]{1,0:T(8,128)(2,1)} %refs_3_.10) | copy-start | bytes 18436
  162.1 22.4 %all-to-all-start.6 = ((bf16[64,8,512]{2,1,0:T(8,128)(2,1)}), bf16[64,8,512]{2,1,0:T(8,128)(2,1)S(1)}, u32[]{:S(2)}, u32[]{:S(2)}) async-start(bf16[64,8,512]{2,1,0:T(8,128)(2,1)} %bitcast.28), calls=%async_computation.6 | async-start | bytes 1048576 | tf_op jit(solution)/shard_map/all_to_all | solution.py:512
  166.9 17.7 %copy-start.5 = (bf16[6,512]{1,0:T(8,128)(2,1)S(1)}, bf16[6,512]{1,0:T(8,128)(2,1)}, u32[]{:S(2)}) copy-start(bf16[6,512]{1,0:T(8,128)(2,1)} %refs_3_.11) | copy-start | bytes 18436

commit v4 on v3

--- a/solution.py
+++ b/solution.py
@@ -201,7 +201,7 @@
             )
             if index == target:
                 total += crossing[:, cols]
-            out_ref[span, cols] = total.astype(out_ref.dtype)
+            out_ref[span, cols] = total.astype(BF16)
 
 
 def open_raster(x, in_map, out_map, decay_f, decay_r, grad, route, pay, stage):
@@ -332,7 +332,7 @@
     pay[:, 384:512] = (cut_state(state) + stage[3]).astype(BF16)
 
 
-def inner_back_scan(inner, back, in_map, out_map, decay_r, local):
+def inner_back_scan(decay_r, inner, back, in_map, out_map, local):
     apply_inner(inner, back, out_map, in_map, running_of(decay_r), True, local)
 
 
@@ -363,7 +363,7 @@
     pay.send(cols=slice(128, 256))
 
 
-def inner_back_raster(inner, back, in_map, out_map, decay_f, skip, local):
+def inner_back_raster(decay_f, inner, back, in_map, out_map, skip, local):
     apply_inner(inner, back, out_map, in_map, running_of(decay_f), False, local)
     local[...] = (local[...].astype(F32) + skip[...] * back[...].astype(F32)).astype(BF16)
 
@@ -372,12 +372,10 @@
     running = running_of(decay_r)
     entering = join_state(got[:, 0:128])
     pay[:, 384:512] = carry(links, got[:, 128:256], False).astype(BF16)
-    pay.send(cols=slice(384, 512))
     for rows in BANDS:
         value = local[rows, :].astype(F32) + jnp.exp(running[rows]) * dot(in_map[rows, :], entering)
         put_band(stage, route, rows, value)
     pay[:, 0:384] = sent(stage, 3).astype(BF16)
-    pay.send(cols=slice(0, 384))
 
 
 def finish_back_raster(got, in_map, local, decay_f, route, out, stage):
@@ -447,7 +445,7 @@
     )(*operands)
 
 
-def kernel(body, outs, *operands, arrived=0, stage=0, flops=400_000_000):
+def kernel(body, outs, *operands, arrived=0, stage=0, after=(), flops=400_000_000):
     shapes = [jax.ShapeDtypeStruct(*out[:2]) for out in outs]
     size = sum(a.size * a.dtype.itemsize for a in (*operands, *shapes))
     sends = [(*out, 1)[2] for out in outs]
@@ -458,8 +456,8 @@
     ]
 
     def wrapped(*refs):
-        sources, targets = refs[:count], refs[count : count + len(outs)]
-        scratch = iter(refs[count + len(outs) :])
+        sources, refs = refs[:count], refs[count + len(after) :]
+        targets, scratch = refs[: len(outs)], iter(refs[len(outs) :])
         held = [(next(scratch), next(scratch)) if mine else None for mine in own]
         given = list(sources)
         for place in sorted(range(count), key=lambda k: operands[k].size):
@@ -499,13 +497,13 @@
             pltpu.HBM(shape.shape, shape.dtype) if times else shape
             for shape, times in zip(shapes, sends, strict=True)
         ],
-        in_specs=[apart if mine else whole for mine in own],
+        in_specs=[apart if mine else whole for mine in own] + [apart] * len(after),
         out_specs=[apart if times else whole for times in sends],
         scratch_shapes=scratch_shapes,
         compiler_params=pltpu.CompilerParams(vmem_limit_bytes=48 * 2**20),
         cost_estimate=pl.CostEstimate(flops=flops, bytes_accessed=size, transcendentals=0),
         name=body.__name__,
-    )(*operands)
+    )(*operands, *(pltpu.with_memory_space_constraint(a, pltpu.HBM) for a in after))
 
 
 def exchange(pay):
@@ -570,9 +568,9 @@
         all_stats, combined, y_scan, out_scan, grad_scan, gain, decay_reverse, to_raster, arrived=3, stage=512,
     )
     got4 = exchange(pay4)
-    (local_br,) = whole_kernel(
-        inner_back_scan, [wide16], inner_r, back_scan, in_scan, out_scan, decay_reverse,
-        flops=4_000_000_000,
+    (local_br,) = kernel(
+        inner_back_scan, [wide16], decay_reverse, inner_r, back_scan, in_scan, out_scan,
+        arrived=1, flops=4_000_000_000,
     )
     normed, back, pay5 = kernel(
         middle_raster, [wide16, wide16, pay(256)],
@@ -580,13 +578,14 @@
         to_scan, arrived=1, stage=512,
     )
     got5 = exchange(pay5)
-    (local_bf,) = whole_kernel(
-        inner_back_raster, [wide16], inner_f, back, input_map, output_map, decay_forward, skip,
-        flops=4_000_000_000,
+    (local_bf,) = kernel(
+        inner_back_raster, [wide16],
+        decay_forward, inner_f, back, input_map, output_map, skip, arrived=1, flops=4_000_000_000,
     )
     (pay6,) = kernel(
-        finish_back_scan, [pay(512)],
+        finish_back_scan, [pay(512, 0)],
         got5, in_scan, local_br, decay_reverse, links_f, to_raster, arrived=1, stage=384,
+        after=(local_bf,),
     )
     got6 = exchange(pay6)
     (grad_input,) = kernel(

time: 188 us -> 187 us (level)
  blocking collectives: 63.6 us -> 85.8 us
  waiting for transfers between devices: 57.2 us -> 41 us
  starting transfers between devices: 28.7 us -> 24 us
  Pallas kernels: 35 us -> 32.7 us
    all_to_all x2 -> x3, blocking collectives: 46.8 us -> 69 us  [exchange(): return lax.all_to_all(pay, 'seq', split_axis=0, concat_axis=0, tiled=True)]
    all_to_all x4 -> x3, waiting for transfers between devices: 57.2 us -> 41 us  [exchange(): return lax.all_to_all(pay, 'seq', split_axis=0, concat_axis=0, tiled=True)]
    pallas_call x4 -> x2, Pallas kernels: 16.1 us -> 8.3 us  [whole_kernel(): pl.pallas_call(body, out_shape=shapes, scratch_shapes=[pltpu.VMEM((1, TOK...]
    pallas_call x8 -> x10, Pallas kernels: 19 us -> 24.4 us  [kernel(): pl.pallas_call(wrapped, out_shape=[pltpu.HBM(shape.shape, shape.dtype) if...]
    all_to_all x4 -> x3, starting transfers between devices: 28.7 us -> 24 us  [exchange(): return lax.all_to_all(pay, 'seq', split_axis=0, concat_axis=0, tiled=True)]
  transfers between devices with their start and end apart: 4 -> 3, of which waited for: 4 -> 3; matrix products, arithmetic and copies ran while one was open for 1% -> 1% of each run, Pallas kernels for 9% -> 8%
where the time goes in v4:
time: 187 us; the launch traced here: 186 us
  blocking collectives  85.8 us (46%)
  waiting for transfers between devices  41 us (22%)
  Pallas kernels  32.7 us (17%)
  starting transfers between devices  24 us (13%)
    all_to_all x3, blocking collectives, exchange(): return lax.all_to_all(pay, 'seq', split_axis=0, concat_axis=0, tiled=True)  69 us
    all_to_all x3, waiting for transfers between devices, exchange(): return lax.all_to_all(pay, 'seq', split_axis=0, concat_axis=0, tiled=True)  41 us
    pallas_call x10, Pallas kernels, kernel(): pl.pallas_call(wrapped, out_shape=[pltpu.HBM(shape.shape, shape.dtype) if...  24.4 us
    all_to_all x3, starting transfers between devices, exchange(): return lax.all_to_all(pay, 'seq', split_axis=0, concat_axis=0, tiled=True)  24 us
    all_to_all x1, blocking collectives, shards(): lax.all_to_all(stats, 'head', split_axis=0, concat_axis=0, tiled=True)  16.8 us
    pallas_call x2, Pallas kernels, whole_kernel(): pl.pallas_call(body, out_shape=shapes, scratch_shapes=[pltpu.VMEM((1, TOK...  8.3 us
  transfers between devices with their start and end apart: 3, of which 3 were waited for; matrix products, arithmetic and copies ran while one was open for 1% of the time, Pallas kernels for 8%

profile of v4, /device:TPU:1, one launch (start us, length us, event | category | flops | bytes accessed | tf_op | source)
XLA Modules:
  0.0 185.8 jit_solution(7582362422649136096)
XLA Ops:
  0.6 3.0 %open_raster.1 = bf16[512,1152]{1,0:T(8,128)(2,1)} custom-call(bf16[512,384]{1,0:T(8,128)(2,1)} %refs_2_.3, bf16[512,128]{1,0:T(8,128)(2,1)} %refs_1_.7, bf16[512,128]{1,0:T(8,128)(2,1)} %refs_4_.5, bf16[6,512]{1,0:T(8,128)(2,1)} %refs_3_.13, bf16[6,512]{1,0:T(8,128)(2,1)} %refs_3_.12, bf16[512,384]{1,0:T(8,128)(2,1)} %refs_4_.4, s32[1,64]{1,0:T(1,128)} %bitcast.36), custom_call_target="tpu_custom_call" | custom-call | flops 400000000 | bytes 2240768 | tf_op jit(solution)/shard_map/open_raster/pallas_call | solution.py:494
  3.6 0.0 copy-start.6
  3.6 0.0 copy-start.7
  3.6 11.6 %all-to-all-start = ((bf16[64,8,1152]{2,1,0:T(8,128)(2,1)}), bf16[64,8,1152]{2,1,0:T(8,128)(2,1)S(1)}, u32[]{:S(2)}, u32[]{:S(2)}) async-start(bf16[64,8,1152]{2,1,0:T(8,128)(2,1)} %bitcast.28), calls=%async_computation | async-start | bytes 2359296 | tf_op jit(solution)/shard_map/all_to_all | solution.py:510
  15.3 0.0 copy-done.6
  15.3 0.6 reshape.29.gain.refs_7_.refs_5_.refs_6_
  15.9 0.0 copy-done.7
  15.9 0.1 broadcast_in_dim.3
  15.9 0.7 reshape_reshape.3.skip.refs_6_.refs_5_
  16.6 0.0 copy-start.1
  16.6 3.6 %inner_raster.1 = (bf16[2,6,256,256]{3,2,1,0:T(8,128)(2,1)}, bf16[512,384]{1,0:T(8,128)(2,1)}) custom-call(bf16[512,384]{1,0:T(8,128)(2,1)} %refs_2_.3, bf16[512,128]{1,0:T(8,128)(2,1)} %refs_1_.7, bf16[512,128]{1,0:T(8,128)(2,1)} %refs_4_.5, bf16[6,512]{1,0:T(8,128)(2,1)} %refs_3_.13, f32[1,384]{1,0:T(1,128)} %reshape_reshape.3.skip.refs_6_.refs_5_, ...), custom_call_target="tpu_custom_call" | custom-call | flops 8000000000 | bytes 2630656 | tf_op jit(solution)/shard_map/inner_raster/pallas_call | solution.py:438
  20.3 25.6 %all-to-all-done = bf16[64,8,1152]{2,1,0:T(8,128)(2,1)S(1)} async-done(((bf16[64,8,1152]{2,1,0:T(8,128)(2,1)}), bf16[64,8,1152]{2,1,0:T(8,128)(2,1)S(1)}, u32[]{:S(2)}, u32[]{:S(2)}) %all-to-all-start) | async-done | bytes 1179680 | tf_op jit(solution)/shard_map/all_to_all | solution.py:510
  45.9 0.0 copy-start
  45.9 0.0 copy-done.1
  45.9 2.2 %open_scan.1 = (bf16[512,384]{1,0:T(8,128)(2,1)}, bf16[512,128]{1,0:T(8,128)(2,1)}, bf16[512,256]{1,0:T(8,128)(2,1)}) custom-call(bf16[512,1152]{1,0:T(8,128)(2,1)S(1)} %bitcast.19, bf16[6,512]{1,0:T(8,128)(2,1)S(1)} %copy-done.1, s32[1,64]{1,0:T(1,128)} %bitcast.31), custom_call_target="tpu_custom_call" | custom-call | flops 400000000 | bytes 1972480 | tf_op jit(solution)/shard_map/open_scan/pallas_call | solution.py:494
  48.1 6.6 %all-to-all-start.1 = ((bf16[64,8,256]{2,1,0:T(8,128)(2,1)}), bf16[64,8,256]{2,1,0:T(8,128)(2,1)S(1)}, u32[]{:S(2)}, u32[]{:S(2)}) async-start(bf16[64,8,256]{2,1,0:T(8,128)(2,1)} %bitcast.30), calls=%async_computation.1 | async-start | bytes 524288 | tf_op jit(solution)/shard_map/all_to_all | solution.py:510
  54.7 0.0 copy-done
  54.7 0.0 copy-start.3
  54.7 4.7 %inner_scan.1 = (bf16[512,128]{1,0:T(8,128)(2,1)}, bf16[512,384]{1,0:T(8,128)(2,1)}, bf16[2,6,256,256]{3,2,1,0:T(8,128)(2,1)}, bf16[512,384]{1,0:T(8,128)(2,1)}, f32[64,128]{1,0:T(8,128)}, /*index=5*/f32[64,128]{1,0:T(8,128)}) custom-call(bf16[512,1152]{1,0:T(8,128)(2,1)} %bitcast.20, bf16[512,384]{1,0:T(8,128)(2,1)} %get-tuple-element.25.x.refs_4_, ...), custom_call_target="tpu_custom_call" | custom-call | flops 8000000000 | bytes 4266240 | tf_op jit(solution)/shard_map/inner_scan/pallas_call | solution.py:438
  59.4 0.0 copy-start.2
  59.4 0.0 copy-start.4
  59.4 0.0 copy-start.5
  59.4 8.5 %all-to-all-done.1 = bf16[64,8,256]{2,1,0:T(8,128)(2,1)S(1)} async-done(((bf16[64,8,256]{2,1,0:T(8,128)(2,1)}), bf16[64,8,256]{2,1,0:T(8,128)(2,1)S(1)}, u32[]{:S(2)}, u32[]{:S(2)}) %all-to-all-start.1) | async-done | bytes 262176 | tf_op jit(solution)/shard_map/all_to_all | solution.py:510
  67.9 0.0 copy-done.3
  67.9 2.4 %finish_raster.1 = (bf16[512,384]{1,0:T(8,128)(2,1)}, bf16[512,512]{1,0:T(8,128)(2,1)S(1)}) custom-call(bf16[512,256]{1,0:T(8,128)(2,1)S(1)} %bitcast.25, bf16[512,128]{1,0:T(8,128)(2,1)} %refs_4_.5, bf16[512,384]{1,0:T(8,128)(2,1)} %get-tuple-element.24.refs_2_, bf16[6,512]{1,0:T(8,128)(2,1)S(1)} %copy-done.3, f32[64,128]{1,0:T(8,128)} %get-tuple-element.27.refs_4_.refs_8_, ...), custom_call_target="tpu_custom_call" | custom-call | flops 400000000 | bytes 1743104 | tf_op jit(solution)/shard_map/finish_raster/pallas_call | solution.py:494
  70.3 22.2 %all_to_all.77 = bf16[64,8,512]{2,1,0:T(8,128)(2,1)S(1)} all-to-all(bf16[64,8,512]{2,1,0:T(8,128)(2,1)S(1)} %bitcast.23), channel_id=1, replica_groups=mesh['seq'=64,'head'=8] {'seq'}, dimensions={0} | all-to-all | bytes 1048576 | tf_op jit(solution)/shard_map/all_to_all | solution.py:510
  92.5 0.0 copy-done.2
  92.5 0.0 copy-done.4
  92.5 0.0 copy-done.5
  92.5 1.9 %finish_scan.1 = (bf16[512,384]{1,0:T(8,128)(2,1)S(1)}, f32[512,384]{1,0:T(8,128)S(1)}, f32[64,128]{1,0:T(8,128)S(1)}) custom-call(bf16[512,512]{1,0:T(8,128)(2,1)S(1)} %bitcast.17, bf16[512,128]{1,0:T(8,128)(2,1)} %get-tuple-element.29.refs_1_.refs_3_.refs_4_, bf16[512,384]{1,0:T(8,128)(2,1)} %get-tuple-element.30.refs_2_, bf16[6,512]{1,0:T(8,128)(2,1)S(1)} %copy-done.2, ...), custom_call_target="tpu_custom_call" | custom-call | flops 400000000 | bytes 3056896 | tf_op jit(solution)/shard_map/finish_scan/pallas_call | solution.py:494
  94.4 16.8 %all_to_all.78 = f32[8,8,128]{2,1,0:T(8,128)S(1)} all-to-all(f32[8,8,128]{2,1,0:T(8,128)S(1)} %bitcast.27), channel_id=1, replica_groups=mesh['seq'=64,'head'=8] {'head'}, dimensions={0} | all-to-all | bytes 65536 | tf_op jit(solution)/shard_map/all_to_all | solution.py:565
  111.2 2.1 %open_back.1 = (bf16[512,384]{1,0:T(8,128)(2,1)}, bf16[512,512]{1,0:T(8,128)(2,1)S(1)}) custom-call(f32[64,128]{1,0:T(8,128)S(1)} %bitcast.26, f32[512,384]{1,0:T(8,128)S(1)} %get-tuple-element.33.refs_1_, bf16[512,384]{1,0:T(8,128)(2,1)S(1)} %get-tuple-element.34.refs_2_, bf16[512,128]{1,0:T(8,128)(2,1)} %get-tuple-element.29.refs_1_.refs_3_.refs_4_, ...), custom_call_target="tpu_custom_call" | custom-call | flops 400000000 | bytes 2662144 | tf_op jit(solution)/shard_map/open_back/pallas_call | solution.py:494
  113.3 24.6 %all_to_all.79 = bf16[64,8,512]{2,1,0:T(8,128)(2,1)S(1)} all-to-all(bf16[64,8,512]{2,1,0:T(8,128)(2,1)S(1)} %bitcast.22), channel_id=1, replica_groups=mesh['seq'=64,'head'=8] {'seq'}, dimensions={0} | all-to-all | bytes 1048576 | tf_op jit(solution)/shard_map/all_to_all | solution.py:510
  137.9 2.9 %middle_raster.1 = (bf16[512,384]{1,0:T(8,128)(2,1)}, bf16[512,384]{1,0:T(8,128)(2,1)}, bf16[512,256]{1,0:T(8,128)(2,1)}) custom-call(bf16[512,512]{1,0:T(8,128)(2,1)S(1)} %bitcast.16, bf16[512,384]{1,0:T(8,128)(2,1)} %get-tuple-element.36.refs_1_, bf16[512,384]{1,0:T(8,128)(2,1)} %refs_2_.3, bf16[512,128]{1,0:T(8,128)(2,1)} %refs_4_.5, ...), custom_call_target="tpu_custom_call" | custom-call | flops 400000000 | bytes 2925824 | tf_op jit(solution)/shard_map/middle_raster/pallas_call | solution.py:494
  140.8 5.7 %all-to-all-start.5 = ((bf16[64,8,256]{2,1,0:T(8,128)(2,1)}), bf16[64,8,256]{2,1,0:T(8,128)(2,1)S(1)}, u32[]{:S(2)}, u32[]{:S(2)}) async-start(bf16[64,8,256]{2,1,0:T(8,128)(2,1)} %bitcast.29), calls=%async_computation.5 | async-start | bytes 524288 | tf_op jit(solution)/shard_map/all_to_all | solution.py:510
  146.5 3.0 %inner_back_scan.1.refs_2_ = bf16[512,384]{1,0:T(8,128)(2,1)} custom-call(bf16[6,512]{1,0:T(8,128)(2,1)S(1)} %copy-done.2, bf16[2,6,256,256]{3,2,1,0:T(8,128)(2,1)} %get-tuple-element.39.refs_1_, bf16[512,384]{1,0:T(8,128)(2,1)} %get-tuple-element.40.refs_2_, bf16[512,128]{1,0:T(8,128)(2,1)} %get-tuple-element.26.in_map.refs_3_.refs_1_, ...), custom_call_target="tpu_custom_call" | custom-call | flops 4000000000 | bytes 2627584 | tf_op jit(solution)/shard_map/inner_back_scan/pallas_call | solution.py:494
  149.6 3.2 %inner_back_raster.1.refs_6_.refs_2_ = bf16[512,384]{1,0:T(8,128)(2,1)} custom-call(bf16[6,512]{1,0:T(8,128)(2,1)S(1)} %copy-done.3, bf16[2,6,256,256]{3,2,1,0:T(8,128)(2,1)} %get-tuple-element.42.refs_1_, bf16[512,384]{1,0:T(8,128)(2,1)} %get-tuple-element.43.refs_2_, bf16[512,128]{1,0:T(8,128)(2,1)} %refs_1_.7, bf16[512,128]{1,0:T(8,128)(2,1)} %refs_4_.5, ...), custom_call_target="tpu_custom_call" | custom-call | flops 4000000000 | bytes 2629120 | tf_op jit(solution)/shard_map/inner_back_raster/pallas_call | solution.py:494
  152.8 6.9 %all-to-all-done.5 = bf16[64,8,256]{2,1,0:T(8,128)(2,1)S(1)} async-done(((bf16[64,8,256]{2,1,0:T(8,128)(2,1)}), bf16[64,8,256]{2,1,0:T(8,128)(2,1)S(1)}, u32[]{:S(2)}, u32[]{:S(2)}) %all-to-all-start.5) | async-done | bytes 262176 | tf_op jit(solution)/shard_map/all_to_all | solution.py:510
  159.7 1.6 finish_back_scan.1
  161.3 22.2 %all_to_all.80 = bf16[64,8,512]{2,1,0:T(8,128)(2,1)S(1)} all-to-all(bf16[64,8,512]{2,1,0:T(8,128)(2,1)S(1)} %bitcast.18), channel_id=1, replica_groups=mesh['seq'=64,'head'=8] {'seq'}, dimensions={0} | all-to-all | bytes 1048576 | tf_op jit(solution)/shard_map/all_to_all | solution.py:510
  183.6 2.1 %finish_back_raster.1 = bf16[512,384]{1,0:T(8,128)(2,1)} custom-call(bf16[512,512]{1,0:T(8,128)(2,1)S(1)} %bitcast.24, bf16[512,128]{1,0:T(8,128)(2,1)} %refs_1_.7, bf16[512,384]{1,0:T(8,128)(2,1)} %inner_back_raster.1.refs_6_.refs_2_, bf16[6,512]{1,0:T(8,128)(2,1)S(1)} %copy-done.3, s32[1,64]{1,0:T(1,128)} %bitcast.39), custom_call_target="tpu_custom_call" | custom-call | flops 400000000 | bytes 1448192 | tf_op jit(solution)/shard_map/finish_back_raster/pallas_call | solution.py:494
Async XLA Ops:
  3.6 11.7 %copy-start.6 = (f32[384]{0:T(512)S(1)}, f32[384]{0:T(512)}, u32[]{:S(2)}) copy-start(f32[384]{0:T(512)} %param.16) | copy-start | bytes 4612
  3.6 12.3 %copy-start.7 = (f32[6]{0:T(128)S(1)}, f32[6]{0:T(128)}, u32[]{:S(2)}) copy-start(f32[6]{0:T(128)} %param.15) | copy-start | bytes 76
  3.6 42.2 %all-to-all-start = ((bf16[64,8,1152]{2,1,0:T(8,128)(2,1)}), bf16[64,8,1152]{2,1,0:T(8,128)(2,1)S(1)}, u32[]{:S(2)}, u32[]{:S(2)}) async-start(bf16[64,8,1152]{2,1,0:T(8,128)(2,1)} %bitcast.28), calls=%async_computation | async-start | bytes 2359296 | tf_op jit(solution)/shard_map/all_to_all | solution.py:510
  16.6 29.3 %copy-start.1 = (bf16[6,512]{1,0:T(8,128)(2,1)S(1)}, bf16[6,512]{1,0:T(8,128)(2,1)}, u32[]{:S(2)}) copy-start(bf16[6,512]{1,0:T(8,128)(2,1)} %refs_3_.12) | copy-start | bytes 18436
  45.9 8.9 %copy-start = (bf16[64,8,1152]{2,1,0:T(8,128)(2,1)}, bf16[64,8,1152]{2,1,0:T(8,128)(2,1)S(1)}, u32[]{:S(2)}) copy-start(bf16[64,8,1152]{2,1,0:T(8,128)(2,1)S(1)} %all-to-all-done) | copy-start | bytes 3538948
  48.1 19.8 %all-to-all-start.1 = ((bf16[64,8,256]{2,1,0:T(8,128)(2,1)}), bf16[64,8,256]{2,1,0:T(8,128)(2,1)S(1)}, u32[]{:S(2)}, u32[]{:S(2)}) async-start(bf16[64,8,256]{2,1,0:T(8,128)(2,1)} %bitcast.30), calls=%async_computation.1 | async-start | bytes 524288 | tf_op jit(solution)/shard_map/all_to_all | solution.py:510
  54.7 13.2 %copy-start.3 = (bf16[6,512]{1,0:T(8,128)(2,1)S(1)}, bf16[6,512]{1,0:T(8,128)(2,1)}, u32[]{:S(2)}) copy-start(bf16[6,512]{1,0:T(8,128)(2,1)} %refs_3_.13) | copy-start | bytes 18436
  59.4 33.1 %copy-start.2 = (bf16[6,512]{1,0:T(8,128)(2,1)S(1)}, bf16[6,512]{1,0:T(8,128)(2,1)}, u32[]{:S(2)}) copy-start(bf16[6,512]{1,0:T(8,128)(2,1)} %refs_3_.12) | copy-start | bytes 18436
  59.4 33.1 %copy-start.4 = (f32[1,384]{1,0:T(1,128)S(1)}, f32[1,384]{1,0:T(1,128)}, u32[]{:S(2)}) copy-start(f32[1,384]{1,0:T(1,128)} %reshape.29.gain.refs_7_.refs_5_.refs_6_) | copy-start | bytes 4612
  59.4 33.1 %copy-start.5 = (f32[1,384]{1,0:T(1,128)S(1)}, f32[1,384]{1,0:T(1,128)}, u32[]{:S(2)}) copy-start(f32[1,384]{1,0:T(1,128)} %reshape_reshape.3.skip.refs_6_.refs_5_) | copy-start | bytes 4612
  140.8 18.9 %all-to-all-start.5 = ((bf16[64,8,256]{2,1,0:T(8,128)(2,1)}), bf16[64,8,256]{2,1,0:T(8,128)(2,1)S(1)}, u32[]{:S(2)}, u32[]{:S(2)}) async-start(bf16[64,8,256]{2,1,0:T(8,128)(2,1)} %bitcast.29), calls=%async_computation.5 | async-start | bytes 524288 | tf_op jit(solution)/shard_map/all_to_all | solution.py:510

commit v5 on v4

--- a/solution.py
+++ b/solution.py
@@ -265,28 +265,26 @@
         links[...] = link_decays(slices, lane, work)
 
 
-def finish_raster(got, out_map, local, decay_f, links, route, y, pay, stage):
+def finish_raster(got, out_map, local, decay_f, links, route, pay, stage):
     running = running_of(decay_f)
     entering = join_state(got[:, 0:128])
     pay[:, 384:512] = carry(links, got[:, 128:256], False).astype(BF16)
     for rows in BANDS:
         value = local[rows, :].astype(F32) + jnp.exp(running[rows]) * dot(out_map[rows, :], entering)
-        y[rows, :] = value.astype(BF16)
         put_band(stage, route, rows, value)
-    y.send()
     pay[:, 0:384] = sent(stage, 3).astype(BF16)
 
 
 def finish_scan(
-    got, out_map, local, decay_r, x, grad, skip, gain, route, y, combined, stats, stage
+    got, out_map, local, decay_r, x, grad, skip, gain, route, combined, stats, stage
 ):
     entering = join_state(got[:, 384:512])
     running = running_of(decay_r)
     weight = jnp.exp(running[TOK - 1 : TOK, :] - running)
     fill(stage, got[:, 0:384])
     y_forward = own_band(stage, route, ALL, 3)
-    y[...] = (local[...].astype(F32) + weight * dot(out_map[...], entering)).astype(BF16)
-    total = y_forward + y[...].astype(F32) + skip[...] * x[...].astype(F32)
+    y_reverse = (local[...].astype(F32) + weight * dot(out_map[...], entering)).astype(BF16)
+    total = y_forward + y_reverse.astype(F32) + skip[...] * x[...].astype(F32)
     combined[...] = total
     scaled = gain[...] * grad[...].astype(F32)
     squares, inner = token_sums(total * total), token_sums(total * scaled)
@@ -309,7 +307,7 @@
     return (scale * scaled - combined * pull).astype(BF16)
 
 
-def open_back(stats, combined, y, out_map, grad, gain, decay_r, route, back, pay, stage):
+def open_back(stats, combined, out_map, grad, gain, decay_r, route, back, pay, stage):
     running = running_of(decay_r)
     tile = jnp.sum(stats[...].reshape(8, 8, LANES), axis=0)
     squares = jnp.concatenate([tile[k : k + 1] for k in range(4)], axis=1)
@@ -323,7 +321,7 @@
     lanes = indicator(iota((16, LANES), 1) == CUT + iota((16, LANES), 0))
     wide = dot(parts, both, 0, 0)
     put_band(stage, route, ALL, dot(parts, lanes, 0, 0), 3)
-    put_band(stage, route, ALL, y[...].astype(F32))
+    put_band(stage, route, ALL, combined[...])
     pay[:, 0:384] = sent(stage, 3).astype(BF16)
     scaled = gain[...] * grad[...].astype(F32)
     back[...] = gradient(combined[...], scaled, wide[:, 0:WIDTH], wide[:, WIDTH:])
@@ -337,7 +335,7 @@
 
 
 def middle_raster(
-    got, y_forward, x, out_map, grad, skip, gain, decay_f, links, route, normed, back, pay, stage
+    got, out_map, grad, gain, decay_f, links, route, normed, back, pay, stage
 ):
     running = running_of(decay_f)
     fill(stage, got[...])
@@ -351,8 +349,7 @@
         moved = own_band(stage, route, rows, 4)
         wide = dot(moved[:, 384:512].astype(BF16), both)
         scale = wide[:, 0:WIDTH]
-        total = y_forward[rows, :].astype(F32) + moved[:, 0:384]
-        total += skip[...] * x[rows, :].astype(F32)
+        total = moved[:, 0:384]
         normed[rows, :] = (total * scale * gain[...]).astype(BF16)
         scaled = gain[...] * grad[rows, :].astype(F32)
         back[rows, :] = gradient(total, scaled, scale, wide[:, WIDTH:])
@@ -553,19 +550,19 @@
         inner_scan, [rows16, wide16, inner16, wide16, links32, links32],
         got1, x_scan, in_scan, decay_reverse, to_raster, flops=8_000_000_000, work=True,
     )
-    y_forward, pay3 = kernel(
-        finish_raster, [wide16, pay(512, 0)],
+    (pay3,) = kernel(
+        finish_raster, [pay(512, 0)],
         got2, output_map, local_f, decay_forward, links_r, to_scan, arrived=1, stage=384,
     )
     got3 = exchange(pay3)
-    y_scan, combined, stats = kernel(
-        finish_scan, [(*wide16, 0), (*wide32, 0), ((64, LANES), F32, 0)],
+    combined, stats = kernel(
+        finish_scan, [(*wide32, 0), ((64, LANES), F32, 0)],
         got3, out_scan, local_r, decay_reverse, x_scan, grad_scan, skip, gain, to_raster, arrived=1, stage=384,
     )
     all_stats = lax.all_to_all(stats, "head", split_axis=0, concat_axis=0, tiled=True)
     back_scan, pay4 = kernel(
         open_back, [wide16, pay(512, 0)],
-        all_stats, combined, y_scan, out_scan, grad_scan, gain, decay_reverse, to_raster, arrived=3, stage=512,
+        all_stats, combined, out_scan, grad_scan, gain, decay_reverse, to_raster, arrived=2, stage=512,
     )
     got4 = exchange(pay4)
     (local_br,) = kernel(
@@ -574,7 +571,7 @@
     )
     normed, back, pay5 = kernel(
         middle_raster, [wide16, wide16, pay(256)],
-        got4, y_forward, ssm_input, output_map, grad_normed, skip, gain, decay_forward, links_r,
+        got4, output_map, grad_normed, gain, decay_forward, links_r,
         to_scan, arrived=1, stage=512,
     )
     got5 = exchange(pay5)

time: 187 us -> 186 us (level)
  no operation moved by 1% of the time
where the time goes in v5:
time: 186 us; the launch traced here: 185 us
  blocking collectives  85.8 us (46%)
  waiting for transfers between devices  41 us (22%)
  Pallas kernels  32.1 us (17%)
  starting transfers between devices  24 us (13%)
    all_to_all x3, blocking collectives, exchange(): return lax.all_to_all(pay, 'seq', split_axis=0, concat_axis=0, tiled=True)  69 us
    all_to_all x3, waiting for transfers between devices, exchange(): return lax.all_to_all(pay, 'seq', split_axis=0, concat_axis=0, tiled=True)  41 us
    all_to_all x3, starting transfers between devices, exchange(): return lax.all_to_all(pay, 'seq', split_axis=0, concat_axis=0, tiled=True)  24 us
    pallas_call x10, Pallas kernels, kernel(): pl.pallas_call(wrapped, out_shape=[pltpu.HBM(shape.shape, shape.dtype) if...  23.8 us
    all_to_all x1, blocking collectives, shards(): lax.all_to_all(stats, 'head', split_axis=0, concat_axis=0, tiled=True)  16.8 us
    pallas_call x2, Pallas kernels, whole_kernel(): pl.pallas_call(body, out_shape=shapes, scratch_shapes=[pltpu.VMEM((1, TOK...  8.3 us
  transfers between devices with their start and end apart: 3, of which 3 were waited for; matrix products, arithmetic and copies ran while one was open for 1% of the time, Pallas kernels for 8%

profile of v5, /device:TPU:1, one launch (start us, length us, event | category | flops | bytes accessed | tf_op | source)
XLA Modules:
  0.0 185.2 jit_solution(7913975960278128540)
XLA Ops:
  0.6 3.0 %open_raster.1 = bf16[512,1152]{1,0:T(8,128)(2,1)} custom-call(bf16[512,384]{1,0:T(8,128)(2,1)} %x.1, bf16[512,128]{1,0:T(8,128)(2,1)} %refs_1_.9, bf16[512,128]{1,0:T(8,128)(2,1)} %refs_4_.5, bf16[6,512]{1,0:T(8,128)(2,1)} %refs_3_.11, bf16[6,512]{1,0:T(8,128)(2,1)} %refs_3_.10, bf16[512,384]{1,0:T(8,128)(2,1)} %refs_2_.3, s32[1,64]{1,0:T(1,128)} %bitcast.36), custom_call_target="tpu_custom_call" | custom-call | flops 400000000 | bytes 2240768 | tf_op jit(solution)/shard_map/open_raster/pallas_call | solution.py:491
  3.6 0.0 copy-start.6
  3.6 0.0 copy-start.7
  3.6 11.6 %all-to-all-start = ((bf16[64,8,1152]{2,1,0:T(8,128)(2,1)}), bf16[64,8,1152]{2,1,0:T(8,128)(2,1)S(1)}, u32[]{:S(2)}, u32[]{:S(2)}) async-start(bf16[64,8,1152]{2,1,0:T(8,128)(2,1)} %bitcast.28), calls=%async_computation | async-start | bytes 2359296 | tf_op jit(solution)/shard_map/all_to_all | solution.py:507
  15.3 0.0 copy-done.6
  15.3 0.6 reshape.29.gain.refs_7_.refs_4_.refs_3_
  15.9 0.0 copy-done.7
  15.9 0.1 broadcast_in_dim.3
  15.9 0.6 reshape_reshape.3.skip.refs_6_.refs_5_
  16.6 0.0 copy-start.1
  16.6 3.6 %inner_raster.1 = (bf16[2,6,256,256]{3,2,1,0:T(8,128)(2,1)}, bf16[512,384]{1,0:T(8,128)(2,1)}) custom-call(bf16[512,384]{1,0:T(8,128)(2,1)} %x.1, bf16[512,128]{1,0:T(8,128)(2,1)} %refs_1_.9, bf16[512,128]{1,0:T(8,128)(2,1)} %refs_4_.5, bf16[6,512]{1,0:T(8,128)(2,1)} %refs_3_.11, f32[1,384]{1,0:T(1,128)} %reshape_reshape.3.skip.refs_6_.refs_5_, ...), custom_call_target="tpu_custom_call" | custom-call | flops 8000000000 | bytes 2630656 | tf_op jit(solution)/shard_map/inner_raster/pallas_call | solution.py:435
  20.2 25.7 %all-to-all-done = bf16[64,8,1152]{2,1,0:T(8,128)(2,1)S(1)} async-done(((bf16[64,8,1152]{2,1,0:T(8,128)(2,1)}), bf16[64,8,1152]{2,1,0:T(8,128)(2,1)S(1)}, u32[]{:S(2)}, u32[]{:S(2)}) %all-to-all-start) | async-done | bytes 1179680 | tf_op jit(solution)/shard_map/all_to_all | solution.py:507
  45.9 0.0 copy-start
  45.9 0.0 copy-done.1
  45.9 2.2 %open_scan.1 = (bf16[512,384]{1,0:T(8,128)(2,1)}, bf16[512,128]{1,0:T(8,128)(2,1)}, bf16[512,256]{1,0:T(8,128)(2,1)}) custom-call(bf16[512,1152]{1,0:T(8,128)(2,1)S(1)} %bitcast.18, bf16[6,512]{1,0:T(8,128)(2,1)S(1)} %copy-done.1, s32[1,64]{1,0:T(1,128)} %bitcast.31), custom_call_target="tpu_custom_call" | custom-call | flops 400000000 | bytes 1972480 | tf_op jit(solution)/shard_map/open_scan/pallas_call | solution.py:491
  48.1 6.6 %all-to-all-start.1 = ((bf16[64,8,256]{2,1,0:T(8,128)(2,1)}), bf16[64,8,256]{2,1,0:T(8,128)(2,1)S(1)}, u32[]{:S(2)}, u32[]{:S(2)}) async-start(bf16[64,8,256]{2,1,0:T(8,128)(2,1)} %bitcast.30), calls=%async_computation.1 | async-start | bytes 524288 | tf_op jit(solution)/shard_map/all_to_all | solution.py:507
  54.7 0.0 copy-done
  54.7 0.0 copy-start.3
  54.8 4.7 %inner_scan.1 = (bf16[512,128]{1,0:T(8,128)(2,1)}, bf16[512,384]{1,0:T(8,128)(2,1)}, bf16[2,6,256,256]{3,2,1,0:T(8,128)(2,1)}, bf16[512,384]{1,0:T(8,128)(2,1)}, f32[64,128]{1,0:T(8,128)}, /*index=5*/f32[64,128]{1,0:T(8,128)}) custom-call(bf16[512,1152]{1,0:T(8,128)(2,1)} %bitcast.19, bf16[512,384]{1,0:T(8,128)(2,1)} %get-tuple-element.22.x.refs_4_, ...), custom_call_target="tpu_custom_call" | custom-call | flops 8000000000 | bytes 4266240 | tf_op jit(solution)/shard_map/inner_scan/pallas_call | solution.py:435
  59.4 0.0 copy-start.2
  59.4 0.0 copy-start.4
  59.4 0.0 copy-start.5
  59.4 8.5 %all-to-all-done.1 = bf16[64,8,256]{2,1,0:T(8,128)(2,1)S(1)} async-done(((bf16[64,8,256]{2,1,0:T(8,128)(2,1)}), bf16[64,8,256]{2,1,0:T(8,128)(2,1)S(1)}, u32[]{:S(2)}, u32[]{:S(2)}) %all-to-all-start.1) | async-done | bytes 262176 | tf_op jit(solution)/shard_map/all_to_all | solution.py:507
  67.9 0.0 copy-done.3
  67.9 1.6 finish_raster.1
  69.6 22.2 %all_to_all.77 = bf16[64,8,512]{2,1,0:T(8,128)(2,1)S(1)} all-to-all(bf16[64,8,512]{2,1,0:T(8,128)(2,1)S(1)} %bitcast.23), channel_id=1, replica_groups=mesh['seq'=64,'head'=8] {'seq'}, dimensions={0} | all-to-all | bytes 1048576 | tf_op jit(solution)/shard_map/all_to_all | solution.py:507
  91.8 0.0 copy-done.2
  91.8 0.0 copy-done.4
  91.8 0.0 copy-done.5
  91.8 2.3 %finish_scan.1 = (f32[512,384]{1,0:T(8,128)S(1)}, f32[64,128]{1,0:T(8,128)S(1)}) custom-call(bf16[512,512]{1,0:T(8,128)(2,1)S(1)} %bitcast.16, bf16[512,128]{1,0:T(8,128)(2,1)} %get-tuple-element.25.refs_1_.refs_2_.refs_4_, bf16[512,384]{1,0:T(8,128)(2,1)} %get-tuple-element.26.refs_2_, bf16[6,512]{1,0:T(8,128)(2,1)S(1)} %copy-done.2, ...), custom_call_target="tpu_custom_call" | custom-call | flops 400000000 | bytes 2663680 | tf_op jit(solution)/shard_map/finish_scan/pallas_call | solution.py:491
  94.1 16.8 %all_to_all.78 = f32[8,8,128]{2,1,0:T(8,128)S(1)} all-to-all(f32[8,8,128]{2,1,0:T(8,128)S(1)} %bitcast.27), channel_id=1, replica_groups=mesh['seq'=64,'head'=8] {'head'}, dimensions={0} | all-to-all | bytes 65536 | tf_op jit(solution)/shard_map/all_to_all | solution.py:562
  110.8 2.1 %open_back.1 = (bf16[512,384]{1,0:T(8,128)(2,1)}, bf16[512,512]{1,0:T(8,128)(2,1)S(1)}) custom-call(f32[64,128]{1,0:T(8,128)S(1)} %bitcast.26, f32[512,384]{1,0:T(8,128)S(1)} %get-tuple-element.29.refs_1_, bf16[512,128]{1,0:T(8,128)(2,1)} %get-tuple-element.25.refs_1_.refs_2_.refs_4_, bf16[512,384]{1,0:T(8,128)(2,1)} %get-tuple-element.27.refs_5_.refs_3_, ...), custom_call_target="tpu_custom_call" | custom-call | flops 400000000 | bytes 2268928 | tf_op jit(solution)/shard_map/open_back/pallas_call | solution.py:491
  112.9 24.6 %all_to_all.79 = bf16[64,8,512]{2,1,0:T(8,128)(2,1)S(1)} all-to-all(bf16[64,8,512]{2,1,0:T(8,128)(2,1)S(1)} %bitcast.22), channel_id=1, replica_groups=mesh['seq'=64,'head'=8] {'seq'}, dimensions={0} | all-to-all | bytes 1048576 | tf_op jit(solution)/shard_map/all_to_all | solution.py:507
  137.5 2.6 %middle_raster.1 = (bf16[512,384]{1,0:T(8,128)(2,1)}, bf16[512,384]{1,0:T(8,128)(2,1)}, bf16[512,256]{1,0:T(8,128)(2,1)}) custom-call(bf16[512,512]{1,0:T(8,128)(2,1)S(1)} %bitcast.21, bf16[512,128]{1,0:T(8,128)(2,1)} %refs_4_.5, bf16[512,384]{1,0:T(8,128)(2,1)} %refs_2_.3, f32[1,384]{1,0:T(1,128)S(1)} %copy-done.4, bf16[6,512]{1,0:T(8,128)(2,1)S(1)} %copy-done.3, ...), custom_call_target="tpu_custom_call" | custom-call | flops 400000000 | bytes 2137856 | tf_op jit(solution)/shard_map/middle_raster/pallas_call | solution.py:491
  140.1 5.7 %all-to-all-start.5 = ((bf16[64,8,256]{2,1,0:T(8,128)(2,1)}), bf16[64,8,256]{2,1,0:T(8,128)(2,1)S(1)}, u32[]{:S(2)}, u32[]{:S(2)}) async-start(bf16[64,8,256]{2,1,0:T(8,128)(2,1)} %bitcast.29), calls=%async_computation.5 | async-start | bytes 524288 | tf_op jit(solution)/shard_map/all_to_all | solution.py:507
  145.9 3.1 %inner_back_scan.1.refs_2_ = bf16[512,384]{1,0:T(8,128)(2,1)} custom-call(bf16[6,512]{1,0:T(8,128)(2,1)S(1)} %copy-done.2, bf16[2,6,256,256]{3,2,1,0:T(8,128)(2,1)} %get-tuple-element.33.refs_1_, bf16[512,384]{1,0:T(8,128)(2,1)} %get-tuple-element.34.refs_2_, bf16[512,128]{1,0:T(8,128)(2,1)} %get-tuple-element.23.in_map.refs_3_.refs_1_, ...), custom_call_target="tpu_custom_call" | custom-call | flops 4000000000 | bytes 2627584 | tf_op jit(solution)/shard_map/inner_back_scan/pallas_call | solution.py:491
  148.9 3.2 %inner_back_raster.1.refs_6_.refs_2_ = bf16[512,384]{1,0:T(8,128)(2,1)} custom-call(bf16[6,512]{1,0:T(8,128)(2,1)S(1)} %copy-done.3, bf16[2,6,256,256]{3,2,1,0:T(8,128)(2,1)} %get-tuple-element.36.refs_1_, bf16[512,384]{1,0:T(8,128)(2,1)} %get-tuple-element.37.refs_2_, bf16[512,128]{1,0:T(8,128)(2,1)} %refs_1_.9, bf16[512,128]{1,0:T(8,128)(2,1)} %refs_4_.5, ...), custom_call_target="tpu_custom_call" | custom-call | flops 4000000000 | bytes 2629120 | tf_op jit(solution)/shard_map/inner_back_raster/pallas_call | solution.py:491
  152.2 6.9 %all-to-all-done.5 = bf16[64,8,256]{2,1,0:T(8,128)(2,1)S(1)} async-done(((bf16[64,8,256]{2,1,0:T(8,128)(2,1)}), bf16[64,8,256]{2,1,0:T(8,128)(2,1)S(1)}, u32[]{:S(2)}, u32[]{:S(2)}) %all-to-all-start.5) | async-done | bytes 262176 | tf_op jit(solution)/shard_map/all_to_all | solution.py:507
  159.0 1.6 finish_back_scan.1
  160.7 22.2 %all_to_all.80 = bf16[64,8,512]{2,1,0:T(8,128)(2,1)S(1)} all-to-all(bf16[64,8,512]{2,1,0:T(8,128)(2,1)S(1)} %bitcast.17), channel_id=1, replica_groups=mesh['seq'=64,'head'=8] {'seq'}, dimensions={0} | all-to-all | bytes 1048576 | tf_op jit(solution)/shard_map/all_to_all | solution.py:507
  182.9 2.1 %finish_back_raster.1 = bf16[512,384]{1,0:T(8,128)(2,1)} custom-call(bf16[512,512]{1,0:T(8,128)(2,1)S(1)} %bitcast.24, bf16[512,128]{1,0:T(8,128)(2,1)} %refs_1_.9, bf16[512,384]{1,0:T(8,128)(2,1)} %inner_back_raster.1.refs_6_.refs_2_, bf16[6,512]{1,0:T(8,128)(2,1)S(1)} %copy-done.3, s32[1,64]{1,0:T(1,128)} %bitcast.39), custom_call_target="tpu_custom_call" | custom-call | flops 400000000 | bytes 1448192 | tf_op jit(solution)/shard_map/finish_back_raster/pallas_call | solution.py:491
Async XLA Ops:
  3.6 11.7 %copy-start.6 = (f32[384]{0:T(512)S(1)}, f32[384]{0:T(512)}, u32[]{:S(2)}) copy-start(f32[384]{0:T(512)} %param.16) | copy-start | bytes 4612
  3.6 12.3 %copy-start.7 = (f32[6]{0:T(128)S(1)}, f32[6]{0:T(128)}, u32[]{:S(2)}) copy-start(f32[6]{0:T(128)} %param.15) | copy-start | bytes 76
  3.6 42.2 %all-to-all-start = ((bf16[64,8,1152]{2,1,0:T(8,128)(2,1)}), bf16[64,8,1152]{2,1,0:T(8,128)(2,1)S(1)}, u32[]{:S(2)}, u32[]{:S(2)}) async-start(bf16[64,8,1152]{2,1,0:T(8,128)(2,1)} %bitcast.28), calls=%async_computation | async-start | bytes 2359296 | tf_op jit(solution)/shard_map/all_to_all | solution.py:507
  16.6 29.3 %copy-start.1 = (bf16[6,512]{1,0:T(8,128)(2,1)S(1)}, bf16[6,512]{1,0:T(8,128)(2,1)}, u32[]{:S(2)}) copy-start(bf16[6,512]{1,0:T(8,128)(2,1)} %refs_3_.10) | copy-start | bytes 18436
  45.9 8.9 %copy-start = (bf16[64,8,1152]{2,1,0:T(8,128)(2,1)}, bf16[64,8,1152]{2,1,0:T(8,128)(2,1)S(1)}, u32[]{:S(2)}) copy-start(bf16[64,8,1152]{2,1,0:T(8,128)(2,1)S(1)} %all-to-all-done) | copy-start | bytes 3538948
  48.1 19.8 %all-to-all-start.1 = ((bf16[64,8,256]{2,1,0:T(8,128)(2,1)}), bf16[64,8,256]{2,1,0:T(8,128)(2,1)S(1)}, u32[]{:S(2)}, u32[]{:S(2)}) async-start(bf16[64,8,256]{2,1,0:T(8,128)(2,1)} %bitcast.30), calls=%async_computation.1 | async-start | bytes 524288 | tf_op jit(solution)/shard_map/all_to_all | solution.py:507
  54.7 13.2 %copy-start.3 = (bf16[6,512]{1,0:T(8,128)(2,1)S(1)}, bf16[6,512]{1,0:T(8,128)(2,1)}, u32[]{:S(2)}) copy-start(bf16[6,512]{1,0:T(8,128)(2,1)} %refs_3_.11) | copy-start | bytes 18436
  59.4 32.4 %copy-start.2 = (bf16[6,512]{1,0:T(8,128)(2,1)S(1)}, bf16[6,512]{1,0:T(8,128)(2,1)}, u32[]{:S(2)}) copy-start(bf16[6,512]{1,0:T(8,128)(2,1)} %refs_3_.10) | copy-start | bytes 18436
  59.4 32.4 %copy-start.4 = (f32[1,384]{1,0:T(1,128)S(1)}, f32[1,384]{1,0:T(1,128)}, u32[]{:S(2)}) copy-start(f32[1,384]{1,0:T(1,128)} %reshape.29.gain.refs_7_.refs_4_.refs_3_) | copy-start | bytes 4612
  59.4 32.4 %copy-start.5 = (f32[1,384]{1,0:T(1,128)S(1)}, f32[1,384]{1,0:T(1,128)}, u32[]{:S(2)}) copy-start(f32[1,384]{1,0:T(1,128)} %reshape_reshape.3.skip.refs_6_.refs_5_) | copy-start | bytes 4612
  140.1 18.9 %all-to-all-start.5 = ((bf16[64,8,256]{2,1,0:T(8,128)(2,1)}), bf16[64,8,256]{2,1,0:T(8,128)(2,1)S(1)}, u32[]{:S(2)}, u32[]{:S(2)}) async-start(bf16[64,8,256]{2,1,0:T(8,128)(2,1)} %bitcast.29), calls=%async_computation.5 | async-start | bytes 524288 | tf_op jit(solution)/shard_map/all_to_all | solution.py:507

commit v6 on v5

--- a/solution.py
+++ b/solution.py
@@ -233,28 +233,23 @@
     apply_inner(inner, x, in_map, out_map, running_wide(decay, lower), True, local)
 
 
-def open_scan(got, decay_r, route, x, in_map, pay, stage):
+def open_scan(got, decay_r, route, pay, stage):
     slices = got[:, 1024:1152]
-    running = running_of(decay_r)
     pay[:, 0:128] = carry(link_decays(slices, CUT, stage), slices, True).astype(BF16)
     pay.send(cols=slice(0, 128))
-    fill(stage, jnp.concatenate([got[:, 256:640], got[:, 0:128]], axis=1))
-    for rows in BANDS:
-        moved = own_band(stage, route, rows, 4).astype(BF16)
-        x[rows, :] = moved[:, 0:384]
-        in_map[rows, :] = moved[:, 384:512]
-    x.send()
-    in_map.send()
-    state = local_state(in_map[...], x[...], jnp.exp(running))
+    put_band(stage, route, ALL, jnp.exp(running_of(decay_r)))
+    state = local_state(got[:, 0:128], got[:, 256:640], sent(stage, 3))
     pay[:, 128:256] = cut_state(state).astype(BF16)
     pay.send(cols=slice(128, 256))
 
 
 def inner_scan(
-    got, x, in_map, decay_r, route, out_map, grad, inner, local, links_f, links_r, work
+    got, decay_r, route, x, in_map, out_map, grad, inner, local, links_f, links_r, work
 ):
     take = receive_matrix(route)
+    in_map[...] = dot(take, got[:, 0:128]).astype(BF16)
     out_map[...] = dot(take, got[:, 128:256]).astype(BF16)
+    x[...] = dot(take, got[:, 256:640]).astype(BF16)
     grad[...] = dot(take, got[:, 640:1024]).astype(BF16)
     lower = lower_ones()
     decay = padded_decay(decay_r)
@@ -283,8 +278,8 @@
     weight = jnp.exp(running[TOK - 1 : TOK, :] - running)
     fill(stage, got[:, 0:384])
     y_forward = own_band(stage, route, ALL, 3)
-    y_reverse = (local[...].astype(F32) + weight * dot(out_map[...], entering)).astype(BF16)
-    total = y_forward + y_reverse.astype(F32) + skip[...] * x[...].astype(F32)
+    y_reverse = local[...].astype(F32) + weight * dot(out_map[...], entering)
+    total = y_forward + y_reverse + skip[...] * x[...].astype(F32)
     combined[...] = total
     scaled = gain[...] * grad[...].astype(F32)
     squares, inner = token_sums(total * total), token_sums(total * scaled)
@@ -540,15 +535,14 @@
         inner_raster, [inner16, wide16],
         ssm_input, input_map, output_map, decay_forward, skip, gain, flops=8_000_000_000,
     )
-    x_scan, in_scan, pay2 = kernel(
-        open_scan, [wide16, rows16, pay(256)],
-        got1, decay_reverse, to_raster, arrived=1, stage=512,
+    (pay2,) = kernel(
+        open_scan, [pay(256)], got1, decay_reverse, to_raster, arrived=1, stage=384,
     )
     got2 = exchange(pay2)
     links32 = ((UNITS, LANES), F32)
-    out_scan, grad_scan, inner_r, local_r, links_f, links_r = whole_kernel(
-        inner_scan, [rows16, wide16, inner16, wide16, links32, links32],
-        got1, x_scan, in_scan, decay_reverse, to_raster, flops=8_000_000_000, work=True,
+    x_scan, in_scan, out_scan, grad_scan, inner_r, local_r, links_f, links_r = whole_kernel(
+        inner_scan, [wide16, rows16, rows16, wide16, inner16, wide16, links32, links32],
+        got1, decay_reverse, to_raster, flops=8_000_000_000, work=True,
     )
     (pay3,) = kernel(
         finish_raster, [pay(512, 0)],

time: 186 us -> 186 us (level)
  no operation moved by 1% of the time
where the time goes in v6:
time: 186 us; the launch traced here: 185 us
  blocking collectives  85.8 us (46%)
  waiting for transfers between devices  40.7 us (22%)
  Pallas kernels  32.1 us (17%)
  starting transfers between devices  24 us (13%)
    all_to_all x3, blocking collectives, exchange(): return lax.all_to_all(pay, 'seq', split_axis=0, concat_axis=0, tiled=True)  69 us
    all_to_all x3, waiting for transfers between devices, exchange(): return lax.all_to_all(pay, 'seq', split_axis=0, concat_axis=0, tiled=True)  40.7 us
    all_to_all x3, starting transfers between devices, exchange(): return lax.all_to_all(pay, 'seq', split_axis=0, concat_axis=0, tiled=True)  24 us
    pallas_call x10, Pallas kernels, kernel(): pl.pallas_call(wrapped, out_shape=[pltpu.HBM(shape.shape, shape.dtype) if...  23.4 us
    all_to_all x1, blocking collectives, shards(): lax.all_to_all(stats, 'head', split_axis=0, concat_axis=0, tiled=True)  16.8 us
    pallas_call x2, Pallas kernels, whole_kernel(): pl.pallas_call(body, out_shape=shapes, scratch_shapes=[pltpu.VMEM((1, TOK...  8.62 us
  transfers between devices with their start and end apart: 3, of which 3 were waited for; matrix products, arithmetic and copies ran while one was open for 1% of the time, Pallas kernels for 8%

profile of v6, /device:TPU:1, one launch (start us, length us, event | category | flops | bytes accessed | tf_op | source)
XLA Modules:
  0.0 184.8 jit_solution(5893715873043282188)
XLA Ops:
  0.6 3.0 %open_raster.1 = bf16[512,1152]{1,0:T(8,128)(2,1)} custom-call(bf16[512,384]{1,0:T(8,128)(2,1)} %x.1, bf16[512,128]{1,0:T(8,128)(2,1)} %refs_1_.9, bf16[512,128]{1,0:T(8,128)(2,1)} %refs_4_.5, bf16[6,512]{1,0:T(8,128)(2,1)} %refs_3_.11, bf16[6,512]{1,0:T(8,128)(2,1)} %refs_3_.10, bf16[512,384]{1,0:T(8,128)(2,1)} %refs_2_.3, s32[1,64]{1,0:T(1,128)} %bitcast.36), custom_call_target="tpu_custom_call" | custom-call | flops 400000000 | bytes 2240768 | tf_op jit(solution)/shard_map/open_raster/pallas_call | solution.py:486
  3.6 0.0 copy-start.6
  3.7 0.0 copy-start.7
  3.7 11.6 %all-to-all-start = ((bf16[64,8,1152]{2,1,0:T(8,128)(2,1)}), bf16[64,8,1152]{2,1,0:T(8,128)(2,1)S(1)}, u32[]{:S(2)}, u32[]{:S(2)}) async-start(bf16[64,8,1152]{2,1,0:T(8,128)(2,1)} %bitcast.28), calls=%async_computation | async-start | bytes 2359296 | tf_op jit(solution)/shard_map/all_to_all | solution.py:502
  15.3 0.0 copy-done.6
  15.3 0.5 reshape.29.gain.refs_7_.refs_4_.refs_3_
  15.9 0.0 copy-done.7
  15.9 0.1 broadcast_in_dim.3
  15.9 0.6 reshape_reshape.3.skip.refs_6_.refs_5_
  16.5 0.0 copy-start.1
  16.5 3.6 %inner_raster.1 = (bf16[2,6,256,256]{3,2,1,0:T(8,128)(2,1)}, bf16[512,384]{1,0:T(8,128)(2,1)}) custom-call(bf16[512,384]{1,0:T(8,128)(2,1)} %x.1, bf16[512,128]{1,0:T(8,128)(2,1)} %refs_1_.9, bf16[512,128]{1,0:T(8,128)(2,1)} %refs_4_.5, bf16[6,512]{1,0:T(8,128)(2,1)} %refs_3_.11, f32[1,384]{1,0:T(1,128)} %reshape_reshape.3.skip.refs_6_.refs_5_, ...), custom_call_target="tpu_custom_call" | custom-call | flops 8000000000 | bytes 2630656 | tf_op jit(solution)/shard_map/inner_raster/pallas_call | solution.py:430
  20.2 25.7 %all-to-all-done = bf16[64,8,1152]{2,1,0:T(8,128)(2,1)S(1)} async-done(((bf16[64,8,1152]{2,1,0:T(8,128)(2,1)}), bf16[64,8,1152]{2,1,0:T(8,128)(2,1)S(1)}, u32[]{:S(2)}, u32[]{:S(2)}) %all-to-all-start) | async-done | bytes 1179680 | tf_op jit(solution)/shard_map/all_to_all | solution.py:502
  45.9 0.0 copy-start
  45.9 0.0 copy-done.1
  45.9 1.8 open_scan.1
  47.7 6.6 %all-to-all-start.1 = ((bf16[64,8,256]{2,1,0:T(8,128)(2,1)}), bf16[64,8,256]{2,1,0:T(8,128)(2,1)S(1)}, u32[]{:S(2)}, u32[]{:S(2)}) async-start(bf16[64,8,256]{2,1,0:T(8,128)(2,1)} %bitcast.30), calls=%async_computation.1 | async-start | bytes 524288 | tf_op jit(solution)/shard_map/all_to_all | solution.py:502
  54.4 0.0 copy-done
  54.4 0.0 copy-start.3
  54.4 5.0 %inner_scan.1 = (bf16[512,384]{1,0:T(8,128)(2,1)}, bf16[512,128]{1,0:T(8,128)(2,1)}, bf16[512,128]{1,0:T(8,128)(2,1)}, bf16[512,384]{1,0:T(8,128)(2,1)}, bf16[2,...) custom-call(bf16[512,1152]{1,0:T(8,128)(2,1)} %bitcast.19, ...), custom_call_target="tpu_custom_call" | custom-call | flops 8000000000 | bytes 4266240 | tf_op jit(solution)/shard_map/inner_scan/pallas_call | solution.py:430
  59.4 0.0 copy-start.2
  59.4 0.0 copy-start.4
  59.4 0.0 copy-start.5
  59.4 8.2 %all-to-all-done.1 = bf16[64,8,256]{2,1,0:T(8,128)(2,1)S(1)} async-done(((bf16[64,8,256]{2,1,0:T(8,128)(2,1)}), bf16[64,8,256]{2,1,0:T(8,128)(2,1)S(1)}, u32[]{:S(2)}, u32[]{:S(2)}) %all-to-all-start.1) | async-done | bytes 262176 | tf_op jit(solution)/shard_map/all_to_all | solution.py:502
  67.6 0.0 copy-done.3
  67.6 1.6 finish_raster.1
  69.2 22.2 %all_to_all.77 = bf16[64,8,512]{2,1,0:T(8,128)(2,1)S(1)} all-to-all(bf16[64,8,512]{2,1,0:T(8,128)(2,1)S(1)} %bitcast.23), channel_id=1, replica_groups=mesh['seq'=64,'head'=8] {'seq'}, dimensions={0} | all-to-all | bytes 1048576 | tf_op jit(solution)/shard_map/all_to_all | solution.py:502
  91.4 0.0 copy-done.2
  91.4 0.0 copy-done.4
  91.4 0.0 copy-done.5
  91.4 2.2 %finish_scan.1 = (f32[512,384]{1,0:T(8,128)S(1)}, f32[64,128]{1,0:T(8,128)S(1)}) custom-call(bf16[512,512]{1,0:T(8,128)(2,1)S(1)} %bitcast.16, bf16[512,128]{1,0:T(8,128)(2,1)} %get-tuple-element.21.refs_1_.refs_2_.refs_4_, bf16[512,384]{1,0:T(8,128)(2,1)} %get-tuple-element.22.refs_2_, bf16[6,512]{1,0:T(8,128)(2,1)S(1)} %copy-done.2, ...), custom_call_target="tpu_custom_call" | custom-call | flops 400000000 | bytes 2663680 | tf_op jit(solution)/shard_map/finish_scan/pallas_call | solution.py:486
  93.7 16.8 %all_to_all.78 = f32[8,8,128]{2,1,0:T(8,128)S(1)} all-to-all(f32[8,8,128]{2,1,0:T(8,128)S(1)} %bitcast.27), channel_id=1, replica_groups=mesh['seq'=64,'head'=8] {'head'}, dimensions={0} | all-to-all | bytes 65536 | tf_op jit(solution)/shard_map/all_to_all | solution.py:556
  110.5 2.1 %open_back.1 = (bf16[512,384]{1,0:T(8,128)(2,1)}, bf16[512,512]{1,0:T(8,128)(2,1)S(1)}) custom-call(f32[64,128]{1,0:T(8,128)S(1)} %bitcast.26, f32[512,384]{1,0:T(8,128)S(1)} %get-tuple-element.26.refs_1_, bf16[512,128]{1,0:T(8,128)(2,1)} %get-tuple-element.21.refs_1_.refs_2_.refs_4_, bf16[512,384]{1,0:T(8,128)(2,1)} %get-tuple-element.24.refs_5_.refs_3_, ...), custom_call_target="tpu_custom_call" | custom-call | flops 400000000 | bytes 2268928 | tf_op jit(solution)/shard_map/open_back/pallas_call | solution.py:486
  112.6 24.6 %all_to_all.79 = bf16[64,8,512]{2,1,0:T(8,128)(2,1)S(1)} all-to-all(bf16[64,8,512]{2,1,0:T(8,128)(2,1)S(1)} %bitcast.22), channel_id=1, replica_groups=mesh['seq'=64,'head'=8] {'seq'}, dimensions={0} | all-to-all | bytes 1048576 | tf_op jit(solution)/shard_map/all_to_all | solution.py:502
  137.1 2.6 %middle_raster.1 = (bf16[512,384]{1,0:T(8,128)(2,1)}, bf16[512,384]{1,0:T(8,128)(2,1)}, bf16[512,256]{1,0:T(8,128)(2,1)}) custom-call(bf16[512,512]{1,0:T(8,128)(2,1)S(1)} %bitcast.21, bf16[512,128]{1,0:T(8,128)(2,1)} %refs_4_.5, bf16[512,384]{1,0:T(8,128)(2,1)} %refs_2_.3, f32[1,384]{1,0:T(1,128)S(1)} %copy-done.4, bf16[6,512]{1,0:T(8,128)(2,1)S(1)} %copy-done.3, ...), custom_call_target="tpu_custom_call" | custom-call | flops 400000000 | bytes 2137856 | tf_op jit(solution)/shard_map/middle_raster/pallas_call | solution.py:486
  139.8 5.7 %all-to-all-start.5 = ((bf16[64,8,256]{2,1,0:T(8,128)(2,1)}), bf16[64,8,256]{2,1,0:T(8,128)(2,1)S(1)}, u32[]{:S(2)}, u32[]{:S(2)}) async-start(bf16[64,8,256]{2,1,0:T(8,128)(2,1)} %bitcast.29), calls=%async_computation.5 | async-start | bytes 524288 | tf_op jit(solution)/shard_map/all_to_all | solution.py:502
  145.5 3.1 %inner_back_scan.1.refs_2_ = bf16[512,384]{1,0:T(8,128)(2,1)} custom-call(bf16[6,512]{1,0:T(8,128)(2,1)S(1)} %copy-done.2, bf16[2,6,256,256]{3,2,1,0:T(8,128)(2,1)} %get-tuple-element.31.refs_1_, bf16[512,384]{1,0:T(8,128)(2,1)} %get-tuple-element.32.refs_2_, bf16[512,128]{1,0:T(8,128)(2,1)} %get-tuple-element.30.refs_3_.refs_1_, ...), custom_call_target="tpu_custom_call" | custom-call | flops 4000000000 | bytes 2627584 | tf_op jit(solution)/shard_map/inner_back_scan/pallas_call | solution.py:486
  148.6 3.2 %inner_back_raster.1.refs_6_.refs_2_ = bf16[512,384]{1,0:T(8,128)(2,1)} custom-call(bf16[6,512]{1,0:T(8,128)(2,1)S(1)} %copy-done.3, bf16[2,6,256,256]{3,2,1,0:T(8,128)(2,1)} %get-tuple-element.34.refs_1_, bf16[512,384]{1,0:T(8,128)(2,1)} %get-tuple-element.35.refs_2_, bf16[512,128]{1,0:T(8,128)(2,1)} %refs_1_.9, bf16[512,128]{1,0:T(8,128)(2,1)} %refs_4_.5, ...), custom_call_target="tpu_custom_call" | custom-call | flops 4000000000 | bytes 2629120 | tf_op jit(solution)/shard_map/inner_back_raster/pallas_call | solution.py:486
  151.8 6.9 %all-to-all-done.5 = bf16[64,8,256]{2,1,0:T(8,128)(2,1)S(1)} async-done(((bf16[64,8,256]{2,1,0:T(8,128)(2,1)}), bf16[64,8,256]{2,1,0:T(8,128)(2,1)S(1)}, u32[]{:S(2)}, u32[]{:S(2)}) %all-to-all-start.5) | async-done | bytes 262176 | tf_op jit(solution)/shard_map/all_to_all | solution.py:502
  158.7 1.6 finish_back_scan.1
  160.3 22.2 %all_to_all.80 = bf16[64,8,512]{2,1,0:T(8,128)(2,1)S(1)} all-to-all(bf16[64,8,512]{2,1,0:T(8,128)(2,1)S(1)} %bitcast.17), channel_id=1, replica_groups=mesh['seq'=64,'head'=8] {'seq'}, dimensions={0} | all-to-all | bytes 1048576 | tf_op jit(solution)/shard_map/all_to_all | solution.py:502
  182.6 2.1 %finish_back_raster.1 = bf16[512,384]{1,0:T(8,128)(2,1)} custom-call(bf16[512,512]{1,0:T(8,128)(2,1)S(1)} %bitcast.24, bf16[512,128]{1,0:T(8,128)(2,1)} %refs_1_.9, bf16[512,384]{1,0:T(8,128)(2,1)} %inner_back_raster.1.refs_6_.refs_2_, bf16[6,512]{1,0:T(8,128)(2,1)S(1)} %copy-done.3, s32[1,64]{1,0:T(1,128)} %bitcast.39), custom_call_target="tpu_custom_call" | custom-call | flops 400000000 | bytes 1448192 | tf_op jit(solution)/shard_map/finish_back_raster/pallas_call | solution.py:486
Async XLA Ops:
  3.6 11.7 %copy-start.6 = (f32[384]{0:T(512)S(1)}, f32[384]{0:T(512)}, u32[]{:S(2)}) copy-start(f32[384]{0:T(512)} %param.16) | copy-start | bytes 4612
  3.7 12.2 %copy-start.7 = (f32[6]{0:T(128)S(1)}, f32[6]{0:T(128)}, u32[]{:S(2)}) copy-start(f32[6]{0:T(128)} %param.15) | copy-start | bytes 76
  3.7 42.2 %all-to-all-start = ((bf16[64,8,1152]{2,1,0:T(8,128)(2,1)}), bf16[64,8,1152]{2,1,0:T(8,128)(2,1)S(1)}, u32[]{:S(2)}, u32[]{:S(2)}) async-start(bf16[64,8,1152]{2,1,0:T(8,128)(2,1)} %bitcast.28), calls=%async_computation | async-start | bytes 2359296 | tf_op jit(solution)/shard_map/all_to_all | solution.py:502
  16.5 29.4 %copy-start.1 = (bf16[6,512]{1,0:T(8,128)(2,1)S(1)}, bf16[6,512]{1,0:T(8,128)(2,1)}, u32[]{:S(2)}) copy-start(bf16[6,512]{1,0:T(8,128)(2,1)} %refs_3_.10) | copy-start | bytes 18436
  45.9 8.5 %copy-start = (bf16[64,8,1152]{2,1,0:T(8,128)(2,1)}, bf16[64,8,1152]{2,1,0:T(8,128)(2,1)S(1)}, u32[]{:S(2)}) copy-start(bf16[64,8,1152]{2,1,0:T(8,128)(2,1)S(1)} %all-to-all-done) | copy-start | bytes 3538948
  47.7 19.8 %all-to-all-start.1 = ((bf16[64,8,256]{2,1,0:T(8,128)(2,1)}), bf16[64,8,256]{2,1,0:T(8,128)(2,1)S(1)}, u32[]{:S(2)}, u32[]{:S(2)}) async-start(bf16[64,8,256]{2,1,0:T(8,128)(2,1)} %bitcast.30), calls=%async_computation.1 | async-start | bytes 524288 | tf_op jit(solution)/shard_map/all_to_all | solution.py:502
  54.4 13.2 %copy-start.3 = (bf16[6,512]{1,0:T(8,128)(2,1)S(1)}, bf16[6,512]{1,0:T(8,128)(2,1)}, u32[]{:S(2)}) copy-start(bf16[6,512]{1,0:T(8,128)(2,1)} %refs_3_.11) | copy-start | bytes 18436
  59.4 32.1 %copy-start.2 = (bf16[6,512]{1,0:T(8,128)(2,1)S(1)}, bf16[6,512]{1,0:T(8,128)(2,1)}, u32[]{:S(2)}) copy-start(bf16[6,512]{1,0:T(8,128)(2,1)} %refs_3_.10) | copy-start | bytes 18436
  59.4 32.1 %copy-start.4 = (f32[1,384]{1,0:T(1,128)S(1)}, f32[1,384]{1,0:T(1,128)}, u32[]{:S(2)}) copy-start(f32[1,384]{1,0:T(1,128)} %reshape.29.gain.refs_7_.refs_4_.refs_3_) | copy-start | bytes 4612
  59.4 32.1 %copy-start.5 = (f32[1,384]{1,0:T(1,128)S(1)}, f32[1,384]{1,0:T(1,128)}, u32[]{:S(2)}) copy-start(f32[1,384]{1,0:T(1,128)} %reshape_reshape.3.skip.refs_6_.refs_5_) | copy-start | bytes 4612
  139.8 18.9 %all-to-all-start.5 = ((bf16[64,8,256]{2,1,0:T(8,128)(2,1)}), bf16[64,8,256]{2,1,0:T(8,128)(2,1)S(1)}, u32[]{:S(2)}, u32[]{:S(2)}) async-start(bf16[64,8,256]{2,1,0:T(8,128)(2,1)} %bitcast.29), calls=%async_computation.5 | async-start | bytes 524288 | tf_op jit(solution)/shard_map/all_to_all | solution.py:502
